TPU v7x, 32 devices: a whole 2x2x4 slice. The times are simulated.
32 devices in a mesh: grp: 2 (over x), wide: 4 (over z), narrow: 4 (over y, core).
Axes of the slice: x: 2, y: 2, z: 4, core: 2. Of those that a mesh axis runs over, the one named last changes fastest.
Arguments:
- img_in: bfloat16 [4, 1024, 768], P('wide', 'narrow'), may hold values from -6 to 6
- tri_in: bfloat16 [4, 1536, 1024], P('wide', 'narrow'), may hold values from -16 to 16
- cam: float32 [4, 1024], P('wide'), may hold values from -6 to 6
- targets: float32 [4, 3, 1536], P('wide', None, 'narrow'), may hold values from 0 to 1
- fg_mask: int32 [4, 1536], P('wide', 'narrow'), may hold values 0 or 1
- counts: int32 [4, 4], P('wide'), may hold values from 96 to 384, as said below
- ln1_gain: bfloat16 [768], P(('wide', 'narrow')), may hold values from 0.5 to 1.5
- ln1_bias: bfloat16 [768], P(('wide', 'narrow')), may hold values from -1.25 to 1.25
- enc_qkv: bfloat16 [768, 2304], P(('wide', 'narrow')), may hold values from -0.21875 to 0.21875
- enc_qv_bias: bfloat16 [1536], P(('wide', 'narrow')), may hold values from -1.25 to 1.25
- enc_proj: bfloat16 [768, 768], P(('wide', 'narrow')), may hold values from -0.875 to 0.875
- enc_proj_bias: bfloat16 [768], P(('wide', 'narrow')), may hold values from -1.25 to 1.25
- ln2_gain: bfloat16 [768], P(('wide', 'narrow')), may hold values from 0.5 to 1.5
- ln2_bias: bfloat16 [768], P(('wide', 'narrow')), may hold values from -1.25 to 1.25
- enc_fc1: bfloat16 [768, 3072], P(('wide', 'narrow')), may hold values from -0.21875 to 0.21875
- enc_fc1_bias: bfloat16 [3072], P(('wide', 'narrow')), may hold values from -1.25 to 1.25
- enc_fc2: bfloat16 [3072, 768], P(('wide', 'narrow')), may hold values from -0.21875 to 0.21875
- enc_fc2_bias: bfloat16 [768], P(('wide', 'narrow')), may hold values from -1.25 to 1.25
- dec_mod: bfloat16 [1024, 6144], P(('wide', 'narrow')), may hold values from -0.046875 to 0.046875
- dec_qkv: bfloat16 [1024, 3072], P(('wide', 'narrow')), may hold values from -0.1875 to 0.1875
- dec_proj: bfloat16 [1024, 1024], P(('wide', 'narrow')), may hold values from -0.75 to 0.75
- dec_cross_q: bfloat16 [1024, 1024], P(('wide', 'narrow')), may hold values from -0.1875 to 0.1875
- dec_cross_kv: bfloat16 [768, 2048], P(('wide', 'narrow')), may hold values from -0.21875 to 0.21875
- dec_cross_proj: bfloat16 [1024, 1024], P(('wide', 'narrow')), may hold values from -0.75 to 0.75
- dec_fc1: bfloat16 [1024, 4096], P(('wide', 'narrow')), may hold values from -0.1875 to 0.1875
- dec_fc1_bias: bfloat16 [4096], P(('wide', 'narrow')), may hold values from -1.25 to 1.25
- dec_fc2: bfloat16 [4096, 1024], P(('wide', 'narrow')), may hold values from -0.1875 to 0.1875
- dec_fc2_bias: bfloat16 [1024], P(('wide', 'narrow')), may hold values from -1.25 to 1.25
- dec_head: bfloat16 [1024, 4], P(('wide', 'narrow')), may hold values from -0.005859375 to 0.005859375
Outputs:
- loss: float32 [], replicated
- img_grad: float32 [4, 1024, 768], P('wide', 'narrow')
- tri_grad: float32 [4, 1536, 1024], P('wide', 'narrow')
- ln1_gain_grad: float32 [768], P(('wide', 'narrow'))
- ln1_bias_grad: float32 [768], P(('wide', 'narrow'))
- enc_qkv_grad: float32 [768, 2304], P(('wide', 'narrow'))
- enc_qv_bias_grad: float32 [1536], P(('wide', 'narrow'))
- enc_proj_grad: float32 [768, 768], P(('wide', 'narrow'))
- enc_proj_bias_grad: float32 [768], P(('wide', 'narrow'))
- ln2_gain_grad: float32 [768], P(('wide', 'narrow'))
- ln2_bias_grad: float32 [768], P(('wide', 'narrow'))
- enc_fc1_grad: float32 [768, 3072], P(('wide', 'narrow'))
- enc_fc1_bias_grad: float32 [3072], P(('wide', 'narrow'))
- enc_fc2_grad: float32 [3072, 768], P(('wide', 'narrow'))
- enc_fc2_bias_grad: float32 [768], P(('wide', 'narrow'))
- dec_mod_grad: float32 [1024, 6144], P(('wide', 'narrow'))
- dec_qkv_grad: float32 [1024, 3072], P(('wide', 'narrow'))
- dec_proj_grad: float32 [1024, 1024], P(('wide', 'narrow'))
- dec_cross_q_grad: float32 [1024, 1024], P(('wide', 'narrow'))
- dec_cross_kv_grad: float32 [768, 2048], P(('wide', 'narrow'))
- dec_cross_proj_grad: float32 [1024, 1024], P(('wide', 'narrow'))
- dec_fc1_grad: float32 [1024, 4096], P(('wide', 'narrow'))
- dec_fc1_bias_grad: float32 [4096], P(('wide', 'narrow'))
- dec_fc2_grad: float32 [4096, 1024], P(('wide', 'narrow'))
- dec_fc2_bias_grad: float32 [1024], P(('wide', 'narrow'))
- dec_head_grad: float32 [1024, 4], P(('wide', 'narrow'))
Inputs may be any that keep to these rules, and one draw needn't show every extreme that they name: `counts`: each count lies between 384 // 4 (at least 1) and 384; some view of some object has all 384 rays live.
All inputs are finite; a program needn't handle non-finite values. No bound on the sum of `fg_mask` on one device may be relied on, other than what follows from the above.
Results may differ from a plain program's by a relative error of at most 0.028.
Values may be sent and summed in bfloat16 or wider, within the bound.
A program may use at most 576 MiB of HBM per device.

v0:
```python
import jax
import jax.numpy as jnp
from jax import lax
from jax.sharding import PartitionSpec as P

ENC_HEADS = 12
DEC_HEADS = 16
TRI_TOK = 1536
VIEWS = 4


NORM_EPS = 1e-06
PRECISE = lax.Precision.HIGHEST


def passed_along(block, axis, distance):
    devices = range(lax.axis_size(axis))
    route = [(i - distance, i) for i in devices if i - distance in devices]
    return lax.ppermute(block, axis, route)


def matmul_plain(first_op, second_op):
    return jnp.dot(first_op, second_op, preferred_element_type=jnp.float32)


def matmul_left(first_op, second_op):
    return lax.dot_general(
        first_op, second_op, (((0,), (0,)), ((), ())), preferred_element_type=jnp.float32
    )


def matmul_right(first_op, second_op):
    return lax.dot_general(
        first_op, second_op, (((1,), (1,)), ((), ())), preferred_element_type=jnp.float32
    )


def to_bf16(value):
    return value.astype(jnp.bfloat16)


def flat_rows(tensor):
    return tensor.reshape(-1, tensor.shape[-1])


def column_sums(gradient):
    return jnp.sum(gradient.astype(jnp.float32), 0)


def layer_norm(values):
    centered = values - jnp.mean(values, -1, keepdims=True)
    return centered * lax.rsqrt(jnp.mean(centered * centered, -1, keepdims=True) + NORM_EPS)


def affine_norm(values, gain, shift):
    return layer_norm(values) * gain + shift


def modulated_norm(values, gamma, beta):
    return layer_norm(values) * (1.0 + gamma[:, None, :]) + beta[:, None, :]


def gelu_exact(values):
    return jax.nn.gelu(values, approximate=False)


def gelu_grad(pre_act, upstream):
    return jax.vjp(gelu_exact, pre_act)[1](upstream)[0]


def on_group(active, method, operands):

    def skipped(*inputs):
        return jax.tree.map(jnp.zeros_like, method(*inputs))

    return lax.cond(active, method, skipped, *operands)


def head_groups(tensor, head_count):
    object_count, row_count, width_all = tensor.shape
    head_size = width_all // head_count
    parted = tensor.reshape(object_count, row_count, head_count // 4, 4, head_size)
    return jnp.transpose(parted, (0, 2, 1, 3, 4)).reshape(
        object_count * (head_count // 4), row_count, 4, head_size
    )


def merge_groups(tensor, object_count):
    group_total, row_count, group_heads, head_size = tensor.shape
    parted = tensor.reshape(
        object_count, group_total // object_count, row_count, group_heads, head_size
    )
    return jnp.transpose(parted, (0, 2, 1, 3, 4)).reshape(
        object_count, row_count, group_total // object_count * group_heads * head_size
    )


def attend_forward(queries, key_rows, value_rows, head_count):
    object_count = queries.shape[0]
    scaling = (queries.shape[2] // head_count) ** (-0.5)

    def group_forward(pieces):
        q_part, k_part, v_part = pieces
        scores = (
            jnp.einsum("rhd,shd->hrs", q_part, k_part, preferred_element_type=jnp.float32) * scaling
        )
        row_max = jnp.max(scores, -1, keepdims=True)
        exp_terms = jnp.exp(scores - row_max)
        row_sum = jnp.sum(exp_terms, -1, keepdims=True)
        attended = jnp.einsum(
            "hrs,shd->rhd", to_bf16(exp_terms / row_sum), v_part, preferred_element_type=jnp.float32
        )
        return (attended, (row_max + jnp.log(row_sum))[..., 0])

    attended, log_sums = lax.map(
        group_forward,
        (
            head_groups(queries, head_count),
            head_groups(key_rows, head_count),
            head_groups(value_rows, head_count),
        ),
    )
    return (to_bf16(merge_groups(attended, object_count)), log_sums)


def attend_backward(queries, key_rows, value_rows, log_sums, grad_out, head_count):
    object_count = queries.shape[0]
    scaling = (queries.shape[2] // head_count) ** (-0.5)

    def group_backward(pieces):
        q_part, k_part, v_part, sums_part, g_part = pieces
        scores = (
            jnp.einsum("rhd,shd->hrs", q_part, k_part, preferred_element_type=jnp.float32) * scaling
        )
        weights = jnp.exp(scores - sums_part[..., None])
        grad_weights = jnp.einsum(
            "rhd,shd->hrs", g_part, v_part, preferred_element_type=jnp.float32
        )
        grad_scores = to_bf16(
            weights * (grad_weights - jnp.sum(weights * grad_weights, -1, keepdims=True))
        )
        grad_q = (
            jnp.einsum("hrs,shd->rhd", grad_scores, k_part, preferred_element_type=jnp.float32)
            * scaling
        )
        grad_k = (
            jnp.einsum("hrs,rhd->shd", grad_scores, q_part, preferred_element_type=jnp.float32)
            * scaling
        )
        grad_v = jnp.einsum(
            "hrs,rhd->shd", to_bf16(weights), g_part, preferred_element_type=jnp.float32
        )
        return (grad_q, grad_k, grad_v)

    grad_q, grad_k, grad_v = lax.map(
        group_backward,
        (
            head_groups(queries, head_count),
            head_groups(key_rows, head_count),
            head_groups(value_rows, head_count),
            log_sums,
            head_groups(grad_out, head_count),
        ),
    )
    return (
        merge_groups(grad_q, object_count),
        merge_groups(grad_k, object_count),
        merge_groups(grad_v, object_count),
    )


def ray_loss(final_rows, head_weight, target_rgb, foreground, valid_rays):
    predicted = jnp.einsum("ord,dc->orc", final_rows, head_weight, precision=PRECISE)
    colour = jax.nn.sigmoid(predicted[..., :3])
    residue = colour - jnp.swapaxes(target_rgb, 1, 2)
    opacity = predicted[..., 3]
    per_ray = jnp.sum(residue * residue, -1) + jax.nn.softplus(opacity) - foreground * opacity
    return jnp.sum(valid_rays * per_ray)


def fetch(shards):
    flattened = jnp.concatenate([shard.reshape(1, -1) for shard in shards], 1)
    everything = lax.all_gather(flattened, ("wide", "narrow"), axis=0, tiled=True)
    outputs = []
    offset = 0
    for shard in shards:
        length = shard.size
        outputs.append(everything[:, offset : offset + length].reshape((-1,) + shard.shape[1:]))
        offset += length
    return outputs


def unpack_rows(summed, gradients, shard_count):
    outputs = []
    offset = 0
    for gradient in gradients:
        length = gradient.size // shard_count
        outputs.append(
            summed[offset : offset + length].reshape(
                (gradient.shape[0] // shard_count,) + gradient.shape[1:]
            )
        )
        offset += length
    return outputs


def reduce_grads(gradients):
    shard_count = lax.axis_size(("wide", "narrow"))
    packed = jnp.concatenate([gradient.reshape(shard_count, -1) for gradient in gradients], 1)
    own_piece = lax.psum_scatter(packed, ("wide", "narrow"), scatter_dimension=0, tiled=True)
    summed = lax.psum(own_piece.astype(jnp.bfloat16), "grp").astype(jnp.float32).reshape(-1)
    return unpack_rows(summed, gradients, shard_count)


def local(
    img_in,
    tri_in,
    cam,
    targets,
    fg_mask,
    counts,
    ln1_gain,
    ln1_bias,
    enc_qkv,
    enc_qv_bias,
    enc_proj,
    enc_proj_bias,
    ln2_gain,
    ln2_bias,
    enc_fc1,
    enc_fc1_bias,
    enc_fc2,
    enc_fc2_bias,
    dec_mod,
    dec_qkv,
    dec_proj,
    dec_cross_q,
    dec_cross_kv,
    dec_cross_proj,
    dec_fc1,
    dec_fc1_bias,
    dec_fc2,
    dec_fc2_bias,
    dec_head,
):
    is_encoder = lax.axis_index("grp") == 0
    is_decoder = lax.axis_index("grp") == 1
    object_count, image_rows, enc_width = img_in.shape
    plane_rows, dec_width = (tri_in.shape[1], tri_in.shape[2])
    g_ln1, b_ln1, w_qkv, b_qv, w_proj, b_proj, g_ln2, b_ln2, w_fc1, b_fc1, w_fc2, b_fc2 = fetch(
        (
            ln1_gain,
            ln1_bias,
            enc_qkv,
            enc_qv_bias,
            enc_proj,
            enc_proj_bias,
            ln2_gain,
            ln2_bias,
            enc_fc1,
            enc_fc1_bias,
            enc_fc2,
            enc_fc2_bias,
        )
    )
    w_mod, w_dqkv, w_dproj, w_cq, w_ckv, w_cproj, w_dfc1, b_dfc1, w_dfc2, b_dfc2, w_head = fetch(
        (
            dec_mod,
            dec_qkv,
            dec_proj,
            dec_cross_q,
            dec_cross_kv,
            dec_cross_proj,
            dec_fc1,
            dec_fc1_bias,
            dec_fc2,
            dec_fc2_bias,
            dec_head,
        )
    )
    gain_one, shift_one = (g_ln1.astype(jnp.float32), b_ln1.astype(jnp.float32))
    gain_two, shift_two = (g_ln2.astype(jnp.float32), b_ln2.astype(jnp.float32))
    bias_proj, bias_fc1, bias_fc2 = (
        b_proj.astype(jnp.float32),
        b_fc1.astype(jnp.float32),
        b_fc2.astype(jnp.float32),
    )
    bias_dfc1, bias_dfc2 = (b_dfc1.astype(jnp.float32), b_dfc2.astype(jnp.float32))
    head_f32 = w_head.astype(jnp.float32)
    image_x = img_in.astype(jnp.float32)
    plane_x = tri_in.astype(jnp.float32)
    ray_slots = TRI_TOK // VIEWS
    row_index = lax.axis_index("narrow") * plane_rows + jnp.arange(plane_rows, dtype=jnp.int32)
    view_index = row_index // ray_slots
    slot_index = row_index % ray_slots
    view_ids = jnp.arange(VIEWS, dtype=jnp.int32)
    limits = jnp.sum(
        jnp.where(view_index[None, :, None] == view_ids[None, None, :], counts[:, None, :], 0), -1
    )
    valid_rays = (slot_index[None, :] < limits).astype(jnp.float32)
    foreground = fg_mask.astype(jnp.float32)

    def enc_front(image_x):
        normed = to_bf16(flat_rows(affine_norm(image_x, gain_one, shift_one)))
        bias_full = jnp.concatenate(
            [b_qv[:enc_width], jnp.zeros((enc_width,), jnp.bfloat16), b_qv[enc_width:]]
        ).astype(jnp.float32)
        return to_bf16(matmul_plain(normed, w_qkv) + bias_full).reshape(
            object_count, image_rows, 3 * enc_width
        )

    def dec_front(plane_x):
        modulation = jnp.dot(cam, w_mod.astype(jnp.float32), precision=PRECISE).reshape(
            object_count, 6, dec_width
        )
        normed = to_bf16(flat_rows(modulated_norm(plane_x, modulation[:, 0], modulation[:, 1])))
        return (
            modulation,
            to_bf16(matmul_plain(normed, w_dqkv)).reshape(object_count, plane_rows, 3 * dec_width),
        )

    enc_rows = on_group(is_encoder, enc_front, (image_x,))
    modulation, dec_rows = on_group(is_decoder, dec_front, (plane_x,))
    enc_keys, dec_keys = (
        lax.all_gather(enc_rows[:, :, enc_width:], "narrow", axis=1, tiled=True),
        lax.all_gather(dec_rows[:, :, dec_width:], "narrow", axis=1, tiled=True),
    )

    def enc_rest(image_x, qkv_rows, all_keys):
        attended, log_sums = attend_forward(
            qkv_rows[:, :, :enc_width],
            all_keys[:, :, :enc_width],
            all_keys[:, :, enc_width:],
            ENC_HEADS,
        )
        hidden = image_x + (matmul_plain(flat_rows(attended), w_proj) + bias_proj).reshape(
            image_x.shape
        )
        normed_two = to_bf16(flat_rows(affine_norm(hidden, gain_two, shift_two)))
        pre_act = matmul_plain(normed_two, w_fc1) + bias_fc1
        activated = to_bf16(gelu_exact(pre_act))
        output = hidden + (matmul_plain(activated, w_fc2) + bias_fc2).reshape(image_x.shape)
        return (to_bf16(output), attended, log_sums, hidden, pre_act)

    def dec_self(plane_x, qkv_rows, all_keys, modulation):
        attended, log_sums = attend_forward(
            qkv_rows[:, :, :dec_width],
            all_keys[:, :, :dec_width],
            all_keys[:, :, dec_width:],
            DEC_HEADS,
        )
        after_self = plane_x + matmul_plain(flat_rows(attended), w_dproj).reshape(plane_x.shape)
        normed_two = to_bf16(
            flat_rows(modulated_norm(after_self, modulation[:, 2], modulation[:, 3]))
        )
        cross_rows = to_bf16(matmul_plain(normed_two, w_cq)).reshape(plane_x.shape)
        return (attended, log_sums, after_self, normed_two, cross_rows)

    enc_out, enc_attended, enc_sums, enc_hidden, enc_pre = on_group(
        is_encoder, enc_rest, (image_x, enc_rows, enc_keys)
    )
    self_attended, self_sums, after_self, normed_two, cross_rows = on_group(
        is_decoder, dec_self, (plane_x, dec_rows, dec_keys, modulation)
    )
    image_recv = passed_along(enc_out, "grp", 1)

    def project_image(image_part):
        return to_bf16(matmul_plain(flat_rows(image_part), w_ckv)).reshape(
            object_count, image_part.shape[1], 2 * dec_width
        )

    cross_kv = lax.all_gather(
        on_group(is_decoder, project_image, (image_recv,)), "narrow", axis=1, tiled=True
    )

    def dec_rest(
        after_self, normed_two, cross_rows, cross_kv, modulation, targets, foreground, valid_rays
    ):
        cross_keys, cross_values = (cross_kv[:, :, :dec_width], cross_kv[:, :, dec_width:])
        attended, log_sums = attend_forward(cross_rows, cross_keys, cross_values, DEC_HEADS)
        after_cross = after_self + matmul_plain(flat_rows(attended), w_cproj).reshape(
            after_self.shape
        )
        normed_three = to_bf16(
            flat_rows(modulated_norm(after_cross, modulation[:, 4], modulation[:, 5]))
        )
        pre_act = matmul_plain(normed_three, w_dfc1) + bias_dfc1
        activated = to_bf16(gelu_exact(pre_act))
        final_rows = after_cross + (matmul_plain(activated, w_dfc2) + bias_dfc2).reshape(
            after_cross.shape
        )

        def ray_total(rows_in, head_in):
            return ray_loss(rows_in, head_in, targets, foreground, valid_rays)

        total, ray_pull = jax.vjp(ray_total, final_rows, head_f32)
        grad_final, grad_head = ray_pull(jnp.ones((), jnp.float32))
        grad_branch = to_bf16(flat_rows(grad_final))
        grad_fc2 = matmul_left(activated, grad_branch)
        grad_bfc2 = column_sums(grad_branch)
        grad_pre = to_bf16(gelu_grad(pre_act, matmul_right(grad_branch, w_dfc2)))
        grad_fc1 = matmul_left(normed_three, grad_pre)
        grad_bfc1 = column_sums(grad_pre)
        _, norm_pull = jax.vjp(modulated_norm, after_cross, modulation[:, 4], modulation[:, 5])
        grad_cross_in, grad_gamma3, grad_beta3 = norm_pull(
            matmul_right(grad_pre, w_dfc1).reshape(after_cross.shape)
        )
        grad_after_cross = grad_final + grad_cross_in
        grad_branch = to_bf16(flat_rows(grad_after_cross))
        grad_cproj = matmul_left(flat_rows(attended), grad_branch)
        grad_attended = to_bf16(matmul_right(grad_branch, w_cproj)).reshape(attended.shape)
        grad_cq_rows, grad_ck, grad_cv = attend_backward(
            cross_rows, cross_keys, cross_values, log_sums, grad_attended, DEC_HEADS
        )
        grad_cq_rows = to_bf16(flat_rows(grad_cq_rows))
        grad_cq = matmul_left(normed_two, grad_cq_rows)
        _, norm_pull_two = jax.vjp(modulated_norm, after_self, modulation[:, 2], modulation[:, 3])
        grad_self_in, grad_gamma2, grad_beta2 = norm_pull_two(
            matmul_right(grad_cq_rows, w_cq).reshape(after_self.shape)
        )
        grad_after_self = grad_after_cross + grad_self_in
        grad_mod_late = jnp.stack([grad_gamma2, grad_beta2, grad_gamma3, grad_beta3], 1)
        late_grads = (grad_head, grad_fc2, grad_bfc2, grad_fc1, grad_bfc1, grad_cproj, grad_cq)
        return (
            total,
            jnp.sum(valid_rays),
            grad_after_self,
            grad_mod_late,
            jnp.concatenate([grad_ck, grad_cv], -1),
            late_grads,
        )

    total, live_count, grad_after_self, grad_mod_late, cross_partial, late_grads = on_group(
        is_decoder,
        dec_rest,
        (after_self, normed_two, cross_rows, cross_kv, modulation, targets, foreground, valid_rays),
    )
    cross_own = lax.psum_scatter(
        cross_partial.astype(jnp.bfloat16), "narrow", scatter_dimension=1, tiled=True
    ).astype(jnp.float32)

    def cross_back(grad_rows, image_part):
        grad_rows = to_bf16(flat_rows(grad_rows))
        grad_ckv = matmul_left(flat_rows(image_part), grad_rows)
        return (grad_ckv, to_bf16(matmul_right(grad_rows, w_ckv)).reshape(image_part.shape))

    grad_ckv, grad_image = on_group(is_decoder, cross_back, (cross_own, image_recv))
    image_grad_back = passed_along(grad_image, "grp", -1)
    grad_head, grad_dfc2, grad_bdfc2, grad_dfc1, grad_bdfc1, grad_cproj, grad_cq = late_grads
    late_out = reduce_grads(
        [grad_head, grad_dfc2, grad_bdfc2, grad_dfc1, grad_bdfc1, grad_cproj, grad_cq, grad_ckv]
    )

    def dec_back_self(grad_after_self, attended, log_sums, qkv_rows, all_keys):
        grad_branch = to_bf16(flat_rows(grad_after_self))
        grad_dproj = matmul_left(flat_rows(attended), grad_branch)
        grad_attended = to_bf16(matmul_right(grad_branch, w_dproj)).reshape(attended.shape)
        grad_q, grad_k, grad_v = attend_backward(
            qkv_rows[:, :, :dec_width],
            all_keys[:, :, :dec_width],
            all_keys[:, :, dec_width:],
            log_sums,
            grad_attended,
            DEC_HEADS,
        )
        return (grad_dproj, grad_q, jnp.concatenate([grad_k, grad_v], -1))

    def enc_back_rest(grad_out, image_x, hidden, pre_act, attended, log_sums, qkv_rows, all_keys):
        grad_out = grad_out.astype(jnp.float32)
        grad_branch = to_bf16(flat_rows(grad_out))
        normed_two, norm_pull = jax.vjp(affine_norm, hidden, gain_two, shift_two)
        activated = to_bf16(gelu_exact(pre_act))
        grad_fc2 = matmul_left(activated, grad_branch)
        grad_bfc2 = column_sums(grad_branch)
        grad_pre = to_bf16(gelu_grad(pre_act, matmul_right(grad_branch, w_fc2)))
        grad_fc1 = matmul_left(to_bf16(flat_rows(normed_two)), grad_pre)
        grad_bfc1 = column_sums(grad_pre)
        grad_hidden_in, grad_g2, grad_b2 = norm_pull(
            matmul_right(grad_pre, w_fc1).reshape(hidden.shape)
        )
        grad_hidden = grad_out + grad_hidden_in
        grad_branch = to_bf16(flat_rows(grad_hidden))
        grad_proj = matmul_left(flat_rows(attended), grad_branch)
        grad_bproj = column_sums(grad_branch)
        grad_attended = to_bf16(matmul_right(grad_branch, w_proj)).reshape(attended.shape)
        grad_q, grad_k, grad_v = attend_backward(
            qkv_rows[:, :, :enc_width],
            all_keys[:, :, :enc_width],
            all_keys[:, :, enc_width:],
            log_sums,
            grad_attended,
            ENC_HEADS,
        )
        return (
            grad_hidden,
            grad_q,
            jnp.concatenate([grad_k, grad_v], -1),
            (grad_g2, grad_b2, grad_proj, grad_bproj, grad_fc1, grad_bfc1, grad_fc2, grad_bfc2),
        )

    grad_dproj, dec_grad_q, dec_kv_partial = on_group(
        is_decoder, dec_back_self, (grad_after_self, self_attended, self_sums, dec_rows, dec_keys)
    )
    enc_grad_hidden, enc_grad_q, enc_kv_partial, enc_late = on_group(
        is_encoder,
        enc_back_rest,
        (image_grad_back, image_x, enc_hidden, enc_pre, enc_attended, enc_sums, enc_rows, enc_keys),
    )
    enc_kv_own, dec_kv_own = (
        lax.psum_scatter(
            enc_kv_partial.astype(jnp.bfloat16), "narrow", scatter_dimension=1, tiled=True
        ).astype(jnp.float32),
        lax.psum_scatter(
            dec_kv_partial.astype(jnp.bfloat16), "narrow", scatter_dimension=1, tiled=True
        ).astype(jnp.float32),
    )

    def enc_back_front(image_x, grad_hidden, grad_q, grad_kv):
        grad_rows = to_bf16(flat_rows(jnp.concatenate([grad_q, grad_kv], -1)))
        normed, norm_pull = jax.vjp(affine_norm, image_x, gain_one, shift_one)
        grad_qkv = matmul_left(to_bf16(flat_rows(normed)), grad_rows)
        bias_sums = column_sums(grad_rows)
        grad_qv = jnp.concatenate([bias_sums[:enc_width], bias_sums[2 * enc_width :]])
        grad_in, grad_g1, grad_b1 = norm_pull(matmul_right(grad_rows, w_qkv).reshape(image_x.shape))
        return (grad_hidden + grad_in, (grad_g1, grad_b1, grad_qkv, grad_qv))

    def dec_back_front(plane_x, modulation, grad_after_self, grad_q, grad_kv, grad_mod_late):
        grad_rows = to_bf16(flat_rows(jnp.concatenate([grad_q, grad_kv], -1)))
        normed, norm_pull = jax.vjp(modulated_norm, plane_x, modulation[:, 0], modulation[:, 1])
        grad_dqkv = matmul_left(to_bf16(flat_rows(normed)), grad_rows)
        grad_in, grad_gamma1, grad_beta1 = norm_pull(
            matmul_right(grad_rows, w_dqkv).reshape(plane_x.shape)
        )
        grad_mod = jnp.concatenate(
            [grad_gamma1[:, None], grad_beta1[:, None], grad_mod_late], 1
        ).reshape(object_count, 6 * dec_width)
        grad_wmod = jnp.dot(jnp.transpose(cam), grad_mod, precision=PRECISE)
        return (grad_after_self + grad_in, grad_wmod, grad_dqkv)

    img_grad, enc_early = on_group(
        is_encoder, enc_back_front, (image_x, enc_grad_hidden, enc_grad_q, enc_kv_own)
    )
    tri_grad, grad_wmod, grad_dqkv = on_group(
        is_decoder,
        dec_back_front,
        (plane_x, modulation, grad_after_self, dec_grad_q, dec_kv_own, grad_mod_late),
    )
    early_out = reduce_grads([grad_wmod, grad_dqkv, grad_dproj])
    grad_g1, grad_b1, grad_qkv, grad_qv = enc_early
    grad_g2, grad_b2, grad_proj, grad_bproj, grad_fc1, grad_bfc1, grad_fc2, grad_bfc2 = enc_late
    enc_out_grads = reduce_grads(
        [
            grad_g1,
            grad_b1,
            grad_qkv,
            grad_qv,
            grad_proj,
            grad_bproj,
            grad_g2,
            grad_b2,
            grad_fc1,
            grad_bfc1,
            grad_fc2,
            grad_bfc2,
        ]
    )
    img_grad, tri_grad = (
        lax.psum(img_grad.astype(jnp.bfloat16), "grp").astype(jnp.float32),
        lax.psum(tri_grad.astype(jnp.bfloat16), "grp").astype(jnp.float32),
    )
    loss_total, ray_count = lax.psum((total, live_count), ("grp", "wide", "narrow"))
    loss = loss_total / ray_count
    return (
        loss,
        img_grad,
        tri_grad,
        enc_out_grads[0],
        enc_out_grads[1],
        enc_out_grads[2],
        enc_out_grads[3],
        enc_out_grads[4],
        enc_out_grads[5],
        enc_out_grads[6],
        enc_out_grads[7],
        enc_out_grads[8],
        enc_out_grads[9],
        enc_out_grads[10],
        enc_out_grads[11],
        early_out[0],
        early_out[1],
        early_out[2],
        late_out[6],
        late_out[7],
        late_out[5],
        late_out[3],
        late_out[4],
        late_out[1],
        late_out[2],
        late_out[0],
    )


def solution(mesh):
    return jax.shard_map(
        local,
        mesh=mesh,
        in_specs=(
            P("wide", "narrow", None),
            P("wide", "narrow", None),
            P("wide", None),
            P("wide", None, "narrow"),
            P("wide", "narrow"),
            P("wide", None),
            P(("wide", "narrow")),
            P(("wide", "narrow")),
            P(("wide", "narrow"), None),
            P(("wide", "narrow")),
            P(("wide", "narrow"), None),
            P(("wide", "narrow")),
            P(("wide", "narrow")),
            P(("wide", "narrow")),
            P(("wide", "narrow"), None),
            P(("wide", "narrow")),
            P(("wide", "narrow"), None),
            P(("wide", "narrow")),
            P(("wide", "narrow"), None),
            P(("wide", "narrow"), None),
            P(("wide", "narrow"), None),
            P(("wide", "narrow"), None),
            P(("wide", "narrow"), None),
            P(("wide", "narrow"), None),
            P(("wide", "narrow"), None),
            P(("wide", "narrow")),
            P(("wide", "narrow"), None),
            P(("wide", "narrow")),
            P(("wide", "narrow"), None),
        ),
        out_specs=(
            P(),
            P("wide", "narrow", None),
            P("wide", "narrow", None),
            P(("wide", "narrow")),
            P(("wide", "narrow")),
            P(("wide", "narrow"), None),
            P(("wide", "narrow")),
            P(("wide", "narrow"), None),
            P(("wide", "narrow")),
            P(("wide", "narrow")),
            P(("wide", "narrow")),
            P(("wide", "narrow"), None),
            P(("wide", "narrow")),
            P(("wide", "narrow"), None),
            P(("wide", "narrow")),
            P(("wide", "narrow"), None),
            P(("wide", "narrow"), None),
            P(("wide", "narrow"), None),
            P(("wide", "narrow"), None),
            P(("wide", "narrow"), None),
            P(("wide", "narrow"), None),
            P(("wide", "narrow"), None),
            P(("wide", "narrow")),
            P(("wide", "narrow"), None),
            P(("wide", "narrow")),
            P(("wide", "narrow"), None),
        ),
        check_vma=False,
    )
```

profile of v0, /device:TPU:0, one launch (start us, length us, event | category | flops | bytes accessed | tf_op | source)
XLA Modules:
  0.0 4474.2 jit_solution(4365264603607182229)
XLA Ops:
  14.7 6.6 dynamic-update-slice.22
  26.0 8.9 dynamic-update-slice.28
  35.3 8.8 dynamic-update-slice.30
  72.8 119.9 %all-gather.16.cloned.1.call-done = bf16[16,1,442944]{2,1,0:T(2,128)(2,1)} async-done(((bf16[1,1,442944]{2,1,0:T(2,128)(2,1)}), bf16[16,1,442944]{2,1,0:T(2,128)(2,1)}) %all-gather.16.cloned.1.call-update) | async-done | bytes 14174224 | tf_op jit(solution)/shard_map/all_gather | solution.py:183
  192.8 14.8 copy.243
  226.4 403.0 %all-gather.14.cloned.1.call-done = bf16[16,1,1409600]{2,1,0:T(2,128)(2,1)} async-done(((bf16[1,1,1409600]{2,1,0:T(2,128)(2,1)}), bf16[16,1,1409600]{2,1,0:T(2,128)(2,1)}) %all-gather.14.cloned.1.call-update) | async-done | bytes 45107216 | tf_op jit(solution)/shard_map/all_gather | solution.py:183
  629.4 45.0 %copy.242 = bf16[16,1,1409600]{2,0,1:T(8,128)(2,1)} copy(bf16[16,1,1409600]{2,1,0:T(2,128)(2,1)} %all-gather.14.cloned.1.call-done) | data formatting | bytes 90214400
  674.4 6.4 slice.355
  680.8 6.4 reshape.1623
  696.9 7.3 fusion.378
  720.5 52.1 %conditional.14 = (bf16[1,256,768]{2,1,0:T(8,128)(2,1)}, bf16[1,256,768]{1,2,0:T(8,128)(2,1)}, f32[3,4,256]{2,1,0:T(4,128)}, f32[1,256,768]{2,1,0:T(8,128)}, f32[256,3072]{1,0:T(8,128)}) conditional(s32[]{:T(128)} %convert_element_type.430, () %tuple.170, (bf16[1,256,2304]{2,1,0:T(8,128)(2,1)S(1)}, bf16[1,1024,1536]{1,2,0:T(8,128)(2,1)}, ...), branch_computations={%region_4.5_spmd, %region_5.12_spmd} | conditional | flops 3050442496 | bytes 49940700 | solution.py:76
  730.3 19.0 while.72
  761.0 11.7 fusion.45
  772.6 20.8 collective-permute-start
  818.9 24.6 all-gather.12.cloned.1.call-done
  843.5 31.3 conditional.16
  874.8 6.6 copy.207
  888.8 8.7 copy.214
  898.2 312.6 %reduce-scatter.4.cloned.1.call-done = bf16[1,256,2048]{2,1,0:T(8,128)(2,1)} async-done(((bf16[1,1024,2048]{2,1,0:T(8,128)(2,1)}), bf16[1,256,2048]{2,1,0:T(8,128)(2,1)}) %reduce-scatter.4.cloned.1.call-update) | async-done | bytes 1048592 | tf_op jit(solution)/shard_map/reduce_scatter | solution.py:438
  1215.6 11.4 constant_dynamic-update-slice_fusion.9
  1228.3 46.8 %dynamic-update-slice.3 = f32[16,754240]{1,0:T(8,128)} dynamic-update-slice(f32[16,754240]{1,0:T(8,128)} %dynamic-update-slice.2, f32[16,262144]{1,0:T(8,128)} %get-tuple-element.643, s32[]{} %constant.569, s32[]{} %constant.572) | dynamic-update-slice | bytes 33554436
  1276.7 14.0 dynamic-update-slice.5
  1290.7 13.8 dynamic-update-slice.6
  1304.5 18.8 dynamic-update-slice.7
  1323.3 108.2 %conditional.18 = (f32[1,256,768]{2,1,0:T(8,128)S(1)}, bf16[1,256,768]{1,2,0:T(8,128)(2,1)}, bf16[1,1024,1536]{1,2,0:T(8,128)(2,1)}, f32[16,48]{1,0:T(8,128)S(1)...) conditional(s32[]{:T(128)} %convert_element_type.430, ...), branch_computations={%region_58.59_spmd, %region_59.72_spmd} | conditional | flops 6242298880 | bytes 218218432 | solution.py:76
  1326.2 11.4 convert_reduce_fusion
  1351.2 27.0 while.76
  1390.4 6.9 fusion.217
  1397.3 10.8 reshape.1531
  1408.8 11.6 fusion.212
  1420.4 10.7 reshape.1533
  1437.7 15.6 conditional.21
  1438.6 9.6 reshape.1559
  1453.3 34.7 pad_maximum_fusion.6
  1488.0 21.6 conditional.19
  1512.4 20.5 dynamic-update-slice.10
  1534.4 8.1 dynamic-update-slice.12
  1546.9 27.4 dynamic-update-slice.16
  1575.8 26.9 dynamic-update-slice.18
  1604.1 2475.8 %all-reduce.12 = (bf16[16,442944]{1,0:T(8,128)(2,1)}, bf16[16,655360]{1,0:T(8,128)(2,1)}, bf16[16,754240]{1,0:T(8,128)(2,1)}) all-reduce(f32[16,442944]{1,0:T(8,128)} %dynamic-update-slice.19, f32[16,655360]{1,0:T(8,128)} %pad_maximum_fusion.6, ...), channel_id=5, replica_groups=mesh['grp'=2,'wide'=4,'narrow'=4] {'wide','narrow'}, use_global_device_ids=true, to_apply=%region_98.99.clone | all-reduce | flops 29640704 | bytes 177844224
  4086.2 8.7 dynamic-slice_convert_fusion.1
  4094.9 9.1 dynamic-slice_convert_fusion
  4104.1 112.0 %all-reduce.5 = (f32[]{:T(128)}, f32[]{:T(128)}) all-reduce(f32[]{:T(128)} %get-tuple-element.606, f32[]{:T(128)} %get-tuple-element.607), channel_id=1, replica_groups=mesh['grp'=2,'wide'=4,'narrow'=4] {'grp','wide','narrow'}, use_global_device_ids=true, to_apply=%region_53.54 | all-reduce | flops 2 | bytes 16 | tf_op jit(solution)/shard_map/psum | solution.py:571
  4217.4 163.2 %all-reduce.11.cloned.1.call-done = (bf16[1,256,768]{2,1,0:T(8,128)(2,1)}, bf16[1,384,1024]{2,1,0:T(8,128)(2,1)}, bf16[1,442944]{1,0:T(2,128)(2,1)}, bf16[1,655360]{1,0:T(2,128)(2,1)}, bf16[1,754240]{1,0:T(2,128)(2,1)}) async-done(((bf16[1,256,768]{2,1,0:T(8,128)(2,1)}, bf16[1,384,1024]{2,1,0:T(8,128)(2,1)}, bf16[1,442944]{1,0:T(2,128)(2,1)}, bf16[1,655360]{1,0:T(2,128)(2,1)}, bf16[1,754240]{1,0:T(2,128)(2,1)}), ...) | async-done | bytes 4884752 | tf_op jit(solution)/shard_map/psum | solution.py:568
  4387.8 7.3 slice_reduce_fusion.4
  4399.2 16.2 slice_reduce_fusion
  4415.5 8.5 slice_reduce_fusion.3
  4432.3 12.2 slice_reduce_fusion.1
  (439 shorter events, 358.8 us)
Async XLA Ops:
  7.2 14.2 copy-start.103
  7.2 16.8 copy-start.104
  7.2 185.6 %all-gather.16.cloned.1.call-start = ((), (), s32[]{:S(2)}) async-start(), calls=%async_computation.10 | async-start | bytes 30124544 | tf_op jit(solution)/shard_map/all_gather | solution.py:183
  46.3 583.1 %all-gather.14.cloned.1.call-start = ((), (), s32[]{:S(2)}) async-start(), calls=%async_computation.9 | async-start | bytes 95857152 | tf_op jit(solution)/shard_map/all_gather | solution.py:183
  61.7 9.7 copy-start.101
  72.7 647.8 %all-gather.10.cloned.1.call-start = ((), (), s32[]{:S(2)}) async-start(), calls=%async_computation.4 | async-start | bytes 3932160 | tf_op jit(solution)/shard_map/all_gather | solution.py:325
  72.8 647.7 %copy-start.3 = (f32[1,256,768]{2,1,0:T(8,128)}, f32[1,256,768]{2,1,0:T(8,128)S(1)}, u32[]{:S(2)}) copy-start(f32[1,256,768]{2,1,0:T(8,128)S(1)} %convert_element_type.431) | copy-start | bytes 2359300
  223.7 496.8 %copy-start.7 = (bf16[1,256,2304]{2,1,0:T(8,128)(2,1)}, bf16[1,256,2304]{2,1,0:T(8,128)(2,1)S(1)}, u32[]{:S(2)}) copy-start(bf16[1,256,2304]{2,1,0:T(8,128)(2,1)S(1)} %get-tuple-element.2016) | copy-start | bytes 3538948
  225.0 590.5 %all-gather.8.cloned.1.call-start = ((), (), s32[]{:S(2)}) async-start(), calls=%async_computation.3 | async-start | bytes 7864320 | tf_op jit(solution)/shard_map/all_gather | solution.py:326
  226.4 589.1 %copy-start = (f32[1,384,1024]{2,1,0:T(8,128)}, f32[1,384,1024]{2,1,0:T(8,128)S(1)}, u32[]{:S(2)}) copy-start(f32[1,384,1024]{2,1,0:T(8,128)S(1)} %convert_element_type.429) | copy-start | bytes 4718596
  696.7 146.8 %all-gather.12.cloned.1.call-start = ((), (), s32[]{:S(2)}) async-start(), calls=%async_computation.5 | async-start | bytes 5242880 | tf_op jit(solution)/shard_map/all_gather | solution.py:372
  710.0 10.5 copy-start.69
  710.1 10.4 copy-start.78
  730.3 19.0 copy-start.21
  772.6 30.0 collective-permute-start
  804.1 406.7 %reduce-scatter.4.cloned.1.call-start = ((), (), s32[]{:S(2)}) async-start(), calls=%async_computation.6 | async-start | bytes 5242880 | tf_op jit(solution)/shard_map/reduce_scatter | solution.py:438
  815.5 28.0 copy-start.90
  818.9 24.6 copy-start.16
  818.9 24.6 copy-start.75
  881.4 555.0 %reduce-scatter.8.cloned.1.call-start = ((), (), s32[]{:S(2)}) async-start(), calls=%async_computation.8 | async-start | bytes 7864320 | tf_op jit(solution)/shard_map/reduce_scatter | solution.py:513
  898.1 312.7 %copy-start.34 = (bf16[768,2048]{1,0:T(8,128)(2,1)S(1)}, bf16[768,2048]{1,0:T(8,128)(2,1)}, u32[]{:S(2)}) copy-start(bf16[768,2048]{1,0:T(8,128)(2,1)} %reshape.1642) | copy-start | bytes 9437188
  898.2 589.8 %reduce-scatter.6.cloned.1.call-start = ((), (), s32[]{:S(2)}) async-start(), calls=%async_computation.7 | async-start | bytes 3932160 | tf_op jit(solution)/shard_map/reduce_scatter | solution.py:510
  1214.3 109.0 %collective-permute-start.1 = (bf16[1,256,768]{2,1,0:T(8,128)(2,1)S(1)}, bf16[1,256,768]{2,1,0:T(8,128)(2,1)S(1)}, u32[]{:S(2)}, u32[]{:S(2)}) collective-permute-start(bf16[1,256,768]{2,1,0:T(8,128)(2,1)S(1)} %get-tuple-element.609), channel_id=1, source_target_pairs={{16,0},{17,1},{18,2},{19,3},{20,4},{21,5},{22,6},{23,7},{24,8},{25... | collective-permute-start | bytes 1179656 | tf_op jit(solution)/shard_map/ppermute | solution.py:19
  1215.6 11.4 copy-start.82
  1304.5 18.8 copy-start.8
  1304.5 18.8 copy-start.70
  1304.5 18.8 copy-start.79
  1323.3 14.2 copy-start.60
  1323.3 14.2 slice-start.3
  1324.8 16.7 copy-start.87
  1326.2 15.3 copy-start.96
  1326.2 11.4 slice-start.4
  1344.1 38.8 copy-start.12
  1397.3 10.8 copy-start.99
  1397.3 11.5 copy-start.62
  1420.4 10.7 copy-start.91
  1420.4 10.7 copy-start.13
  1436.3 2944.3 %all-reduce.11.cloned.1.call-start = ((), (), s32[]{:S(2)}) async-start(), calls=%async_computation.11 | async-start | bytes 17180672 | tf_op jit(solution)/shard_map/psum | solution.py:568
  1453.2 34.7 copy-start.4
  1453.2 34.7 copy-start.68
  1453.3 34.7 copy-start.77
  1532.9 9.6 copy-start.84
  1532.9 12.5 copy-start.83
  1575.8 26.9 copy-start.86
  4380.6 15.8 copy-start.43
  4399.2 26.2 copy-start.42
  4428.6 17.7 copy-start.65
  4430.6 16.5 copy-start.57
  (48 other events, 187.6 us)
Sparse Core Ops, SparseCore 0:
  46.4 146.3 all-gather.15
  194.4 434.9 all-gather.13
  631.5 28.9 all-gather.9
  696.8 109.6 all-gather.7
  808.4 35.0 all-gather.11
  881.5 329.2 reduce-scatter.3
  1213.5 122.7 reduce-scatter.7
  1436.4 36.9 reduce-scatter.5
  4104.2 276.3 all-reduce.10
where the time goes:
time: 4490 us; the launch traced here: 4470 us
  blocking collectives  2590 us (58%)
  waiting for transfers between devices  1020 us (23%)
  local copies, waits for them, and re-layouts  634 us (14%)
  matrix products  104 us (2%)
  other arithmetic  74.9 us (2%)
    unnamed x1, blocking collectives  2480 us
    all_gather x2, waiting for transfers between devices, fetch(): lax.all_gather(flattened, ('wide', 'narrow'), axis=0, tiled=True)  523 us
    reduce_scatter x1, waiting for transfers between devices, local(): lax.psum_scatter(cross_partial.astype(jnp.bfloat16), 'narrow', scatter_di...  313 us
    unnamed x157, local copies, waits for them, and re-layouts  311 us
    psum x1, waiting for transfers between devices, local(): lax.psum(img_grad.astype(jnp.bfloat16), 'grp').astype(jnp.float32)  163 us
    psum x1, blocking collectives, local(): lax.psum((total, live_count), ('grp', 'wide', 'narrow'))  112 us
  transfers between devices with their start and end apart: 11, of which 5 were waited for; matrix products, arithmetic and copies ran while one was open for 11% of the time, Pallas kernels for 0%

commit v1 on v0

v1 whole, which is shorter than its diff:
```python
import functools
import types

import jax
import jax.numpy as jnp
from jax import lax
from jax.experimental import pallas as pl
from jax.experimental.pallas import tpu as pltpu
from jax.sharding import PartitionSpec as P

HEAD = 64
VIEWS = 4
NORM_EPS = 1e-06
PRECISE = lax.Precision.HIGHEST
F32 = jnp.float32
BF16 = jnp.bfloat16
MIB = 1 << 20
VMEM = pl.BlockSpec(memory_space=pltpu.VMEM)
HBM = pl.BlockSpec(memory_space=pl.ANY)
MESH = pl.DeviceIdType.MESH
BLOCKS = ("wide", "narrow")


def shape_of(shape, dtype):
    return jax.ShapeDtypeStruct(shape, dtype)


def to_bf16(value):
    return value.astype(BF16)


def dot_plain(a, b):
    return jnp.dot(a, b, preferred_element_type=F32)


def dot_right(a, b):
    return lax.dot_general(a, b, (((1,), (1,)), ((), ())), preferred_element_type=F32)


def dot_left(a, b):
    return lax.dot_general(a, b, (((0,), (0,)), ((), ())), preferred_element_type=F32)


class Crew:
    def __init__(self, send, recv, here, lines):
        self.send_sems, self.recv_sems, self.here_sems = send, recv, here
        self.used = self.kept = 0
        self.sent = []
        self.group = lax.axis_index("grp")
        self.wide = lax.axis_index("wide")
        self.narrow = lax.axis_index("narrow")
        self.at_core = self.narrow + 1 - 2 * lax.rem(self.narrow, 2)
        self.at_row = lax.rem(self.narrow + 2, 4)
        self.at_cross = lax.rem(self.at_core + 2, 4)
        self.grp = {"grp": 1 - self.group}
        self.core = {"narrow": self.at_core}
        self.row = {"narrow": self.at_row}
        self.places = [lax.rem(self.wide + d, 4) for d in (1, 2, 3)] if lines else []
        self.line = [{"wide": place} for place in self.places]

    def greet(self):
        barrier = pltpu.get_barrier_semaphore()
        targets = [self.grp, self.core, self.row] + self.line
        for target in targets:
            pl.semaphore_signal(barrier, inc=1, device_id=target, device_id_type=MESH)
        pl.semaphore_wait(barrier, len(targets))

    def send(self, source, landing, target):
        copy = pltpu.make_async_remote_copy(
            src_ref=source,
            dst_ref=landing,
            send_sem=self.send_sems.at[self.used],
            recv_sem=self.recv_sems.at[self.used],
            device_id=target,
            device_id_type=MESH,
        )
        self.used += 1
        self.sent.append(copy)
        copy.start()
        return copy

    def keep(self, source, landing):
        copy = pltpu.make_async_copy(source, landing, self.here_sems.at[self.kept])
        self.kept += 1
        copy.start()
        return copy

    def close(self):
        for copy in self.sent:
            copy.wait_send()


class Gather:
    def __init__(self, crew, piece, full, cut, buf):
        self.crew, self.piece, self.full, self.cut, self.buf = crew, piece, full, cut, buf
        self.steps = [self.start, self.turn, self.cross, self.finish]
        self.load = None

    def start(self):
        crew = self.crew
        source = self.piece.at[:, self.cut]
        own = self.full.at[crew.wide, crew.narrow, :, self.cut]
        self.own = crew.keep(source, own)
        self.lines = [crew.send(source, own, target) for target in crew.line]

    def turn(self):
        crew = self.crew
        self.own.wait()
        for copy in self.lines:
            copy.wait_recv()
        mine = self.full.at[:, crew.narrow, :, self.cut]
        self.row = crew.send(mine, mine, crew.row)
        self.core = crew.send(mine, mine, crew.core)

    def cross(self):
        crew = self.crew
        self.row.wait_recv()
        other = self.full.at[:, crew.at_row, :, self.cut]
        self.far = crew.send(other, other, crew.core)

    def finish(self):
        self.core.wait_recv()
        self.far.wait_recv()
        if self.buf is not None:
            self.load = self.crew.keep(
                self.full.at[:, :, :, self.cut], self.buf.at[:, :, :, self.cut]
            )


class Scatter:
    def __init__(self, crew, part, pair, single, lines, out):
        self.crew, self.part, self.pair, self.single, self.lines = crew, part, pair, single, lines
        self.out = out
        self.steps = [self.start, self.turn, self.along, self.over, self.finish]

    def start(self):
        crew, part = self.crew, self.part
        self.core = crew.send(part.at[:, crew.at_core], self.pair.at[0], crew.core)
        self.far = crew.send(part.at[:, crew.at_cross], self.pair.at[1], crew.core)

    def add(self, place, landing):
        part = self.part

        def one(i, carry):
            total = part[i, place].astype(F32) + landing[i].astype(F32)
            part[i, place] = total.astype(part.dtype)
            return carry

        lax.fori_loop(0, part.shape[0], one, 0)

    def turn(self):
        crew = self.crew
        self.far.wait_recv()
        self.add(crew.at_row, self.pair.at[1])
        self.row = crew.send(self.part.at[:, crew.at_row], self.single, crew.row)
        self.core.wait_recv()
        self.add(crew.narrow, self.pair.at[0])

    def along(self):
        crew, part = self.crew, self.part
        self.row.wait_recv()
        self.add(crew.narrow, self.single)
        self.copies = [
            crew.send(part.at[place, crew.narrow], self.lines.at[i], target)
            for i, (place, target) in enumerate(zip(crew.places, crew.line))
        ]

    def over(self):
        crew, part = self.crew, self.part
        for copy in self.copies:
            copy.wait_recv()
        total = part[crew.wide, crew.narrow].astype(F32)
        for i in range(3):
            total = total + self.lines[i].astype(F32)
        self.out[0] = total.astype(self.out.dtype)
        self.other = crew.send(self.out.at[0], self.out.at[1], crew.grp)

    def finish(self):
        self.other.wait_recv()


class Pipe:
    def __init__(self, ahead):
        self.ahead, self.queue, self.jobs = ahead, [], []

    def plan(self, job):
        job.at = 0
        self.queue.append(job)

    def begin(self, job):
        job.steps[0]()
        job.at = 1
        self.jobs.append(job)

    def fill(self):
        while self.queue and sum(job.at == 1 for job in self.jobs) < self.ahead:
            self.begin(self.queue.pop(0))

    def pump(self):
        fresh = False
        for job in list(self.jobs):
            if job.at == 1:
                if fresh:
                    continue
                fresh = True
            job.steps[job.at]()
            job.at += 1
            if job.at == len(job.steps):
                self.jobs.remove(job)
        self.fill()

    def need(self, job):
        while job.at < len(job.steps):
            self.pump()

    def drain(self):
        while self.jobs or self.queue:
            self.pump()


class Matrix:
    def __init__(self, buf, pipe):
        self.buf, self.pipe, self.jobs, self.load = buf, pipe, [], None

    def need(self, index=None):
        for i, job in enumerate(self.jobs):
            if index is None or index == i:
                self.pipe.need(job)
                if not getattr(job, "loaded", False):
                    job.load.wait()
                    job.loaded = True
        if self.load is not None:
            self.load.wait()
            self.load = None

    def cols(self, cut):
        value = self.buf[..., cut]
        return value.reshape(-1, value.shape[-1])

    def rows(self, i):
        if len(self.buf.shape) == 4:
            return self.buf[i].reshape(-1, self.buf.shape[3])
        height = self.buf.shape[0] // 4
        return self.buf[pl.ds(i * height, height), :]

    def half(self, index):
        if len(self.buf.shape) == 4:
            return self.buf[pl.ds(index * 2, 2)].reshape(-1, self.buf.shape[3])
        height = self.buf.shape[0] // 2
        return self.buf[pl.ds(pl.multiple_of(index * height, height), height), :]

    def all(self):
        return self.cols(slice(None))


class Part:
    def __init__(self, body, **named):
        self.body = body
        self.ins = named.get("ins", {})
        self.outs = named.get("outs", {})
        self.scratch = named.get("scratch", {})
        self.given = named.get("given", {})
        self.moved = named.get("moved", {})
        self.sums = named.get("sums", {})


def grad_scratch(rows, cols, dtype):
    return (
        pltpu.VMEM((2, 4, rows, cols), dtype),
        pltpu.VMEM((4, rows, cols), dtype),
        pltpu.VMEM((3, rows, cols), dtype),
    )


def run(parts, collective, lines, ahead=2, links=0, flops=0, moved=0, limit=61):
    arrays, in_specs, out_shapes, out_specs, scratch = [], [], [], [], []
    layout = []
    for part in parts:
        named = []
        for name, value in part.ins.items():
            arrays.append(value)
            in_specs.append(VMEM)
        for name, value in part.given.items():
            arrays.append(value)
            in_specs.append(HBM)
            scratch.append(pltpu.VMEM(value.shape, BF16))
        for name, (_, piece, _, loaded) in part.moved.items():
            arrays.append(piece)
            in_specs.append(HBM)
            shape = (4, 4) + piece.shape
            out_shapes.append(shape_of(shape, piece.dtype))
            out_specs.append(HBM)
            if loaded:
                scratch.append(pltpu.VMEM(shape, piece.dtype))
        for name, value in part.outs.items():
            out_shapes.append(value)
            out_specs.append(VMEM)
        for name, (rows, cols, weight, dtype) in part.sums.items():
            out_shapes.append(shape_of((2, rows, cols), dtype))
            out_specs.append(VMEM)
            scratch.extend(grad_scratch(rows, cols, dtype))
            if weight is None:
                scratch.append(pltpu.VMEM((4, 4, rows, cols), dtype))
        for name, value in part.scratch.items():
            scratch.append(value)
    n_in, n_out = len(arrays), len(out_shapes)
    count = max(links, 1)
    scratch = scratch + [pltpu.SemaphoreType.DMA((count,))] * 3

    def kernel(*refs):
        ins, outs = iter(refs[:n_in]), iter(refs[n_in : n_in + n_out])
        rest = iter(refs[n_in + n_out : -3])
        crew = Crew(*refs[-3:], lines)
        pipe = Pipe(ahead)
        crew.greet()
        planned, spaces, loads = [], [], []
        for part in parts:
            space = types.SimpleNamespace()
            for name in part.ins:
                setattr(space, name, next(ins))
            for name in part.given:
                matrix = Matrix(next(rest), pipe)
                loads.append((matrix, next(ins)))
                setattr(space, name, matrix)
            for name, (order, piece, cuts, loaded) in part.moved.items():
                source, full = next(ins), next(outs)
                buf = next(rest) if loaded else None
                matrix = Matrix(buf, pipe)
                setattr(space, name, matrix)
                for i, cut in enumerate(cuts):
                    job = Gather(crew, source, full, cut, buf)
                    matrix.jobs.append(job)
                    planned.append((order + 0.01 * i, job))
            for name in part.outs:
                setattr(space, name, next(outs))
            for name, (rows, cols, weight, dtype) in part.sums.items():
                out = next(outs)
                landings = [next(rest) for _ in range(3)]
                own = next(rest) if weight is None else getattr(space, weight).buf
                setattr(space, "d_" + name, Scatter(crew, own, *landings, out))
            for name in part.scratch:
                setattr(space, name, next(rest))
            spaces.append(space)
        for _, job in sorted(planned, key=lambda entry: entry[0]):
            pipe.plan(job)
        pipe.fill()
        for matrix, source in loads:
            matrix.load = crew.keep(source, matrix.buf)
        strands = [part.body(space, crew, pipe) for part, space in zip(parts, spaces)]
        while strands:
            for strand in list(strands):
                if next(strand, True):
                    strands.remove(strand)
        pipe.drain()
        for matrix, _ in loads:
            matrix.need()
        crew.close()

    results = pl.pallas_call(
        kernel,
        out_shape=out_shapes,
        in_specs=in_specs,
        out_specs=out_specs,
        scratch_shapes=scratch,
        compiler_params=pltpu.CompilerParams(
            vmem_limit_bytes=limit * MIB, collective_id=collective, has_side_effects=True
        ),
        cost_estimate=pl.CostEstimate(
            flops=int(flops), bytes_accessed=int(moved), transcendentals=0
        ),
    )(*arrays)
    results = iter(results)
    given = []
    for part in parts:
        space = types.SimpleNamespace()
        for name in part.moved:
            setattr(space, name, next(results))
        for name in part.outs:
            setattr(space, name, next(results))
        for name in part.sums:
            setattr(space, "d_" + name, next(results))
        given.append(space)
    return given


def normalise(x):
    centered = x - jnp.mean(x, -1, keepdims=True)
    scale = lax.rsqrt(jnp.mean(centered * centered, -1, keepdims=True) + NORM_EPS)
    return centered * scale, scale


def norm_back(values, gain, grad):
    xhat, scale = normalise(values)
    inner = grad * gain
    term = inner - jnp.mean(inner, -1, keepdims=True)
    term = term - xhat * jnp.mean(inner * xhat, -1, keepdims=True)
    return (
        term * scale,
        jnp.sum(grad * xhat, 0, keepdims=True),
        jnp.sum(grad, 0, keepdims=True),
    )


def column_sums(value):
    return jnp.sum(value.astype(F32), 0, keepdims=True)


def gelu_pair(pre):
    cdf = 0.5 * (1.0 + lax.erf(pre * 0.7071067811865476))
    return cdf, pre * cdf


def gelu_slope(pre):
    return gelu_pair(pre)[0] + pre * (0.3989422804014327 * jnp.exp(-0.5 * pre * pre))


def head_masks(rows):
    lane = lax.broadcasted_iota(jnp.int32, (rows, 2 * HEAD), 1)
    return [lane < HEAD, lane >= HEAD]


class Spread:
    def __init__(self, crew, keyvals):
        self.crew, self.keyvals = crew, keyvals
        self.row = crew.send(keyvals.at[0], keyvals.at[2], crew.row)
        self.core = crew.send(keyvals.at[0], keyvals.at[1], crew.core)

    def cross(self):
        self.row.wait_recv()
        self.far = self.crew.send(self.keyvals.at[2], self.keyvals.at[3], self.crew.core)

    def finish(self):
        self.core.wait_recv()
        self.far.wait_recv()


class Fold:
    def __init__(self, crew, dkeyvals, landing):
        self.crew, self.dkeyvals, self.landing = crew, dkeyvals, landing
        self.core = crew.send(dkeyvals.at[1], landing.at[0], crew.core)
        self.far = crew.send(dkeyvals.at[3], landing.at[1], crew.core)

    def turn(self):
        dkeyvals, landing = self.dkeyvals, self.landing
        self.far.wait_recv()
        dkeyvals[2] = (dkeyvals[2].astype(F32) + landing[1].astype(F32)).astype(BF16)
        self.row = self.crew.send(dkeyvals.at[2], landing.at[2], self.crew.row)

    def finish(self):
        landing = self.landing
        self.core.wait_recv()
        own = self.dkeyvals[0].astype(F32) + landing[0].astype(F32)
        self.row.wait_recv()
        return (own + landing[2].astype(F32)).astype(BF16)


def attend(q_ref, keyvals, out_ref, out_first, sums_ref, half, first, last):
    rows = q_ref.shape[0]
    masks = head_masks(rows)

    def pair(i, carry):
        cut = pl.ds(pl.multiple_of(i * 2 * HEAD, 2 * HEAD), 2 * HEAD)
        cut_v = pl.ds(pl.multiple_of(half + i * 2 * HEAD, 2 * HEAD), 2 * HEAD)
        q_now = q_ref[:, cut] * BF16(HEAD**-0.5)
        parts = []
        for a in range(2):
            q_head = jnp.where(masks[a], q_now, BF16(0))
            scores = [dot_right(keyvals[j, :, cut], q_head) for j in range(4)]
            top = functools.reduce(jnp.maximum, [jnp.max(s, 0, keepdims=True) for s in scores])
            total, mixed = 0.0, 0.0
            for j in range(4):
                e = jnp.exp(scores[j] - top)
                total = total + jnp.sum(e, 0, keepdims=True)
                mixed = mixed + dot_left(keyvals[j, :, cut_v], e.astype(BF16))
            parts.append(mixed[a * HEAD : (a + 1) * HEAD] * (1.0 / total))
            sums_ref[i, a : a + 1, :] = top + jnp.log(total)
        place = pl.ds(pl.multiple_of(out_first + i * 2 * HEAD, 2 * HEAD), 2 * HEAD)
        out_ref[:, place] = jnp.concatenate(parts, 0).T.astype(BF16)
        return carry

    lax.fori_loop(first, last, pair, 0)


def attend_back(q_ref, keyvals, sums_ref, g_ref, dq_ref, dkeyvals, half, first, last):
    rows = q_ref.shape[0]
    masks = head_masks(rows)

    def pair(i, carry):
        cut = pl.ds(pl.multiple_of(i * 2 * HEAD, 2 * HEAD), 2 * HEAD)
        cut_v = pl.ds(pl.multiple_of(half + i * 2 * HEAD, 2 * HEAD), 2 * HEAD)
        q_now = q_ref[:, cut] * BF16(HEAD**-0.5)
        parts, dk_first, dv_first = [], [], []
        for a in range(2):
            q_head = jnp.where(masks[a], q_now, BF16(0))
            g_head = jnp.where(masks[a], g_ref[:, cut], BF16(0))
            log_sum = sums_ref[i, a : a + 1, :]
            weights, dweights, delta = [], [], 0.0
            for j in range(4):
                p = jnp.exp(dot_right(keyvals[j, :, cut], q_head) - log_sum)
                dp = dot_right(keyvals[j, :, cut_v], g_head)
                delta = delta + jnp.sum(p * dp, 0, keepdims=True)
                weights.append(p)
                dweights.append(dp)
            mixed = 0.0
            for j in range(4):
                ds = (weights[j] * (dweights[j] - delta)).astype(BF16)
                dk = dot_plain(ds, q_head)
                dv = dot_plain(weights[j].astype(BF16), g_head)
                mixed = mixed + dot_left(keyvals[j, :, cut], ds)
                if a == 0:
                    dk_first.append(dk)
                    dv_first.append(dv)
                else:
                    dkeyvals[j, :, cut] = (dk_first[j] + dk).astype(BF16)
                    dkeyvals[j, :, cut_v] = (dv_first[j] + dv).astype(BF16)
            parts.append(mixed[a * HEAD : (a + 1) * HEAD] * HEAD**-0.5)
        dq_ref[:, cut] = jnp.concatenate(parts, 0).T.astype(BF16)
        return carry

    lax.fori_loop(first, last, pair, 0)


def own_cut(crew, half):
    return pl.ds(pl.multiple_of(crew.group * half, half), half)


def send_half(crew, buffer, half):
    cut = own_cut(crew, half)
    return crew.send(buffer.at[:, cut], buffer.at[:, cut], crew.grp)


def grad_into(job, pipe, x, grad):
    part = job.part
    wide, narrow, rows, cols = part.shape
    width = 512 if cols % 512 == 0 else 384
    turned = x[...].T
    for first in range(0, cols, width):
        cut = pl.ds(first, width)
        term = dot_plain(turned, grad[:, first : first + width])
        part[:, :, :, cut] = term.astype(part.dtype).reshape(wide, narrow, rows, width)
    pipe.begin(job)


def begin_part(cam, mod, small, enc_qkv, dec_qkv):
    width = mod.shape[1]
    depth = mod.shape[0]

    def body(r, crew, pipe):
        cams = r.cams
        copies = [
            crew.send(r.cam.at[place * 4 + crew.narrow], cams.at[crew.wide], target)
            for place, target in zip(crew.places, crew.line)
        ]
        cams[crew.wide] = r.cam[crew.wide * 4 + crew.narrow]
        for copy in copies:
            copy.wait_recv()
        rows = cams[...].reshape(4, cams.shape[2])[:, :depth]
        high = to_bf16(rows)
        left = rows - high.astype(F32)
        middle = to_bf16(left)
        low = to_bf16(left - middle.astype(F32))
        terms = [dot_plain(part, r.mod[...]) for part in (high, middle, low)]
        r.terms[...] = (terms[0] + (terms[1] + terms[2])).reshape(4, 1, width)
        copies = [
            crew.send(r.terms.at[place], r.landed.at[i], target)
            for i, (place, target) in enumerate(zip(crew.places, crew.line))
        ]
        for copy in copies:
            copy.wait_recv()
        r.held[0] = r.terms[crew.wide] + (r.landed[0] + r.landed[1] + r.landed[2])
        crew.send(r.held.at[0], r.held.at[1], crew.core).wait_recv()
        r.held[2] = r.held[0] + r.held[1]
        crew.send(r.held.at[2], r.held.at[3], crew.row).wait_recv()
        r.modulation[...] = r.held[2] + r.held[3]
        yield

    return Part(
        body,
        ins=dict(cam=cam, mod=mod),
        moved=dict(
            small=(0, small, [slice(None)], False),
            enc_qkv=(1, enc_qkv, [slice(None)], False),
            dec_qkv=(2, dec_qkv, [pl.ds(i * 512, 512) for i in range(3)], False),
        ),
        outs=dict(
            modulation=shape_of((1, width), F32),
            cams=shape_of((4, 1, 128), F32),
        ),
        scratch=dict(
            terms=pltpu.VMEM((4, 1, width), F32),
            landed=pltpu.VMEM((3, 1, width), F32),
            held=pltpu.VMEM((4, 1, width), F32),
        ),
    )


def encoder_part(x, params, given, moved, cross_half):
    rows, width = x.shape
    half = width // 2
    inner = params["bias_fc1"].shape[1]
    pairs = half // (2 * HEAD)

    def body(r, crew, pipe):
        x_now = r.x[...].astype(F32)
        normed = normalise(x_now)[0] * r.gain_one[...] + r.shift_one[...]
        r.normed_one[...] = to_bf16(normed)
        r.qkv.need()
        out = dot_plain(r.normed_one[...], r.qkv.all()) + r.bias_qkv[...]
        r.queries[...] = to_bf16(out[:, :half])
        r.keyvals[0] = to_bf16(out[:, half:])
        spread = Spread(crew, r.keyvals)
        yield
        spread.cross()
        pipe.pump()
        yield
        spread.finish()
        attend(r.queries, r.keyvals, r.attended, crew.group * half, r.sums, half, 0, pairs)
        copy = send_half(crew, r.attended, half)
        pipe.pump()
        yield
        r.proj.need()
        copy.wait_recv()
        hidden = r.x[...].astype(F32) + dot_plain(r.attended[...], r.proj.all())
        hidden = hidden + r.bias_proj[...]
        r.hidden[...] = hidden
        normed = normalise(hidden)[0] * r.gain_two[...] + r.shift_two[...]
        r.normed_two[...] = to_bf16(normed)
        r.fc1.need()
        step = inner // 4
        total = 0.0
        for i in range(4):
            cut = pl.ds(i * step, step)
            pre = dot_plain(r.normed_two[...], r.fc1.cols(cut)) + r.bias_fc1[:, cut]
            r.pre[:, cut] = pre
            act = to_bf16(gelu_pair(pre)[1])
            r.act[:, cut] = act
            if i == 0:
                r.fc2.need()
            total = total + dot_plain(act, r.fc2.rows(i))
        r.term[...] = to_bf16(total)
        copy = crew.send(r.term, r.landed, crew.grp)
        pipe.pump()
        yield
        copy.wait_recv()
        both = r.term[...].astype(F32) + r.landed[...].astype(F32)
        r.image[...] = to_bf16(r.hidden[...] + both + r.bias_fc2[...])
        r.cross_kv.need()
        r.cross_keyvals[0] = to_bf16(dot_plain(r.image[...], r.cross_kv.all()))
        spread = Spread(crew, r.cross_keyvals)
        yield
        spread.cross()
        yield
        spread.finish()

    ins = dict(x=x)
    ins.update(params)
    return Part(
        body,
        ins=ins,
        given=given,
        moved=moved,
        outs=dict(
            normed_one=shape_of((rows, width), BF16),
            queries=shape_of((rows, half), BF16),
            keyvals=shape_of((4, rows, width), BF16),
            attended=shape_of((rows, width), BF16),
            sums=shape_of((pairs, 2, rows), F32),
            hidden=shape_of((rows, width), F32),
            normed_two=shape_of((rows, width), BF16),
            pre=shape_of((rows, inner), F32),
            act=shape_of((rows, inner), BF16),
            image=shape_of((rows, width), BF16),
            cross_keyvals=shape_of((4, rows, 2 * cross_half), BF16),
        ),
        scratch=dict(term=pltpu.VMEM((rows, width), BF16), landed=pltpu.VMEM((rows, width), BF16)),
    )


def self_part(x, modulation, given, moved):
    rows, width = x.shape
    half = width // 2
    pairs = half // (2 * HEAD)

    def body(r, crew, pipe):
        normed = normalise(r.x[...].astype(F32))[0]
        r.normed_one[...] = to_bf16(normed * (1.0 + r.modulation[0:1]) + r.modulation[1:2])
        r.qkv.need()
        for i in range(3):
            cut = pl.ds(i * half, half)
            out = to_bf16(dot_plain(r.normed_one[...], r.qkv.cols(cut)))
            if i == 0:
                r.queries[...] = out
            else:
                r.keyvals[0, :, pl.ds((i - 1) * half, half)] = out
        spread = Spread(crew, r.keyvals)
        yield
        spread.cross()
        yield
        spread.finish()
        first = crew.group * half
        attend(r.queries, r.keyvals, r.attended, first, r.sums, half, 0, pairs // 2)
        pipe.pump()
        attend(r.queries, r.keyvals, r.attended, first, r.sums, half, pairs // 2, pairs)
        copy = send_half(crew, r.attended, half)
        pipe.pump()
        yield
        r.proj.need()
        copy.wait_recv()
        after = r.x[...].astype(F32) + dot_plain(r.attended[...], r.proj.all())
        r.after_self[...] = after
        normed = normalise(after)[0] * (1.0 + r.modulation[2:3]) + r.modulation[3:4]
        r.normed_two[...] = to_bf16(normed)
        r.cross_q.need()
        r.cross_queries[...] = to_bf16(dot_plain(r.normed_two[...], r.cross_q.all()))

    return Part(
        body,
        ins=dict(x=x, modulation=modulation),
        given=given,
        moved=moved,
        outs=dict(
            normed_one=shape_of((rows, width), BF16),
            queries=shape_of((rows, half), BF16),
            keyvals=shape_of((4, rows, width), BF16),
            attended=shape_of((rows, width), BF16),
            sums=shape_of((pairs, 2, rows), F32),
            after_self=shape_of((rows, width), F32),
            normed_two=shape_of((rows, width), BF16),
            cross_queries=shape_of((rows, half), BF16),
        ),
    )


def cross_part(queries, keyvals, after_self, modulation, bias_fc1, bias_fc2, given, moved):
    rows, width = after_self.shape
    half = width // 2
    pairs = half // (2 * HEAD)
    inner = bias_fc1.shape[1]

    def body(r, crew, pipe):
        first = crew.group * half
        attend(r.queries, r.keyvals, r.attended, first, r.sums, half, 0, pairs // 2)
        pipe.pump()
        attend(r.queries, r.keyvals, r.attended, first, r.sums, half, pairs // 2, pairs)
        copy = send_half(crew, r.attended, half)
        pipe.pump()
        r.proj.need()
        copy.wait_recv()
        after = r.after_self[...] + dot_plain(r.attended[...], r.proj.all())
        r.after_cross[...] = after
        normed = normalise(after)[0] * (1.0 + r.modulation[4:5]) + r.modulation[5:6]
        r.normed_three[...] = to_bf16(normed)
        step = inner // 4
        for i in range(4):
            if i % 2 == 0:
                r.fc1.need(i // 2)
            cut = pl.ds(i * step, step)
            pre = dot_plain(r.normed_three[...], r.fc1.cols(cut)) + r.bias_fc1[:, cut]
            r.pre[:, cut] = pre
            r.act[:, cut] = to_bf16(gelu_pair(pre)[1])
        copies = []
        for i in range(2):
            r.fc2.need(i)
            cut = pl.ds(i * half, half)
            r.term[:, cut] = to_bf16(dot_plain(r.act[...], r.fc2.cols(cut)))
            copies.append(crew.send(r.term.at[:, cut], r.landed.at[:, cut], crew.grp))
        for i, copy in enumerate(copies):
            cut = pl.ds(i * half, half)
            copy.wait_recv()
            both = r.term[:, cut].astype(F32) + r.landed[:, cut].astype(F32)
            r.final[:, cut] = r.after_cross[:, cut] + both + r.bias_fc2[:, cut]
        yield

    return Part(
        body,
        ins=dict(
            queries=queries,
            keyvals=keyvals,
            after_self=after_self,
            modulation=modulation,
            bias_fc1=bias_fc1,
            bias_fc2=bias_fc2,
        ),
        given=given,
        moved=moved,
        outs=dict(
            attended=shape_of((rows, width), BF16),
            sums=shape_of((pairs, 2, rows), F32),
            after_cross=shape_of((rows, width), F32),
            normed_three=shape_of((rows, width), BF16),
            pre=shape_of((rows, inner), F32),
            act=shape_of((rows, inner), BF16),
            final=shape_of((rows, width), F32),
        ),
        scratch=dict(term=pltpu.VMEM((rows, width), BF16), landed=pltpu.VMEM((rows, width), BF16)),
    )


def feed_back(r, grad):
    inner = r.pre.shape[1]
    step = inner // 4
    total = 0.0
    r.fc2.need()
    for i in range(4):
        cut = pl.ds(i * step, step)
        dact = dot_right(grad, r.fc2.rows(i))
        dpre = to_bf16(gelu_slope(r.pre[:, cut]) * dact)
        r.dpre[:, cut] = dpre
        r.pre_sums[:, cut] = column_sums(dpre)
        if i == 0:
            r.fc1.need()
        total = total + dot_right(dpre, r.fc1.cols(cut))
    return to_bf16(total)


def both_of(r):
    return r.term[...].astype(F32) + r.landed[...].astype(F32)


def cross_back_part(ins, given, sums):
    rows, width = ins["after_cross"].shape
    inner = ins["pre"].shape[1]
    held, image_width = ins["image"].shape
    half = width // 2
    pairs = half // (2 * HEAD)
    moving = bool(sums)

    def body(r, crew, pipe):
        r.branch[...] = to_bf16(r.grad[...])
        r.term[...] = feed_back(r, r.branch[...])
        copy = crew.send(r.term, r.landed, crew.grp)
        if moving:
            grad_into(r.d_fc2, pipe, r.act, r.branch)
            grad_into(r.d_fc1, pipe, r.normed_three, r.dpre)
        copy.wait_recv()
        gain = 1.0 + r.modulation[4:5]
        grad_in, r.gamma_three[...], r.beta_three[...] = norm_back(
            r.after_cross[...], gain, both_of(r)
        )
        after = r.grad[...] + grad_in
        r.grad_after[...] = after
        r.cross_branch[...] = to_bf16(after)
        r.proj.need()
        r.dattended[...] = to_bf16(dot_right(r.cross_branch[...], r.proj.half(crew.group)))
        pipe.pump()
        args = (r.queries, r.keyvals, r.sums, r.dattended, r.cross_dq, r.dkeyvals, half)
        attend_back(*args, 0, pairs // 2)
        pipe.pump()
        attend_back(*args, pairs // 2, pairs)
        fold = Fold(crew, r.dkeyvals, r.landing)
        r.cross_q.need()
        r.term_two[...] = to_bf16(dot_right(r.cross_dq[...], r.cross_q.all()))
        copy = crew.send(r.term_two, r.landed_two, crew.grp)
        fold.turn()
        pipe.pump()
        copy.wait_recv()
        gain = 1.0 + r.modulation[2:3]
        both = r.term_two[...].astype(F32) + r.landed_two[...].astype(F32)
        grad_in, r.gamma_two[...], r.beta_two[...] = norm_back(r.after_self[...], gain, both)
        r.cross_dkv[...] = fold.finish()
        r.cross_kv.need()
        r.term_image[...] = to_bf16(dot_right(r.cross_dkv[...], r.cross_kv.all()))
        copy = crew.send(r.term_image, r.landed_image, crew.grp)
        r.grad_self[...] = r.grad_after[...] + grad_in
        pipe.pump()
        copy.wait_recv()
        both = r.term_image[...].astype(F32) + r.landed_image[...].astype(F32)
        r.image_grad[...] = to_bf16(both)
        yield

    outs = dict(
        pre_sums=shape_of((1, inner), F32),
        gamma_three=shape_of((1, width), F32),
        beta_three=shape_of((1, width), F32),
        gamma_two=shape_of((1, width), F32),
        beta_two=shape_of((1, width), F32),
        cross_branch=shape_of((rows, width), BF16),
        cross_dq=shape_of((rows, half), BF16),
        cross_dkv=shape_of((held, width), BF16),
        grad_self=shape_of((rows, width), F32),
        image_grad=shape_of((held, image_width), BF16),
    )
    wide_row = pltpu.VMEM((rows, width), BF16)
    scratch = dict(
        branch=wide_row,
        term=wide_row,
        landed=wide_row,
        term_two=wide_row,
        landed_two=wide_row,
        grad_after=pltpu.VMEM((rows, width), F32),
        dattended=pltpu.VMEM((rows, half), BF16),
        dkeyvals=pltpu.VMEM((4, held, width), BF16),
        landing=pltpu.VMEM((3, held, width), BF16),
        term_image=pltpu.VMEM((held, image_width), BF16),
        landed_image=pltpu.VMEM((held, image_width), BF16),
    )
    if moving:
        scratch.update(dpre=pltpu.VMEM((rows, inner), BF16))
    else:
        outs.update(dpre=shape_of((rows, inner), BF16))
    return Part(body, ins=ins, given=given, sums=sums, outs=outs, scratch=scratch)


def self_back_part(ins, given, sums):
    rows, width = ins["x"].shape
    half = width // 2
    pairs = half // (2 * HEAD)
    moving = bool(sums)

    def body(r, crew, pipe):
        r.branch[...] = to_bf16(r.grad_self[...])
        r.proj.need()
        r.dattended[...] = to_bf16(dot_right(r.branch[...], r.proj.half(crew.group)))
        if moving:
            grad_into(
                r.d_cross_proj,
                pipe,
                r.cross_attended,
                r.cross_branch[:, own_cut(crew, half)],
            )
            grad_into(r.d_cross_q, pipe, r.normed_two, r.cross_dq)
            grad_into(r.d_cross_kv, pipe, r.image, r.cross_dkv)
        yield
        args = (r.queries, r.keyvals, r.sums, r.dattended, r.dq, r.dkeyvals, half)
        attend_back(*args, 0, pairs // 2)
        pipe.pump()
        attend_back(*args, pairs // 2, pairs)
        fold = Fold(crew, r.dkeyvals, r.landing)
        if moving:
            grad_into(r.d_proj, pipe, r.attended, r.branch[:, own_cut(crew, half)])
        yield
        fold.turn()
        r.drows[:, pl.ds(0, half)] = r.dq[...]
        pipe.pump()
        yield
        r.drows[:, pl.ds(half, 2 * half)] = fold.finish()
        r.qkv.need()
        r.term[...] = to_bf16(dot_right(r.drows[...], r.qkv.all()))
        copy = crew.send(r.term, r.landed, crew.grp)
        if moving:
            grad_into(r.d_qkv, pipe, r.normed_one, r.drows)
        yield
        copy.wait_recv()
        gain = 1.0 + r.modulation[0:1]
        grad_in, r.gamma_one[...], r.beta_one[...] = norm_back(
            r.x[...].astype(F32), gain, both_of(r)
        )
        r.x_grad[...] = r.grad_self[...] + grad_in

    outs = dict(
        gamma_one=shape_of((1, width), F32),
        beta_one=shape_of((1, width), F32),
        x_grad=shape_of((rows, width), F32),
    )
    wide_row = pltpu.VMEM((rows, width), BF16)
    scratch = dict(
        term=wide_row,
        landed=wide_row,
        dattended=pltpu.VMEM((rows, half), BF16),
        dq=pltpu.VMEM((rows, half), BF16),
        dkeyvals=pltpu.VMEM((4, rows, width), BF16),
        landing=pltpu.VMEM((3, rows, width), BF16),
    )
    if moving:
        scratch.update(branch=wide_row, drows=pltpu.VMEM((rows, 3 * half), BF16))
    else:
        outs.update(
            branch=shape_of((rows, width), BF16), drows=shape_of((rows, 3 * half), BF16)
        )
    return Part(body, ins=ins, given=given, sums=sums, outs=outs, scratch=scratch)


def encoder_back_part(ins, given, sums):
    rows, width = ins["x"].shape
    half = width // 2
    pairs = half // (2 * HEAD)
    inner = ins["pre"].shape[1]
    moving = bool(sums)

    def body(r, crew, pipe):
        r.term[...] = feed_back(r, r.image_grad[...])
        copy = crew.send(r.term, r.landed, crew.grp)
        if moving:
            grad_into(r.d_fc2, pipe, r.act, r.image_grad)
            grad_into(r.d_fc1, pipe, r.normed_two, r.dpre)
        yield
        copy.wait_recv()
        grad_in, r.gain_two_grad[...], r.shift_two_grad[...] = norm_back(
            r.hidden[...], r.gain_two[...], both_of(r)
        )
        grad_hidden = r.image_grad[...].astype(F32) + grad_in
        r.grad_hidden[...] = grad_hidden
        r.branch[...] = to_bf16(grad_hidden)
        r.branch_sums[...] = column_sums(r.branch[...])
        r.proj.need()
        r.dattended[...] = to_bf16(dot_right(r.branch[...], r.proj.half(crew.group)))
        pipe.pump()
        attend_back(
            r.queries, r.keyvals, r.sums, r.dattended, r.dq, r.dkeyvals, half, 0, pairs
        )
        fold = Fold(crew, r.dkeyvals, r.landing)
        if moving:
            grad_into(r.d_proj, pipe, r.attended, r.branch[:, own_cut(crew, half)])
        yield
        fold.turn()
        r.drows[:, pl.ds(0, half)] = r.dq[...]
        pipe.pump()
        yield
        r.drows[:, pl.ds(half, 2 * half)] = fold.finish()
        r.row_sums[...] = column_sums(r.drows[...])
        r.qkv.need()
        r.term_two[...] = to_bf16(dot_right(r.drows[...], r.qkv.all()))
        copy = crew.send(r.term_two, r.landed_two, crew.grp)
        if moving:
            grad_into(r.d_qkv, pipe, r.normed_one, r.drows)
        yield
        copy.wait_recv()
        both = r.term_two[...].astype(F32) + r.landed_two[...].astype(F32)
        grad_in, r.gain_one_grad[...], r.shift_one_grad[...] = norm_back(
            r.x[...].astype(F32), r.gain_one[...], both
        )
        r.x_grad[...] = r.grad_hidden[...] + grad_in

    vector = shape_of((1, width), F32)
    outs = dict(
        pre_sums=shape_of((1, inner), F32),
        gain_two_grad=vector,
        shift_two_grad=vector,
        branch_sums=vector,
        row_sums=shape_of((1, 3 * half), F32),
        gain_one_grad=vector,
        shift_one_grad=vector,
        x_grad=shape_of((rows, width), F32),
    )
    wide_row = pltpu.VMEM((rows, width), BF16)
    scratch = dict(
        term=wide_row,
        landed=wide_row,
        term_two=wide_row,
        landed_two=wide_row,
        grad_hidden=pltpu.VMEM((rows, width), F32),
        dattended=pltpu.VMEM((rows, half), BF16),
        dq=pltpu.VMEM((rows, half), BF16),
        dkeyvals=pltpu.VMEM((4, rows, width), BF16),
        landing=pltpu.VMEM((3, rows, width), BF16),
    )
    if moving:
        scratch.update(
            branch=wide_row,
            dpre=pltpu.VMEM((rows, inner), BF16),
            drows=pltpu.VMEM((rows, 3 * half), BF16),
        )
    else:
        outs.update(
            branch=shape_of((rows, width), BF16),
            dpre=shape_of((rows, inner), BF16),
            drows=shape_of((rows, 3 * half), BF16),
        )
    return Part(body, ins=ins, given=given, sums=sums, outs=outs, scratch=scratch)


def end_part(small, mods):
    width = mods.shape[1]

    def body(r, crew, pipe):
        r.d_small.part[...] = r.packed[...]
        pipe.begin(r.d_small)
        copy = crew.send(r.mods, r.held.at[0], crew.core)
        copy.wait_recv()
        r.held[1] = r.mods[...] + r.held[0]
        copy = crew.send(r.held.at[1], r.held.at[2], crew.row)
        pipe.pump()
        copy.wait_recv()
        r.held[3] = r.held[1] + r.held[2]
        r.everyone[crew.wide] = r.held[3]
        copies = [
            crew.send(r.held.at[3], r.everyone.at[crew.wide], target) for target in crew.line
        ]
        pipe.pump()
        for copy in copies:
            copy.wait_recv()
        yield

    return Part(
        body,
        ins=dict(packed=small, mods=mods),
        outs=dict(everyone=shape_of((4, 1, width), F32)),
        sums=dict(small=(small.shape[2], small.shape[3], None, F32)),
        scratch=dict(held=pltpu.VMEM((4, 1, width), F32)),
    )


def plain_grad(x, grad):
    term = to_bf16(dot_left(x, grad))
    return lax.psum_scatter(term, BLOCKS, scatter_dimension=0, tiled=True)


def take(value, index, axis):
    return lax.dynamic_index_in_dim(value, index, axis, False)


def ray_loss(final_rows, head_weight, target_rgb, foreground, valid_rays):
    predicted = jnp.dot(final_rows, head_weight, precision=PRECISE)
    colour = jax.nn.sigmoid(predicted[:, :3])
    residue = colour - jnp.swapaxes(target_rgb, 0, 1)
    opacity = predicted[:, 3]
    per_ray = jnp.sum(residue * residue, -1) + jax.nn.softplus(opacity) - foreground * opacity
    return jnp.sum(valid_rays * per_ray)


def local(
    img_in,
    tri_in,
    cam,
    targets,
    fg_mask,
    counts,
    ln1_gain,
    ln1_bias,
    enc_qkv,
    enc_qv_bias,
    enc_proj,
    enc_proj_bias,
    ln2_gain,
    ln2_bias,
    enc_fc1,
    enc_fc1_bias,
    enc_fc2,
    enc_fc2_bias,
    dec_mod,
    dec_qkv,
    dec_proj,
    dec_cross_q,
    dec_cross_kv,
    dec_cross_proj,
    dec_fc1,
    dec_fc1_bias,
    dec_fc2,
    dec_fc2_bias,
    dec_head,
):
    group = lax.axis_index("grp")
    wide = lax.axis_index("wide")
    narrow = lax.axis_index("narrow")
    wides = lax.axis_size("wide")
    blocks = wides * lax.axis_size("narrow")
    block = wide * lax.axis_size("narrow") + narrow
    moving = wides == 4
    enc_width = img_in.shape[2]
    plane_rows, dec_width = tri_in.shape[1:]
    enc_half, dec_half = enc_width // 2, dec_width // 2
    enc_ff, dec_ff = enc_fc1.shape[1], dec_fc1.shape[1]
    enc_inner, dec_inner = enc_ff // blocks // 2, dec_ff // blocks // 2
    mod_rows = dec_mod.shape[0]

    def columns(shard, parts, width):
        cut = take(shard.reshape(shard.shape[0], parts, 2, width), group, 2)
        return cut.reshape(shard.shape[0], parts * width)

    def half_rows(shard):
        return take(shard.reshape(2, shard.shape[0] // 2, shard.shape[1]), group, 0)

    small_parts = (
        ln1_gain,
        ln1_bias,
        enc_qv_bias,
        enc_proj_bias,
        ln2_gain,
        ln2_bias,
        enc_fc1_bias,
        enc_fc2_bias,
        dec_fc1_bias,
        dec_fc2_bias,
        dec_head.reshape(-1),
    )
    small = jnp.concatenate(small_parts)
    piece = types.SimpleNamespace(
        enc_qkv=columns(enc_qkv, 3, enc_half),
        dec_qkv=columns(dec_qkv, 3, dec_half),
        enc_proj=enc_proj,
        enc_fc1=columns(enc_fc1, blocks, enc_inner),
        enc_fc2=half_rows(enc_fc2),
        dec_proj=dec_proj,
        cross_q=columns(dec_cross_q, 1, dec_half),
        cross_kv=columns(dec_cross_kv, 2, dec_half),
        cross_proj=dec_cross_proj,
        dec_fc1=columns(dec_fc1, blocks, dec_inner),
        dec_fc2=half_rows(dec_fc2),
    )

    if moving:
        length = small.shape[0]
        padded = jnp.pad(small, (0, 16 * 128 - length)).reshape(16, 128)
        cam_blocks = jnp.pad(cam.reshape(blocks, 1, mod_rows), ((0, 0), (0, 0), (0, 128 - mod_rows)))
        (first,) = run(
            [begin_part(cam_blocks, dec_mod, padded, piece.enc_qkv, piece.dec_qkv)],
            1,
            True,
            links=64,
        )
        small_all = first.small.reshape(blocks, 16 * 128)[:, :length]
        modulation = first.modulation.reshape(6, dec_width)
        cam_cut = first.cams.reshape(4, 128)[:, :mod_rows]
        full = types.SimpleNamespace(enc_qkv=first.enc_qkv, dec_qkv=first.dec_qkv)
    else:
        small_all = lax.all_gather(small, BLOCKS, axis=0)
        cam_all = lax.all_gather(cam, "wide", axis=0, tiled=True)
        cam_cut = lax.dynamic_slice_in_dim(cam_all, block * mod_rows, mod_rows, 1)
        term = jnp.dot(cam_cut, dec_mod.astype(F32), precision=PRECISE)
        term = lax.psum(term, "narrow")
        modulation = lax.psum_scatter(term, "wide", scatter_dimension=0, tiled=True)
        modulation = modulation.reshape(6, dec_width)
        full = types.SimpleNamespace(
            **{
                name: lax.all_gather(value, BLOCKS, axis=0, tiled=True)
                for name, value in vars(piece).items()
            }
        )
    unpacked, offset = [], 0
    for part in small_parts:
        length = part.shape[0]
        unpacked.append(small_all[:, offset : offset + length].reshape(1, -1).astype(F32))
        offset += length
    (
        gain_one,
        shift_one,
        bias_qv,
        bias_proj,
        gain_two,
        shift_two,
        bias_fc1,
        bias_fc2,
        bias_dfc1,
        bias_dfc2,
        head_flat,
    ) = unpacked
    head = head_flat.reshape(dec_width, 4)
    qv_half = take(bias_qv.reshape(2, 2, enc_half), group, 1)
    bias_qkv = jnp.concatenate([qv_half[0], jnp.zeros((enc_half,), F32), qv_half[1]])
    bias_qkv = bias_qkv.reshape(1, -1)
    fc1_half = take(bias_fc1.reshape(blocks, 2, enc_inner), group, 1).reshape(1, -1)
    dfc1_half = take(bias_dfc1.reshape(blocks, 2, dec_inner), group, 1).reshape(1, -1)

    ray_slots = plane_rows * lax.axis_size("narrow") // VIEWS
    row_index = narrow * plane_rows + jnp.arange(plane_rows, dtype=jnp.int32)
    view_index, slot_index = row_index // ray_slots, row_index % ray_slots
    view_ids = jnp.arange(VIEWS, dtype=jnp.int32)
    limits = jnp.sum(jnp.where(view_index[:, None] == view_ids[None, :], counts, 0), -1)
    valid_rays = (slot_index < limits).astype(F32)
    foreground = fg_mask[0].astype(F32)

    every = [slice(None)]

    def split(given, moved):
        if moving:
            return given, moved
        for name, (_, value, _, _) in moved.items():
            given[name] = full_of(value)
        return given, {}

    def full_of(value):
        for name, known in vars(piece).items():
            if known is value:
                return getattr(full, name)
        raise KeyError

    enc_given, enc_moved = split(
        dict(qkv=full.enc_qkv),
        dict(
            proj=(0, piece.enc_proj, every, True),
            fc1=(1, piece.enc_fc1, every, True),
            fc2=(2, piece.enc_fc2, every, True),
            cross_kv=(5, piece.cross_kv, every, True),
        ),
    )
    self_given, self_moved = split(
        dict(qkv=full.dec_qkv),
        dict(proj=(3, piece.dec_proj, every, True), cross_q=(4, piece.cross_q, every, True)),
    )
    enc, own = run(
        [
            encoder_part(
                img_in[0],
                dict(
                    gain_one=gain_one,
                    shift_one=shift_one,
                    bias_qkv=bias_qkv,
                    bias_proj=bias_proj,
                    gain_two=gain_two,
                    shift_two=shift_two,
                    bias_fc1=fc1_half,
                    bias_fc2=bias_fc2,
                ),
                enc_given,
                enc_moved,
                dec_half,
            ),
            self_part(tri_in[0], modulation, self_given, self_moved),
        ],
        2,
        moving,
        links=64,
    )
    if moving:
        full.enc_proj, full.enc_fc1, full.enc_fc2 = enc.proj, enc.fc1, enc.fc2
        full.cross_kv, full.dec_proj, full.cross_q = enc.cross_kv, own.proj, own.cross_q
    pair_cuts = [pl.ds(0, dec_ff // 4), pl.ds(dec_ff // 4, dec_ff // 4)]
    cross_given, cross_moved = split(
        dict(),
        dict(
            proj=(0, piece.cross_proj, every, True),
            fc1=(1, piece.dec_fc1, pair_cuts, True),
            fc2=(2, piece.dec_fc2, [pl.ds(0, dec_half), pl.ds(dec_half, dec_half)], True),
        ),
    )
    (cross,) = run(
        [
            cross_part(
                own.cross_queries,
                enc.cross_keyvals,
                own.after_self,
                modulation,
                dfc1_half,
                bias_dfc2,
                cross_given,
                cross_moved,
            )
        ],
        3,
        moving,
        links=64,
    )
    if moving:
        full.cross_proj, full.dec_fc1, full.dec_fc2 = cross.proj, cross.fc1, cross.fc2

    def ray_total(rows_in, head_in):
        return ray_loss(rows_in, head_in, targets[0], foreground, valid_rays)

    total, ray_pull = jax.vjp(ray_total, cross.final, head)
    grad_final, grad_head = ray_pull(jnp.ones((), F32))

    def sums_of(**named):
        return named if moving else {}

    (late,) = run(
        [
            cross_back_part(
                dict(
                    grad=grad_final,
                    pre=cross.pre,
                    act=cross.act,
                    normed_three=cross.normed_three,
                    after_cross=cross.after_cross,
                    modulation=modulation,
                    queries=own.cross_queries,
                    keyvals=enc.cross_keyvals,
                    sums=cross.sums,
                    after_self=own.after_self,
                    image=enc.image,
                ),
                dict(
                    fc2=full.dec_fc2,
                    fc1=full.dec_fc1,
                    proj=full.cross_proj,
                    cross_q=full.cross_q,
                    cross_kv=full.cross_kv,
                ),
                sums_of(
                    fc2=(piece.dec_fc2.shape[0], dec_width, "fc2", BF16),
                    fc1=(piece.dec_fc1.shape[0], dec_ff // 2, "fc1", BF16),
                ),
            )
        ],
        4,
        moving,
        links=64,
    )
    self_rows, enc_rows = dec_qkv.shape[0], enc_qkv.shape[0]
    (front,) = run(
        [
            self_back_part(
                dict(
                    grad_self=late.grad_self,
                    attended=own.attended,
                    queries=own.queries,
                    keyvals=own.keyvals,
                    sums=own.sums,
                    normed_one=own.normed_one,
                    x=tri_in[0],
                    modulation=modulation,
                    cross_attended=cross.attended,
                    cross_branch=late.cross_branch,
                    normed_two=own.normed_two,
                    cross_dq=late.cross_dq,
                    image=enc.image,
                    cross_dkv=late.cross_dkv,
                ),
                dict(proj=full.dec_proj, qkv=full.dec_qkv),
                sums_of(
                    cross_proj=(self_rows, dec_half, None, BF16),
                    cross_q=(self_rows, dec_half, None, BF16),
                    cross_kv=(enc_rows, dec_width, None, BF16),
                    proj=(self_rows, dec_half, None, BF16),
                    qkv=(self_rows, 3 * dec_half, "qkv", BF16),
                ),
            )
        ],
        5,
        moving,
        links=96,
    )
    (back,) = run(
        [
            encoder_back_part(
                dict(
                    image_grad=late.image_grad,
                    pre=enc.pre,
                    act=enc.act,
                    hidden=enc.hidden,
                    normed_one=enc.normed_one,
                    normed_two=enc.normed_two,
                    x=img_in[0],
                    attended=enc.attended,
                    queries=enc.queries,
                    keyvals=enc.keyvals,
                    sums=enc.sums,
                    gain_one=gain_one,
                    gain_two=gain_two,
                ),
                dict(
                    fc2=full.enc_fc2, fc1=full.enc_fc1, proj=full.enc_proj, qkv=full.enc_qkv
                ),
                sums_of(
                    fc2=(piece.enc_fc2.shape[0], enc_width, "fc2", BF16),
                    fc1=(enc_rows, enc_ff // 2, "fc1", BF16),
                    proj=(enc_rows, enc_half, None, BF16),
                    qkv=(enc_rows, 3 * enc_half, "qkv", BF16),
                ),
            )
        ],
        6,
        moving,
        links=96,
    )

    def placed(half, count, width):
        cut = half.reshape(count, 1, width)
        zero = jnp.zeros_like(cut)
        low = jnp.where(group == 0, cut, zero)
        high = jnp.where(group == 0, zero, cut)
        return jnp.concatenate([low, high], 1).reshape(-1)

    row_sums = back.row_sums[0]
    qv_sums = jnp.concatenate([row_sums[:enc_half], row_sums[2 * enc_half :]])
    loss_terms = jnp.stack([total, jnp.sum(valid_rays)])
    small_grads = (
        0.5 * back.gain_one_grad,
        0.5 * back.shift_one_grad,
        placed(qv_sums, 2, enc_half),
        0.5 * back.branch_sums,
        0.5 * back.gain_two_grad,
        0.5 * back.shift_two_grad,
        placed(back.pre_sums, blocks, enc_inner),
        0.5 * column_sums(late.image_grad),
        placed(late.pre_sums, blocks, dec_inner),
        0.5 * column_sums(to_bf16(grad_final)),
        0.5 * grad_head,
        jnp.tile(0.5 * loss_terms, blocks),
    )
    packed = jnp.concatenate([part.reshape(blocks, -1) for part in small_grads], 1)
    grad_mod = jnp.concatenate(
        [
            front.gamma_one,
            front.beta_one,
            late.gamma_two,
            late.beta_two,
            late.gamma_three,
            late.beta_three,
        ],
        1,
    )
    length = packed.shape[1]
    if moving:
        packed = jnp.pad(packed, ((0, 0), (0, 16 * 128 - length))).reshape(4, 4, 16, 128)
        (last,) = run([end_part(packed, grad_mod)], 7, True, links=32)
        small_sum = (last.d_small[0] + last.d_small[1]).reshape(-1)[:length]
        mod_all = last.everyone.reshape(4, -1)
    else:
        small_sum = take(lax.psum(packed, ("grp", "wide", "narrow")), block, 0)
        mod_all = lax.all_gather(lax.psum(grad_mod, "narrow"), "wide", axis=0, tiled=True)
    small_out, offset = [], 0
    for part in small_grads:
        count = part.size // blocks
        small_out.append(small_sum[offset : offset + count])
        offset += count
    loss = small_out[11][0] / small_out[11][1]
    grad_wmod = jnp.dot(jnp.transpose(cam_cut), mod_all, precision=PRECISE)

    def own_half(value):
        return take(value.reshape(value.shape[0], 2, -1), group, 1)

    def halves_of(reduced, x, grad):
        if not moving:
            half = plain_grad(x, grad)
            reduced = jnp.stack([half, lax.ppermute(half, "grp", [(0, 1), (1, 0)])])
        return jnp.where(group == 0, reduced, reduced[::-1]).astype(F32)

    def full_columns(halves, parts):
        cut = halves.reshape(2, halves.shape[1], parts, -1)
        return jnp.transpose(cut, (1, 2, 0, 3)).reshape(halves.shape[1], -1)

    def full_rows(halves):
        return halves.reshape(-1, halves.shape[2])

    def reduced_of(space, name):
        return getattr(space, name, None)

    if moving:
        self_branch = enc_branch = enc_dpre = dec_dpre = enc_drows = dec_drows = None
    else:
        self_branch, enc_branch = own_half(front.branch), own_half(back.branch)
        enc_dpre, dec_dpre, enc_drows, dec_drows = back.dpre, late.dpre, back.drows, front.drows
    cross_branch = own_half(late.cross_branch)
    get = reduced_of
    out_qkv = halves_of(get(back, "d_qkv"), enc.normed_one, enc_drows)
    out_proj = halves_of(get(back, "d_proj"), enc.attended, enc_branch)
    out_fc1 = halves_of(get(back, "d_fc1"), enc.normed_two, enc_dpre)
    out_fc2 = halves_of(get(back, "d_fc2"), enc.act, late.image_grad)
    out_dqkv = halves_of(get(front, "d_qkv"), own.normed_one, dec_drows)
    out_dproj = halves_of(get(front, "d_proj"), own.attended, self_branch)
    out_cq = halves_of(get(front, "d_cross_q"), own.normed_two, late.cross_dq)
    out_ckv = halves_of(get(front, "d_cross_kv"), enc.image, late.cross_dkv)
    out_cproj = halves_of(get(front, "d_cross_proj"), cross.attended, cross_branch)
    out_dfc1 = halves_of(get(late, "d_fc1"), cross.normed_three, dec_dpre)
    out_dfc2 = halves_of(get(late, "d_fc2"), cross.act, to_bf16(grad_final))

    return (
        loss,
        back.x_grad[None],
        front.x_grad[None],
        small_out[0],
        small_out[1],
        full_columns(out_qkv, 3),
        small_out[2],
        full_columns(out_proj, 1),
        small_out[3],
        small_out[4],
        small_out[5],
        full_columns(out_fc1, blocks),
        small_out[6],
        full_rows(out_fc2),
        small_out[7],
        grad_wmod,
        full_columns(out_dqkv, 3),
        full_columns(out_dproj, 1),
        full_columns(out_cq, 1),
        full_columns(out_ckv, 2),
        full_columns(out_cproj, 1),
        full_columns(out_dfc1, blocks),
        small_out[8],
        full_rows(out_dfc2),
        small_out[9],
        small_out[10].reshape(-1, 4),
    )


def solution(mesh):
    tokens = P("wide", "narrow", None)
    matrix = P(BLOCKS, None)
    vector = P(BLOCKS)
    objects = P("wide", None)
    rays = (P("wide", None, "narrow"), P("wide", "narrow"))
    encoder = (vector, vector, matrix, vector, matrix, vector, vector, vector, matrix, vector)
    encoder = encoder + (matrix, vector)
    decoder = (matrix,) * 7 + (vector, matrix, vector, matrix)
    return jax.shard_map(
        local,
        mesh=mesh,
        in_specs=(tokens, tokens, objects) + rays + (objects,) + encoder + decoder,
        out_specs=(P(), tokens, tokens) + encoder + decoder,
        check_vma=False,
    )
```

time: 4490 us -> 728 us (0.16)
  blocking collectives: 2590 us -> 0 us
  waiting for transfers between devices: 1020 us -> 0 us
  Pallas kernels: 0 us -> 635 us
  local copies, waits for them, and re-layouts: 634 us -> 60.1 us
  matrix products: 104 us -> 7.84 us
  other arithmetic: 74.9 us -> 10.9 us
    unnamed x1 -> x0, blocking collectives: 2480 us -> none
    pallas_call x0 -> x7, Pallas kernels: none -> 635 us  [run(): pl.pallas_call(kernel, out_shape=out_shapes, in_specs=in_specs, out_specs...]
    all_gather x5 -> x0, waiting for transfers between devices: 547 us -> none  [the longest x2 523 us: fetch(): lax.all_gather(flattened, ('wide', 'narrow'), axis=0, tiled=True)]
    reduce_scatter x3 -> x0, waiting for transfers between devices: 313 us -> none  [the longest x1 313 us: local(): lax.psum_scatter(cross_partial.astype(jnp.bfloat16), 'narrow', scatter_di...]
    unnamed x157 -> x99, local copies, waits for them, and re-layouts: 311 us -> 14.7 us
    psum x1 -> x0, waiting for transfers between devices: 163 us -> none  [local(): lax.psum(img_grad.astype(jnp.bfloat16), 'grp').astype(jnp.float32)]
    psum x1 -> x0, blocking collectives: 112 us -> none  [local(): lax.psum((total, live_count), ('grp', 'wide', 'narrow'))]
    reshape x45 -> x40, local copies, waits for them, and re-layouts: 124 us -> 20.7 us  [the longest x19 12.2 us: full_columns(): return jnp.transpose(cut, (1, 2, 0, 3)).reshape(halves.shape[1], -1)]
  transfers between devices with their start and end apart: 11 -> 0, of which waited for: 5 -> 0; matrix products, arithmetic and copies ran while one was open for 11% -> 0% of each run, Pallas kernels for 0% -> 0%
where the time goes in v1:
time: 728 us; the launch traced here: 719 us
  Pallas kernels  635 us (87%)
  local copies, waits for them, and re-layouts  60.1 us (8%)
  other arithmetic  10.9 us (1%)
  matrix products  7.84 us (1%)
    pallas_call x7, Pallas kernels, run(): pl.pallas_call(kernel, out_shape=out_shapes, in_specs=in_specs, out_specs...  635 us
    unnamed x99, local copies, waits for them, and re-layouts  14.7 us

profile of v1, /device:TPU:0, one launch (start us, length us, event | category | flops | bytes accessed | tf_op | source)
XLA Modules:
  0.0 718.6 jit_solution(5642654071553101251)
XLA Ops:
  0.7 1.0 copy-done
  1.7 0.7 convert_reduce_fusion.2
  2.4 0.7 select_reduce_fusion
  3.7 1.3 reduce.38
  5.7 0.8 copy.113
  6.6 6.8 concatenate.46
  14.0 1.0 reshape.646
  15.8 1.6 dynamic-slice_bitcast_fusion.1.refs_12_
  17.4 1.1 reshape.643
  19.8 0.7 dynamic-slice_reduce_fusion.3
  21.2 0.7 dynamic-slice_bitcast_fusion.refs_8_
  22.3 1.2 dynamic-slice_reduce_fusion.1
  23.6 0.9 reshape.641.refs_11_
  24.7 1.3 dynamic-slice_reduce_fusion.2
  26.0 0.7 copy.147
  27.1 1.5 dynamic-slice_reduce_fusion
  28.7 0.8 copy.170
  29.4 62.6 %shard_map.476 = (bf16[4,4,16,128]{3,2,1,0:T(8,128)(2,1)}, bf16[4,4,48,1152]{3,2,1,0:T(8,128)(2,1)}, bf16[4,4,64,1536]{3,2,1,0:T(8,128)(2,1)}, f32[1,6144]{1,0:T(1,128)}, f32[4,1,128]{2,1,0:T(1,128)}) custom-call(f32[16,1,128]{2,1,0:T(1,128)} %pad.18.refs_0_, bf16[64,6144]{1,0:T(8,128)(2,1)} %refs_1_.1, bf16[16,128]{1,0:T(8,128)(2,1)} %pad_bitcast_fusion.1.refs_2_, ...), custom_call_target="tpu_custom_call" | custom-call | tf_op jit(solution)/shard_map/pallas_call | solution.py:359
  92.0 0.9 copy.171
  95.3 1.4 reduce.39
  102.7 119.1 %shard_map.477 = (bf16[4,4,48,768]{3,2,1,0:T(8,128)(2,1)}, bf16[4,4,48,1536]{3,2,1,0:T(8,128)(2,1)}, bf16[4,4,96,768]{3,2,1,0:T(8,128)(2,1)}, bf16[4,4,48,1024]{...) custom-call(bf16[256,768]{1,0:T(8,128)(2,1)} %bitcast.150, ...), custom_call_target="tpu_custom_call" | custom-call | tf_op jit(solution)/shard_map/pallas_call | solution.py:359
  221.8 100.3 %shard_map.478 = (bf16[4,4,64,1024]{3,2,1,0:T(8,128)(2,1)}, bf16[4,4,64,2048]{3,2,1,0:T(8,128)(2,1)}, bf16[4,4,128,1024]{3,2,1,0:T(8,128)(2,1)}, bf16[384,1024]{...) custom-call(bf16[384,512]{1,0:T(8,128)(2,1)} %get-tuple-element.104., ...), custom_call_target="tpu_custom_call" | custom-call | tf_op jit(solution)/shard_map/pallas_call | solution.py:359
  322.1 2.3 fusion.40
  325.2 1.4 maximum_multiply_fusion
  326.6 0.9 convolution_multiply_fusion
  328.1 2.0 convert_reduce_fusion
  330.1 110.3 %shard_map.479 = (f32[1,2048]{1,0:T(1,128)}, f32[1,1024]{1,0:T(1,128)}, f32[1,1024]{1,0:T(1,128)}, f32[1,1024]{1,0:T(1,128)}, f32[1,1024]{1,0:T(1,128)}, /*index...) custom-call(f32[384,1024]{1,0:T(8,128)} %get-tuple-element.310.refs_, ...), custom_call_target="tpu_custom_call" | custom-call | tf_op jit(solution)/shard_map/pallas_call | solution.py:359
  440.3 92.6 %shard_map.480 = (f32[1,1536]{1,0:T(1,128)}, f32[1,768]{1,0:T(1,128)}, f32[1,768]{1,0:T(1,128)}, f32[1,768]{1,0:T(1,128)}, f32[1,1152]{1,0:T(1,128)}, /*index=5*...) custom-call(bf16[256,768]{1,0:T(8,128)(2,1)} %get-tuple-element.119., ...), custom_call_target="tpu_custom_call" | custom-call | tf_op jit(solution)/shard_map/pallas_call | solution.py:359
  533.1 129.9 %shard_map.481 = (f32[1,1024]{1,0:T(1,128)}, f32[1,1024]{1,0:T(1,128)}, f32[384,1024]{1,0:T(8,128)}, bf16[2,64,512]{2,1,0:T(8,128)(2,1)}, bf16[2,64,512]{2,1,0:T...) custom-call(f32[384,1024]{1,0:T(8,128)} %get-tuple-element.140.refs_0_, ...), custom_call_target="tpu_custom_call" | custom-call | tf_op jit(solution)/shard_map/pallas_call | solution.py:359
  664.3 0.7 constant_dynamic-update-slice_fusion.5
  665.1 0.7 constant_dynamic-update-slice_fusion.4
  666.5 20.6 %shard_map.482 = (f32[4,1,6144]{2,1,0:T(1,128)}, f32[2,16,128]{2,1,0:T(8,128)}) custom-call(f32[4,4,16,128]{3,2,1,0:T(8,128)} %bitcast.162, f32[1,6144]{1,0:T(1,128)} %copy-done.22), custom_call_target="tpu_custom_call" | custom-call | tf_op jit(solution)/shard_map/pallas_call | solution.py:359
  687.1 0.7 fusion.45
  687.8 0.7 slice_add_fusion
  695.3 0.8 copy.153
  696.1 0.9 bitcast_convert_fusion.1
  697.7 1.1 reshape.718
  699.4 1.1 reshape.704
  700.6 1.1 bitcast_convert_fusion
  702.0 0.8 copy.155
  703.0 0.8 copy.154
  704.7 1.9 reshape.708
  707.8 1.6 reshape.712
  709.8 0.8 copy.133
  710.6 1.8 reshape.722
  712.5 2.6 fusion.8
  715.0 0.9 copy.180
  715.9 1.1 copy.181
  (188 shorter events, 27.1 us)
Async XLA Ops:
  0.7 1.1 copy-start
  0.7 19.1 %copy-start.14 = (bf16[48,2304]{1,0:T(8,128)(2,1)S(1)}, bf16[48,2304]{1,0:T(8,128)(2,1)}, u32[]{:S(2)}) copy-start(bf16[48,2304]{1,0:T(8,128)(2,1)} %param.37) | copy-start | bytes 663556
  15.0 7.0 copy-start.13
  19.8 4.7 copy-start.9
  22.3 4.4 copy-start.6
  322.1 2.4 copy-start.23
  322.1 2.4 copy-start.25
  322.1 4.5 copy-start.2
  532.9 130.1 %copy-start.35 = (f32[1,768]{1,0:T(1,128)S(1)}, f32[1,768]{1,0:T(1,128)}, u32[]{:S(2)}) copy-start(f32[1,768]{1,0:T(1,128)} %get-tuple-element.132) | copy-start | bytes 9220
  532.9 130.1 %copy-start.37 = (f32[1,1152]{1,0:T(1,128)S(1)}, f32[1,1152]{1,0:T(1,128)}, u32[]{:S(2)}) copy-start(f32[1,1152]{1,0:T(1,128)} %get-tuple-element.134) | copy-start | bytes 13828
  532.9 130.4 %copy-start.4 = (bf16[256,768]{1,0:T(8,128)(2,1)S(1)}, bf16[256,768]{1,0:T(8,128)(2,1)}, u32[]{:S(2)}) copy-start(bf16[256,768]{1,0:T(8,128)(2,1)} %get-tuple-element.119.refs_0_) | copy-start | bytes 1179652
  533.0 130.6 %copy-start.24 = (f32[1,2048]{1,0:T(1,128)S(1)}, f32[1,2048]{1,0:T(1,128)}, u32[]{:S(2)}) copy-start(f32[1,2048]{1,0:T(1,128)} %get-tuple-element.139) | copy-start | bytes 24580
  533.0 130.6 %copy-start.33 = (f32[1,768]{1,0:T(1,128)S(1)}, f32[1,768]{1,0:T(1,128)}, u32[]{:S(2)}) copy-start(f32[1,768]{1,0:T(1,128)} %get-tuple-element.135) | copy-start | bytes 9220
  533.0 130.6 %copy-start.34 = (f32[1,768]{1,0:T(1,128)S(1)}, f32[1,768]{1,0:T(1,128)}, u32[]{:S(2)}) copy-start(f32[1,768]{1,0:T(1,128)} %get-tuple-element.133) | copy-start | bytes 9220
  533.0 130.8 %copy-start.31 = (f32[1,768]{1,0:T(1,128)S(1)}, f32[1,768]{1,0:T(1,128)}, u32[]{:S(2)}) copy-start(f32[1,768]{1,0:T(1,128)} %get-tuple-element.136) | copy-start | bytes 9220
  533.0 130.7 %copy-start.32 = (f32[1,768]{1,0:T(1,128)S(1)}, f32[1,768]{1,0:T(1,128)}, u32[]{:S(2)}) copy-start(f32[1,768]{1,0:T(1,128)} %get-tuple-element.137) | copy-start | bytes 9220
  533.0 130.9 %copy-start.26 = (f32[1,1536]{1,0:T(1,128)S(1)}, f32[1,1536]{1,0:T(1,128)}, u32[]{:S(2)}) copy-start(f32[1,1536]{1,0:T(1,128)} %get-tuple-element.138) | copy-start | bytes 18436
  533.0 132.7 %copy-start.30 = (f32[1,1024]{1,0:T(1,128)S(1)}, f32[1,1024]{1,0:T(1,128)}, u32[]{:S(2)}) copy-start(f32[1,1024]{1,0:T(1,128)} %get-tuple-element.154) | copy-start | bytes 12292
  533.0 132.7 %copy-start.29 = (f32[1,1024]{1,0:T(1,128)S(1)}, f32[1,1024]{1,0:T(1,128)}, u32[]{:S(2)}) copy-start(f32[1,1024]{1,0:T(1,128)} %get-tuple-element.155) | copy-start | bytes 12292
  533.0 132.7 %copy-start.28 = (f32[1,1024]{1,0:T(1,128)S(1)}, f32[1,1024]{1,0:T(1,128)}, u32[]{:S(2)}) copy-start(f32[1,1024]{1,0:T(1,128)} %get-tuple-element.156) | copy-start | bytes 12292
  533.0 132.7 %copy-start.27 = (f32[1,1024]{1,0:T(1,128)S(1)}, f32[1,1024]{1,0:T(1,128)}, u32[]{:S(2)}) copy-start(f32[1,1024]{1,0:T(1,128)} %get-tuple-element.157) | copy-start | bytes 12292
  663.0 31.3 %copy-start.21 = (bf16[2,48,384]{2,1,0:T(8,128)(2,1)S(1)}, bf16[2,48,384]{2,1,0:T(8,128)(2,1)}, u32[]{:S(2)}) copy-start(bf16[2,48,384]{2,1,0:T(8,128)(2,1)} %get-tuple-element.162) | copy-start | bytes 221188
  663.0 32.0 %copy-start.17 = (bf16[2,64,512]{2,1,0:T(8,128)(2,1)S(1)}, bf16[2,64,512]{2,1,0:T(8,128)(2,1)}, u32[]{:S(2)}) copy-start(bf16[2,64,512]{2,1,0:T(8,128)(2,1)} %get-tuple-element.168) | copy-start | bytes 393220
  664.3 31.7 %copy-start.12 = (bf16[2,96,768]{2,1,0:T(8,128)(2,1)S(1)}, bf16[2,96,768]{2,1,0:T(8,128)(2,1)}, u32[]{:S(2)}) copy-start(bf16[2,96,768]{2,1,0:T(8,128)(2,1)} %get-tuple-element.164) | copy-start | bytes 884740
  665.8 0.7 copy-start.22
  694.4 2.6 copy-start.16
  697.0 1.8 copy-start.15
  698.8 1.7 copy-start.8
  699.3 2.4 copy-start.18
  699.3 2.4 copy-start.19
  701.7 2.0 copy-start.11
  704.0 2.5 copy-start.10
  707.2 2.2 copy-start.7
  710.6 1.8 copy-start.20
  710.6 1.8 copy-start.36
  710.6 4.4 copy-start.5
  712.5 3.5 copy-start.3
  715.0 2.0 copy-start.1

commit v2 on v1

--- a/solution.py
+++ b/solution.py
@@ -44,7 +44,8 @@
 class Crew:
     def __init__(self, send, recv, here, lines):
         self.send_sems, self.recv_sems, self.here_sems = send, recv, here
-        self.used = self.kept = 0
+        self.used = self.kept = self.slotted = self.given = 0
+        self.credit = None
         self.sent = []
         self.group = lax.axis_index("grp")
         self.wide = lax.axis_index("wide")
@@ -94,7 +95,7 @@
     def __init__(self, crew, piece, full, cut, buf):
         self.crew, self.piece, self.full, self.cut, self.buf = crew, piece, full, cut, buf
         self.steps = [self.start, self.turn, self.cross, self.finish]
-        self.load = None
+        self.load, self.late = None, False
 
     def start(self):
         crew = self.crew
@@ -121,29 +122,97 @@
     def finish(self):
         self.core.wait_recv()
         self.far.wait_recv()
-        if self.buf is not None:
+        if self.buf is not None and not self.late:
+            self.fetch()
+
+    def fetch(self):
+        if self.load is None:
             self.load = self.crew.keep(
                 self.full.at[:, :, :, self.cut], self.buf.at[:, :, :, self.cut]
             )
 
 
+class GatherRow(Gather):
+    def start(self):
+        crew = self.crew
+        source = self.piece.at[:, self.cut]
+        own = self.full.at[crew.wide, crew.narrow, :, self.cut]
+        self.row = crew.send(source, own, crew.row)
+        self.own = crew.keep(source, own)
+        self.lines = [crew.send(source, own, target) for target in crew.line]
+
+    def turn(self):
+        crew = self.crew
+        self.row.wait_recv()
+        other = self.full.at[crew.wide, crew.at_row, :, self.cut]
+        self.lines += [crew.send(other, other, target) for target in crew.line]
+
+    def cross(self):
+        crew = self.crew
+        self.own.wait()
+        for copy in self.lines:
+            copy.wait_recv()
+        mine = self.full.at[:, crew.narrow, :, self.cut]
+        other = self.full.at[:, crew.at_row, :, self.cut]
+        self.core = crew.send(mine, mine, crew.core)
+        self.far = crew.send(other, other, crew.core)
+
+
+class GatherShared(Gather):
+    def __init__(self, crew, piece, full, cut, buf):
+        half = piece.shape[1] // 2
+        mine = pl.ds(pl.multiple_of(crew.group * half, half), half)
+        super().__init__(crew, piece, full, mine, buf)
+        self.steps = [self.start, self.turn, self.over, self.cross, self.finish]
+
+    def turn(self):
+        crew = self.crew
+        self.own.wait()
+        for copy in self.lines:
+            copy.wait_recv()
+        mine = self.full.at[:, crew.narrow, :, self.cut]
+        self.row = crew.send(mine, mine, crew.row)
+        self.others = [crew.send(mine, mine, crew.grp)]
+
+    def over(self):
+        crew = self.crew
+        self.row.wait_recv()
+        other = self.full.at[:, crew.at_row, :, self.cut]
+        self.others.append(crew.send(other, other, crew.grp))
+
+    def cross(self):
+        crew = self.crew
+        for copy in self.others:
+            copy.wait_recv()
+        mine, other = self.full.at[:, crew.narrow], self.full.at[:, crew.at_row]
+        self.core = crew.send(mine, mine, crew.core)
+        self.far = crew.send(other, other, crew.core)
+        self.cut = slice(None)
+
+
 class Scatter:
-    def __init__(self, crew, part, pair, single, lines, out):
-        self.crew, self.part, self.pair, self.single, self.lines = crew, part, pair, single, lines
-        self.out = out
+    def __init__(self, crew, whole, cut, index):
+        rows = whole.part.shape[2]
+        self.crew, self.part, self.cut, self.index = crew, whole.part, cut, index
+        self.pair = whole.slots.at[index % 2, :, :, pl.ds(0, rows), pl.ds(0, cut.size)]
+        self.single = whole.single.at[:, :, cut]
+        self.lines = whole.lines.at[:, :, cut]
+        self.out = whole.out.at[:, :, cut]
         self.steps = [self.start, self.turn, self.along, self.over, self.finish]
 
     def start(self):
         crew, part = self.crew, self.part
-        self.core = crew.send(part.at[:, crew.at_core], self.pair.at[0], crew.core)
-        self.far = crew.send(part.at[:, crew.at_cross], self.pair.at[1], crew.core)
+        if self.index >= 2:
+            pl.semaphore_wait(crew.credit, 1)
+        self.core = crew.send(part.at[:, crew.at_core, :, self.cut], self.pair.at[0], crew.core)
+        self.far = crew.send(part.at[:, crew.at_cross, :, self.cut], self.pair.at[1], crew.core)
 
     def add(self, place, landing):
-        part = self.part
+        part, cut = self.part, self.cut
 
         def one(i, carry):
-            total = part[i, place].astype(F32) + landing[i].astype(F32)
-            part[i, place] = total.astype(part.dtype)
+            total = part[i, place, :, cut].astype(F32) + landing[i].astype(F32)
+            part[i, place, :, cut] = total.astype(part.dtype)
             return carry
 
         lax.fori_loop(0, part.shape[0], one, 0)
@@ -152,16 +221,18 @@
         crew = self.crew
         self.far.wait_recv()
         self.add(crew.at_row, self.pair.at[1])
-        self.row = crew.send(self.part.at[:, crew.at_row], self.single, crew.row)
+        self.row = crew.send(self.part.at[:, crew.at_row, :, self.cut], self.single, crew.row)
         self.core.wait_recv()
         self.add(crew.narrow, self.pair.at[0])
+        if self.index < crew.slotted - 2:
+            pl.semaphore_signal(crew.credit, inc=1, device_id=crew.core, device_id_type=MESH)
 
     def along(self):
         crew, part = self.crew, self.part
         self.row.wait_recv()
         self.add(crew.narrow, self.single)
         self.copies = [
-            crew.send(part.at[place, crew.narrow], self.lines.at[i], target)
+            crew.send(part.at[place, crew.narrow, :, self.cut], self.lines.at[i], target)
             for i, (place, target) in enumerate(zip(crew.places, crew.line))
         ]
 
@@ -169,19 +240,72 @@
         crew, part = self.crew, self.part
         for copy in self.copies:
             copy.wait_recv()
-        total = part[crew.wide, crew.narrow].astype(F32)
+        total = part[crew.wide, crew.narrow, :, self.cut].astype(F32)
         for i in range(3):
             total = total + self.lines[i].astype(F32)
-        self.out[0] = total.astype(self.out.dtype)
-        self.other = crew.send(self.out.at[0], self.out.at[1], crew.grp)
+        own = self.out.at[crew.group]
+        own[...] = total.astype(part.dtype)
+        self.other = crew.send(own, own, crew.grp)
 
     def finish(self):
         self.other.wait_recv()
 
 
+class ScatterLine(Scatter):
+    def __init__(self, crew, whole, cut, index):
+        super().__init__(crew, whole, cut, index)
+        self.steps = [self.start, self.turn, self.along, self.over, self.finish]
+
+    def turn(self):
+        crew, part = self.crew, self.part
+        self.far.wait_recv()
+        self.add(crew.at_row, self.pair.at[1])
+        self.core.wait_recv()
+        self.add(crew.narrow, self.pair.at[0])
+        if self.index < crew.slotted - 2:
+            pl.semaphore_signal(crew.credit, inc=1, device_id=crew.core, device_id_type=MESH)
+        self.copies = [
+            [
+                crew.send(part.at[place, narrow, :, self.cut], landing.at[i], target)
+                for i, (place, target) in enumerate(zip(crew.places, crew.line))
+            ]
+            for narrow, landing in ((crew.at_row, self.single), (crew.narrow, self.lines))
+        ]
+
+    def total(self, copies, narrow, landing):
+        crew = self.crew
+        for copy in copies:
+            copy.wait_recv()
+        total = self.part[crew.wide, narrow, :, self.cut].astype(F32)
+        for i in range(3):
+            total = total + landing[i].astype(F32)
+        return total.astype(self.part.dtype)
+
+    def along(self):
+        crew, part = self.crew, self.part
+        own = part.at[crew.wide, crew.at_row, :, self.cut]
+        own[...] = self.total(self.copies[0], crew.at_row, self.single)
+        self.row = crew.send(own, self.single.at[3], crew.row)
+
+    def over(self):
+        crew = self.crew
+        total = self.total(self.copies[1], crew.narrow, self.lines)
+        self.row.wait_recv()
+        own = self.out.at[crew.group]
+        total = total.astype(F32) + self.single[3].astype(F32)
+        own[...] = total.astype(self.part.dtype)
+        self.other = crew.send(own, own, crew.grp)
+
+
+class Summed:
+    def __init__(self, part, single, lines, out, slots, kind):
+        self.part, self.single, self.lines, self.out, self.slots = part, single, lines, out, slots
+        self.kind = kind
+
+
 class Pipe:
     def __init__(self, ahead):
-        self.ahead, self.queue, self.jobs = ahead, [], []
+        self.ahead, self.queue, self.jobs, self.pending = ahead, [], [], None
 
     def plan(self, job):
         job.at = 0
@@ -196,39 +320,63 @@
         while self.queue and sum(job.at == 1 for job in self.jobs) < self.ahead:
             self.begin(self.queue.pop(0))
 
-    def pump(self):
-        fresh = False
-        for job in list(self.jobs):
-            if job.at == 1:
-                if fresh:
-                    continue
-                fresh = True
-            job.steps[job.at]()
-            job.at += 1
-            if job.at == len(job.steps):
-                self.jobs.remove(job)
+    def settle(self):
+        if self.pending is not None:
+            self.pending.turn()
+            self.pending.at = 2
+            self.jobs.append(self.pending)
+            self.pending = None
+
+    def add(self, job):
+        job.start()
+        self.settle()
+        self.pending = job
+
+    def go(self, job):
+        job.steps[job.at]()
+        job.at += 1
+        if job.at == len(job.steps):
+            self.jobs.remove(job)
+
+    def pump(self, lag=1):
+        before = self.pending
+        self.settle()
+        waiting = {}
+        for job in self.jobs:
+            if job is not before:
+                waiting.setdefault(job.at, []).append(job)
+        for at in sorted(waiting, reverse=True):
+            if at == 1 or len(waiting[at]) > lag:
+                self.go(waiting[at][0])
         self.fill()
 
     def need(self, job):
         while job.at < len(job.steps):
             self.pump()
+            if job.at and job.at < len(job.steps):
+                self.go(job)
 
     def drain(self):
-        while self.jobs or self.queue:
-            self.pump()
+        while self.jobs or self.queue or self.pending is not None:
+            self.pump(0)
 
 
 class Matrix:
     def __init__(self, buf, pipe):
         self.buf, self.pipe, self.jobs, self.load = buf, pipe, [], None
+        self.loaded = []
 
     def need(self, index=None):
-        for i, job in enumerate(self.jobs):
-            if index is None or index == i:
-                self.pipe.need(job)
-                if not getattr(job, "loaded", False):
-                    job.load.wait()
-                    job.loaded = True
+        wanted = [job for i, job in enumerate(self.jobs) if index is None or index == i]
+        for job in wanted:
+            self.pipe.need(job)
+        for job in self.jobs:
+            if job.at == len(job.steps):
+                job.fetch()
+        for job in wanted:
+            if job not in self.loaded:
+                job.load.wait()
+                self.loaded.append(job)
         if self.load is not None:
             self.load.wait()
             self.load = None
@@ -243,12 +391,6 @@
         height = self.buf.shape[0] // 4
         return self.buf[pl.ds(i * height, height), :]
 
-    def half(self, index):
-        if len(self.buf.shape) == 4:
-            return self.buf[pl.ds(index * 2, 2)].reshape(-1, self.buf.shape[3])
-        height = self.buf.shape[0] // 2
-        return self.buf[pl.ds(pl.multiple_of(index * height, height), height), :]
-
     def all(self):
         return self.cols(slice(None))
 
@@ -257,22 +399,35 @@
     def __init__(self, body, **named):
         self.body = body
         self.ins = named.get("ins", {})
+        self.far = named.get("far", {})
         self.outs = named.get("outs", {})
         self.scratch = named.get("scratch", {})
         self.given = named.get("given", {})
+        self.links = named.get("links", {})
+        self.late = named.get("late", {})
+        self.halves = named.get("halves", {})
         self.moved = named.get("moved", {})
         self.sums = named.get("sums", {})
 
 
+def cuts_of(piece):
+    cols = piece.shape[1]
+    width = width_of(cols)
+    return [pl.ds(first, width) for first in range(0, cols, width)]
+
+
+def width_of(cols):
+    for width in (512, 384):
+        if cols % width == 0:
+            return width
+    return cols
+
+
 def grad_scratch(rows, cols, dtype):
-    return (
-        pltpu.VMEM((2, 4, rows, cols), dtype),
-        pltpu.VMEM((4, rows, cols), dtype),
-        pltpu.VMEM((3, rows, cols), dtype),
-    )
-
-
-def run(parts, collective, lines, ahead=2, links=0, flops=0, moved=0, limit=61):
+    return pltpu.VMEM((4, rows, cols), dtype), pltpu.VMEM((3, rows, cols), dtype)
+
+
+def run(parts, collective, lines, order=(), ahead=4, links=0, flops=0, moved=0, limit=63):
     arrays, in_specs, out_shapes, out_specs, scratch = [], [], [], [], []
     layout = []
     for part in parts:
@@ -280,22 +435,29 @@
         for name, value in part.ins.items():
             arrays.append(value)
             in_specs.append(VMEM)
+        for name, value in part.far.items():
+            arrays.append(value)
+            in_specs.append(HBM)
         for name, value in part.given.items():
             arrays.append(value)
             in_specs.append(HBM)
             scratch.append(pltpu.VMEM(value.shape, BF16))
-        for name, (_, piece, _, loaded) in part.moved.items():
+        for name, value in part.halves.items():
+            arrays.append(value)
+            in_specs.append(HBM)
+            scratch.append(pltpu.VMEM((value.shape[0] // 2,) + value.shape[1:], BF16))
+        for name, (_, _, piece, _, loaded) in part.moved.items():
             arrays.append(piece)
             in_specs.append(HBM)
             shape = (4, 4) + piece.shape
             out_shapes.append(shape_of(shape, piece.dtype))
             out_specs.append(HBM)
-            if loaded:
+            if loaded and name not in part.late:
                 scratch.append(pltpu.VMEM(shape, piece.dtype))
         for name, value in part.outs.items():
             out_shapes.append(value)
             out_specs.append(VMEM)
-        for name, (rows, cols, weight, dtype) in part.sums.items():
+        for name, (kind, rows, cols, weight, dtype) in part.sums.items():
             out_shapes.append(shape_of((2, rows, cols), dtype))
             out_specs.append(VMEM)
             scratch.extend(grad_scratch(rows, cols, dtype))
@@ -305,12 +467,23 @@
             scratch.append(value)
     n_in, n_out = len(arrays), len(out_shapes)
     count = max(links, 1)
+    summed = [entry for part in parts for entry in part.sums.values()]
+    slotted = sum(cols // width_of(cols) for _, _, cols, _, _ in summed)
+    if summed:
+        depth = max(rows for _, rows, _, _, _ in summed)
+        span = max(width_of(cols) for _, _, cols, _, _ in summed)
+        scratch.append(pltpu.VMEM((2, 2, 4, depth, span), summed[0][4]))
+        scratch.append(pltpu.SemaphoreType.REGULAR)
     scratch = scratch + [pltpu.SemaphoreType.DMA((count,))] * 3
 
     def kernel(*refs):
         ins, outs = iter(refs[:n_in]), iter(refs[n_in : n_in + n_out])
         rest = iter(refs[n_in + n_out : -3])
         crew = Crew(*refs[-3:], lines)
+        slots = None
+        if summed:
+            slots, crew.credit = refs[-5:-3]
+            crew.slotted = slotted
         pipe = Pipe(ahead)
         crew.greet()
         planned, spaces, loads = [], [], []
@@ -318,35 +491,56 @@
             space = types.SimpleNamespace()
             for name in part.ins:
                 setattr(space, name, next(ins))
+            for name in part.far:
+                setattr(space, name, next(ins))
             for name in part.given:
                 matrix = Matrix(next(rest), pipe)
                 loads.append((matrix, next(ins)))
                 setattr(space, name, matrix)
-            for name, (order, piece, cuts, loaded) in part.moved.items():
+            for name in part.halves:
+                matrix = Matrix(next(rest), pipe)
+                height = matrix.buf.shape[0]
+                first = pl.multiple_of(crew.group * height, height)
+                loads.append((matrix, next(ins).at[pl.ds(first, height)]))
+                setattr(space, name, matrix)
+            for name, (kind, rank, piece, cuts, loaded) in part.moved.items():
                 source, full = next(ins), next(outs)
-                buf = next(rest) if loaded else None
+                buf = next(rest) if loaded and name not in part.late else None
                 matrix = Matrix(buf, pipe)
                 setattr(space, name, matrix)
                 for i, cut in enumerate(cuts):
-                    job = Gather(crew, source, full, cut, buf)
+                    job = kind(crew, source, full, cut, buf)
                     matrix.jobs.append(job)
-                    planned.append((order + 0.01 * i, job))
+                    planned.append((rank + 0.01 * i, job))
             for name in part.outs:
                 setattr(space, name, next(outs))
-            for name, (rows, cols, weight, dtype) in part.sums.items():
+            for name, (kind, rows, cols, weight, dtype) in part.sums.items():
                 out = next(outs)
-                landings = [next(rest) for _ in range(3)]
+                single, lines_in = next(rest), next(rest)
                 own = next(rest) if weight is None else getattr(space, weight).buf
-                setattr(space, "d_" + name, Scatter(crew, own, *landings, out))
+                setattr(space, "d_" + name, Summed(own, single, lines_in, out, slots, kind))
             for name in part.scratch:
                 setattr(space, name, next(rest))
             spaces.append(space)
+        for part, space in zip(parts, spaces):
+            for name, (other, known) in part.links.items():
+                setattr(space, name, getattr(spaces[parts.index(other)], known))
+        for part, space in zip(parts, spaces):
+            for name, (held, _) in part.late.items():
+                cols = part.moved[name][2].shape[1]
+                rows_in = part.moved[name][2].shape[0]
+                matrix = getattr(space, name)
+                matrix.buf = getattr(space, held).at[:, :, pl.ds(0, rows_in), pl.ds(0, cols)]
+                for job in matrix.jobs:
+                    job.buf, job.late = matrix.buf, part.late[name][1]
         for _, job in sorted(planned, key=lambda entry: entry[0]):
             pipe.plan(job)
         pipe.fill()
         for matrix, source in loads:
             matrix.load = crew.keep(source, matrix.buf)
         strands = [part.body(space, crew, pipe) for part, space in zip(parts, spaces)]
+        for i in order:
+            next(strands[i], None)
         while strands:
             for strand in list(strands):
                 if next(strand, True):
@@ -410,8 +604,9 @@
     return cdf, pre * cdf
 
 
-def gelu_slope(pre):
-    return gelu_pair(pre)[0] + pre * (0.3989422804014327 * jnp.exp(-0.5 * pre * pre))
+def gelu_both(pre):
+    cdf, act = gelu_pair(pre)
+    return act, cdf + pre * (0.3989422804014327 * jnp.exp(-0.5 * pre * pre))
 
 
 def head_masks(rows):
@@ -421,17 +616,17 @@
 
 class Spread:
     def __init__(self, crew, keyvals):
-        self.crew, self.keyvals = crew, keyvals
-        self.row = crew.send(keyvals.at[0], keyvals.at[2], crew.row)
-        self.core = crew.send(keyvals.at[0], keyvals.at[1], crew.core)
-
-    def cross(self):
-        self.row.wait_recv()
-        self.far = self.crew.send(self.keyvals.at[2], self.keyvals.at[3], self.crew.core)
+        self.crew, self.keyvals, self.copies = crew, keyvals, []
+
+    def give(self, slot):
+        copy = self.crew.send(
+            self.keyvals.at[slot], self.keyvals.at[slot + 1], self.crew.core
+        )
+        self.copies.append(copy)
 
     def finish(self):
-        self.core.wait_recv()
-        self.far.wait_recv()
+        for copy in self.copies:
+            copy.wait_recv()
 
 
 class Fold:
@@ -529,21 +724,42 @@
     return crew.send(buffer.at[:, cut], buffer.at[:, cut], crew.grp)
 
 
-def grad_into(job, pipe, x, grad):
-    part = job.part
+def grad_into(crew, whole, pipe, x, grad):
+    part = whole.part
     wide, narrow, rows, cols = part.shape
-    width = 512 if cols % 512 == 0 else 384
+    width = width_of(cols)
     turned = x[...].T
     for first in range(0, cols, width):
         cut = pl.ds(first, width)
         term = dot_plain(turned, grad[:, first : first + width])
         part[:, :, :, cut] = term.astype(part.dtype).reshape(wide, narrow, rows, width)
-    pipe.begin(job)
-
-
-def begin_part(cam, mod, small, enc_qkv, dec_qkv):
-    width = mod.shape[1]
-    depth = mod.shape[0]
+        scatter(crew, whole, pipe, cut)
+
+
+def scatter(crew, whole, pipe, cut):
+    pipe.add(whole.kind(crew, whole, cut, crew.given))
+    crew.given += 1
+
+
+def laid(rows, count, first):
+    span, cols = rows.shape[1], 16 * count
+
+    def place_of(shape):
+        col = lax.broadcasted_iota(jnp.int32, shape, 1)
+        owner = jnp.floor((col.astype(F32) + 0.5) * (1.0 / count)).astype(jnp.int32)
+        return owner, col - owner * count
+
+    lane = lax.broadcasted_iota(jnp.int32, (span, cols), 0)
+    pick = jnp.where(lane == place_of((span, cols))[1] + first, 1.0, 0.0)
+    out = dot_plain(to_bf16(rows), to_bf16(pick))
+    block = lax.broadcasted_iota(jnp.int32, (16, cols), 0)
+    kept = jnp.where(block == place_of((16, cols))[0], out, 0.0)
+    return jnp.sum(kept, 0, keepdims=True)
+
+
+def begin_part(cam, mod, small, enc_width, dec_width, enc_inner, dec_inner):
+    depth, width = mod.shape
+    half = enc_width // 2
 
     def body(r, crew, pipe):
         cams = r.cams
@@ -552,6 +768,7 @@
             for place, target in zip(crew.places, crew.line)
         ]
         cams[crew.wide] = r.cam[crew.wide * 4 + crew.narrow]
+        yield
         for copy in copies:
             copy.wait_recv()
         rows = cams[...].reshape(4, cams.shape[2])[:, :depth]
@@ -565,52 +782,86 @@
             crew.send(r.terms.at[place], r.landed.at[i], target)
             for i, (place, target) in enumerate(zip(crew.places, crew.line))
         ]
+        r.small.need()
+        rows = r.small.buf[...].astype(F32).reshape(16, 16, 128)
+        for i, name in enumerate(
+            (r.gain_one, r.shift_one, r.bias_proj, r.gain_two, r.shift_two, r.bias_fc2)
+        ):
+            name[...] = laid(rows[:, i], enc_width // 16, 0)
+        r.bias_qv[...] = laid(rows[:, 6], enc_width // 8, 0)
+        for i in range(2):
+            source = pl.ds(pl.multiple_of(i * enc_width + crew.group * half, half), half)
+            r.bias_qkv[:, pl.ds(2 * i * half, half)] = r.bias_qv[:, source]
+        r.bias_qkv[:, pl.ds(half, half)] = jnp.zeros((1, half), F32)
         for copy in copies:
             copy.wait_recv()
         r.held[0] = r.terms[crew.wide] + (r.landed[0] + r.landed[1] + r.landed[2])
-        crew.send(r.held.at[0], r.held.at[1], crew.core).wait_recv()
+        copy = crew.send(r.held.at[0], r.held.at[1], crew.core)
+        two = jnp.concatenate([rows[:, 7], rows[:, 8]], 1)
+        r.bias_fc1[...] = laid(two, enc_inner, crew.group * enc_inner)
+        copy.wait_recv()
         r.held[2] = r.held[0] + r.held[1]
-        crew.send(r.held.at[2], r.held.at[3], crew.row).wait_recv()
-        r.modulation[...] = r.held[2] + r.held[3]
-        yield
-
+        copy = crew.send(r.held.at[2], r.held.at[3], crew.row)
+        two = jnp.concatenate([rows[:, 9], rows[:, 10]], 1)
+        r.bias_dfc1[...] = laid(two, dec_inner, crew.group * dec_inner)
+        r.bias_dfc2[...] = laid(rows[:, 11], dec_width // 16, 0)
+        copy.wait_recv()
+        for i in range(6):
+            cut = pl.ds(i * dec_width, dec_width)
+            r.modulation[pl.ds(i, 1), :] = r.held[2, :, cut] + r.held[3, :, cut]
+
+    vector = shape_of((1, enc_width), F32)
     return Part(
         body,
         ins=dict(cam=cam, mod=mod),
-        moved=dict(
-            small=(0, small, [slice(None)], False),
-            enc_qkv=(1, enc_qkv, [slice(None)], False),
-            dec_qkv=(2, dec_qkv, [pl.ds(i * 512, 512) for i in range(3)], False),
-        ),
+        moved=dict(small=(Gather, 0, small, [slice(None)], True)),
         outs=dict(
-            modulation=shape_of((1, width), F32),
+            modulation=shape_of((6, dec_width), F32),
             cams=shape_of((4, 1, 128), F32),
+            gain_one=vector,
+            gain_two=vector,
         ),
         scratch=dict(
             terms=pltpu.VMEM((4, 1, width), F32),
             landed=pltpu.VMEM((3, 1, width), F32),
             held=pltpu.VMEM((4, 1, width), F32),
+            shift_one=pltpu.VMEM((1, enc_width), F32),
+            shift_two=pltpu.VMEM((1, enc_width), F32),
+            bias_proj=pltpu.VMEM((1, enc_width), F32),
+            bias_fc2=pltpu.VMEM((1, enc_width), F32),
+            bias_qv=pltpu.VMEM((1, 2 * enc_width), F32),
+            bias_qkv=pltpu.VMEM((1, 3 * half), F32),
+            bias_fc1=pltpu.VMEM((1, 16 * enc_inner), F32),
+            bias_dfc1=pltpu.VMEM((1, 16 * dec_inner), F32),
+            bias_dfc2=pltpu.VMEM((1, dec_width), F32),
         ),
     )
 
 
-def encoder_part(x, params, given, moved, cross_half):
+def encoder_part(x, params, links, given, moved, late, inner, cross_half):
     rows, width = x.shape
     half = width // 2
-    inner = params["bias_fc1"].shape[1]
     pairs = half // (2 * HEAD)
 
     def body(r, crew, pipe):
+        copy = crew.send(r.x, r.x_row, crew.row)
+        yield
         x_now = r.x[...].astype(F32)
-        normed = normalise(x_now)[0] * r.gain_one[...] + r.shift_one[...]
-        r.normed_one[...] = to_bf16(normed)
+        normed = to_bf16(normalise(x_now)[0] * r.gain_one[...] + r.shift_one[...])
+        r.normed_one[...] = normed
+        copy.wait_recv()
+        x_now = r.x_row[...].astype(F32)
+        other = to_bf16(normalise(x_now)[0] * r.gain_one[...] + r.shift_one[...])
         r.qkv.need()
-        out = dot_plain(r.normed_one[...], r.qkv.all()) + r.bias_qkv[...]
+        weight = r.qkv.all()
+        bias = r.bias_qkv[...]
+        out = dot_plain(normed, weight) + bias
         r.queries[...] = to_bf16(out[:, :half])
         r.keyvals[0] = to_bf16(out[:, half:])
         spread = Spread(crew, r.keyvals)
-        yield
-        spread.cross()
+        spread.give(0)
+        r.keyvals[2] = to_bf16(dot_plain(other, weight[:, half:]) + bias[:, half:])
+        spread.give(2)
         pipe.pump()
         yield
         spread.finish()
@@ -625,15 +876,15 @@
         r.hidden[...] = hidden
         normed = normalise(hidden)[0] * r.gain_two[...] + r.shift_two[...]
         r.normed_two[...] = to_bf16(normed)
-        r.fc1.need()
         step = inner // 4
         total = 0.0
         for i in range(4):
+            if i == 0:
+                r.fc1.need()
             cut = pl.ds(i * step, step)
             pre = dot_plain(r.normed_two[...], r.fc1.cols(cut)) + r.bias_fc1[:, cut]
             r.pre[:, cut] = pre
             act = to_bf16(gelu_pair(pre)[1])
-            r.act[:, cut] = act
             if i == 0:
                 r.fc2.need()
             total = total + dot_plain(act, r.fc2.rows(i))
@@ -644,11 +895,15 @@
         copy.wait_recv()
         both = r.term[...].astype(F32) + r.landed[...].astype(F32)
         r.image[...] = to_bf16(r.hidden[...] + both + r.bias_fc2[...])
+        copy = crew.send(r.image, r.x_row, crew.row)
         r.cross_kv.need()
+        spread = Spread(crew, r.cross_keyvals)
         r.cross_keyvals[0] = to_bf16(dot_plain(r.image[...], r.cross_kv.all()))
-        spread = Spread(crew, r.cross_keyvals)
-        yield
-        spread.cross()
+        spread.give(0)
+        yield
+        copy.wait_recv()
+        r.cross_keyvals[2] = to_bf16(dot_plain(r.x_row[...], r.cross_kv.all()))
+        spread.give(2)
         yield
         spread.finish()
 
@@ -657,8 +912,10 @@
     return Part(
         body,
         ins=ins,
+        links=links,
         given=given,
         moved=moved,
+        late=late,
         outs=dict(
             normed_one=shape_of((rows, width), BF16),
             queries=shape_of((rows, half), BF16),
@@ -668,33 +925,45 @@
             hidden=shape_of((rows, width), F32),
             normed_two=shape_of((rows, width), BF16),
             pre=shape_of((rows, inner), F32),
-            act=shape_of((rows, inner), BF16),
             image=shape_of((rows, width), BF16),
             cross_keyvals=shape_of((4, rows, 2 * cross_half), BF16),
         ),
-        scratch=dict(term=pltpu.VMEM((rows, width), BF16), landed=pltpu.VMEM((rows, width), BF16)),
-    )
-
-
-def self_part(x, modulation, given, moved):
+        scratch=dict(
+            x_row=pltpu.VMEM((rows, width), BF16),
+            term=pltpu.VMEM((rows, width), BF16),
+            landed=pltpu.VMEM((rows, width), BF16),
+        ),
+    )
+
+
+def self_part(x, params, links, given, moved, late, scratch):
     rows, width = x.shape
     half = width // 2
     pairs = half // (2 * HEAD)
 
     def body(r, crew, pipe):
-        normed = normalise(r.x[...].astype(F32))[0]
-        r.normed_one[...] = to_bf16(normed * (1.0 + r.modulation[0:1]) + r.modulation[1:2])
-        r.qkv.need()
-        for i in range(3):
+        copy = crew.send(r.x, r.x_row, crew.row)
+        yield
+        gain, shift = 1.0 + r.modulation[0:1], r.modulation[1:2]
+        r.normed_one[...] = to_bf16(normalise(r.x[...].astype(F32))[0] * gain + shift)
+        copy.wait_recv()
+        r.x_row[...] = to_bf16(normalise(r.x_row[...].astype(F32))[0] * gain + shift)
+        spread = Spread(crew, r.keyvals)
+        for i in (1, 2, 0):
             cut = pl.ds(i * half, half)
-            out = to_bf16(dot_plain(r.normed_one[...], r.qkv.cols(cut)))
+            r.qkv.need(i)
             if i == 0:
-                r.queries[...] = out
+                r.queries[...] = to_bf16(dot_plain(r.normed_one[...], r.qkv.cols(cut)))
             else:
-                r.keyvals[0, :, pl.ds((i - 1) * half, half)] = out
-        spread = Spread(crew, r.keyvals)
-        yield
-        spread.cross()
+                place = pl.ds((i - 1) * half, half)
+                r.keyvals[0, :, place] = to_bf16(
+                    dot_plain(r.normed_one[...], r.qkv.cols(cut))
+                )
+                r.keyvals[2, :, place] = to_bf16(dot_plain(r.x_row[...], r.qkv.cols(cut)))
+            if i == 2:
+                spread.give(0)
+                spread.give(2)
+        pipe.pump()
         yield
         spread.finish()
         first = crew.group * half
@@ -712,12 +981,19 @@
         r.normed_two[...] = to_bf16(normed)
         r.cross_q.need()
         r.cross_queries[...] = to_bf16(dot_plain(r.normed_two[...], r.cross_q.all()))
-
+        pipe.pump()
+
+    ins = dict(x=x)
+    ins.update(params)
+    scratch = dict(scratch)
+    scratch.update(x_row=pltpu.VMEM((rows, width), BF16))
     return Part(
         body,
-        ins=dict(x=x, modulation=modulation),
+        ins=ins,
+        links=links,
         given=given,
         moved=moved,
+        late=late,
         outs=dict(
             normed_one=shape_of((rows, width), BF16),
             queries=shape_of((rows, half), BF16),
@@ -728,14 +1004,13 @@
             normed_two=shape_of((rows, width), BF16),
             cross_queries=shape_of((rows, half), BF16),
         ),
-    )
-
-
-def cross_part(queries, keyvals, after_self, modulation, bias_fc1, bias_fc2, given, moved):
-    rows, width = after_self.shape
+        scratch=scratch,
+    )
+
+
+def cross_part(rows, width, inner, ins, links, given, moved, late):
     half = width // 2
     pairs = half // (2 * HEAD)
-    inner = bias_fc1.shape[1]
 
     def body(r, crew, pipe):
         first = crew.group * half
@@ -752,8 +1027,7 @@
         r.normed_three[...] = to_bf16(normed)
         step = inner // 4
         for i in range(4):
-            if i % 2 == 0:
-                r.fc1.need(i // 2)
+            r.fc1.need(i)
             cut = pl.ds(i * step, step)
             pre = dot_plain(r.normed_three[...], r.fc1.cols(cut)) + r.bias_fc1[:, cut]
             r.pre[:, cut] = pre
@@ -773,26 +1047,24 @@
 
     return Part(
         body,
-        ins=dict(
-            queries=queries,
-            keyvals=keyvals,
-            after_self=after_self,
-            modulation=modulation,
-            bias_fc1=bias_fc1,
-            bias_fc2=bias_fc2,
-        ),
+        ins=ins,
+        links=links,
         given=given,
         moved=moved,
+        late=late,
         outs=dict(
             attended=shape_of((rows, width), BF16),
             sums=shape_of((pairs, 2, rows), F32),
             after_cross=shape_of((rows, width), F32),
             normed_three=shape_of((rows, width), BF16),
             pre=shape_of((rows, inner), F32),
-            act=shape_of((rows, inner), BF16),
             final=shape_of((rows, width), F32),
         ),
-        scratch=dict(term=pltpu.VMEM((rows, width), BF16), landed=pltpu.VMEM((rows, width), BF16)),
+        scratch=dict(
+            act=pltpu.VMEM((rows, inner), BF16),
+            term=pltpu.VMEM((rows, width), BF16),
+            landed=pltpu.VMEM((rows, width), BF16),
+        ),
     )
 
 
@@ -804,7 +1076,9 @@
     for i in range(4):
         cut = pl.ds(i * step, step)
         dact = dot_right(grad, r.fc2.rows(i))
-        dpre = to_bf16(gelu_slope(r.pre[:, cut]) * dact)
+        act, slope = gelu_both(r.pre[:, cut])
+        r.act[:, cut] = to_bf16(act)
+        dpre = to_bf16(slope * dact)
         r.dpre[:, cut] = dpre
         r.pre_sums[:, cut] = column_sums(dpre)
         if i == 0:
@@ -817,7 +1091,7 @@
     return r.term[...].astype(F32) + r.landed[...].astype(F32)
 
 
-def cross_back_part(ins, given, sums):
+def cross_back_part(ins, given, halves, sums):
     rows, width = ins["after_cross"].shape
     inner = ins["pre"].shape[1]
     held, image_width = ins["image"].shape
@@ -830,8 +1104,8 @@
         r.term[...] = feed_back(r, r.branch[...])
         copy = crew.send(r.term, r.landed, crew.grp)
         if moving:
-            grad_into(r.d_fc2, pipe, r.act, r.branch)
-            grad_into(r.d_fc1, pipe, r.normed_three, r.dpre)
+            grad_into(crew, r.d_fc2, pipe, r.act, r.branch)
+            grad_into(crew, r.d_fc1, pipe, r.normed_three, r.dpre)
         copy.wait_recv()
         gain = 1.0 + r.modulation[4:5]
         grad_in, r.gamma_three[...], r.beta_three[...] = norm_back(
@@ -841,7 +1115,10 @@
         r.grad_after[...] = after
         r.cross_branch[...] = to_bf16(after)
         r.proj.need()
-        r.dattended[...] = to_bf16(dot_right(r.cross_branch[...], r.proj.half(crew.group)))
+        r.dattended[...] = to_bf16(dot_right(r.cross_branch[...], r.proj.all()))
+        if moving:
+            branch = r.cross_branch[:, own_cut(crew, half)]
+            grad_into(crew, r.d_proj, pipe, r.attended, branch)
         pipe.pump()
         args = (r.queries, r.keyvals, r.sums, r.dattended, r.cross_dq, r.dkeyvals, half)
         attend_back(*args, 0, pairs // 2)
@@ -852,6 +1129,8 @@
         r.term_two[...] = to_bf16(dot_right(r.cross_dq[...], r.cross_q.all()))
         copy = crew.send(r.term_two, r.landed_two, crew.grp)
         fold.turn()
+        if moving:
+            grad_into(crew, r.d_cross_q, pipe, r.normed_two, r.cross_dq)
         pipe.pump()
         copy.wait_recv()
         gain = 1.0 + r.modulation[2:3]
@@ -895,42 +1174,41 @@
         landed_image=pltpu.VMEM((held, image_width), BF16),
     )
     if moving:
-        scratch.update(dpre=pltpu.VMEM((rows, inner), BF16))
+        scratch.update(
+            act=pltpu.VMEM((rows, inner), BF16), dpre=pltpu.VMEM((rows, inner), BF16)
+        )
     else:
-        outs.update(dpre=shape_of((rows, inner), BF16))
-    return Part(body, ins=ins, given=given, sums=sums, outs=outs, scratch=scratch)
-
-
-def self_back_part(ins, given, sums):
-    rows, width = ins["x"].shape
+        outs.update(act=shape_of((rows, inner), BF16), dpre=shape_of((rows, inner), BF16))
+    return Part(
+        body, ins=ins, given=given, halves=halves, sums=sums, outs=outs, scratch=scratch
+    )
+
+
+def self_back_part(ins, far, given, halves, sums):
+    rows, width = far["x"].shape
     half = width // 2
     pairs = half // (2 * HEAD)
     moving = bool(sums)
 
     def body(r, crew, pipe):
-        r.branch[...] = to_bf16(r.grad_self[...])
+        crew.keep(r.grad_self, r.x_grad).wait()
+        branch = r.drows if moving else r.branch
+        whole = pl.ds(0, width)
+        branch[:, whole] = to_bf16(r.x_grad[...])
         r.proj.need()
-        r.dattended[...] = to_bf16(dot_right(r.branch[...], r.proj.half(crew.group)))
+        r.term[:, pl.ds(0, half)] = to_bf16(dot_right(branch[:, whole], r.proj.all()))
         if moving:
-            grad_into(
-                r.d_cross_proj,
-                pipe,
-                r.cross_attended,
-                r.cross_branch[:, own_cut(crew, half)],
-            )
-            grad_into(r.d_cross_q, pipe, r.normed_two, r.cross_dq)
-            grad_into(r.d_cross_kv, pipe, r.image, r.cross_dkv)
-        yield
-        args = (r.queries, r.keyvals, r.sums, r.dattended, r.dq, r.dkeyvals, half)
+            grad_into(crew, r.d_proj, pipe, r.attended, branch[:, own_cut(crew, half)])
+        if moving:
+            grad_into(crew, r.d_cross_kv, pipe, r.image, r.cross_dkv)
+        yield
+        args = (r.queries, r.keyvals, r.sums, r.term, r.drows, r.dkeyvals, half)
         attend_back(*args, 0, pairs // 2)
         pipe.pump()
         attend_back(*args, pairs // 2, pairs)
         fold = Fold(crew, r.dkeyvals, r.landing)
-        if moving:
-            grad_into(r.d_proj, pipe, r.attended, r.branch[:, own_cut(crew, half)])
         yield
         fold.turn()
-        r.drows[:, pl.ds(0, half)] = r.dq[...]
         pipe.pump()
         yield
         r.drows[:, pl.ds(half, 2 * half)] = fold.finish()
@@ -938,14 +1216,17 @@
         r.term[...] = to_bf16(dot_right(r.drows[...], r.qkv.all()))
         copy = crew.send(r.term, r.landed, crew.grp)
         if moving:
-            grad_into(r.d_qkv, pipe, r.normed_one, r.drows)
-        yield
+            grad_into(crew, r.d_qkv, pipe, r.normed_one, r.drows)
+        held = (r.drows if moving else r.held).at[:, pl.ds(0, width)]
+        fetch = crew.keep(r.x, held)
+        yield
+        fetch.wait()
         copy.wait_recv()
         gain = 1.0 + r.modulation[0:1]
         grad_in, r.gamma_one[...], r.beta_one[...] = norm_back(
-            r.x[...].astype(F32), gain, both_of(r)
+            held[...].astype(F32), gain, both_of(r)
         )
-        r.x_grad[...] = r.grad_self[...] + grad_in
+        r.x_grad[...] += grad_in
 
     outs = dict(
         gamma_one=shape_of((1, width), F32),
@@ -956,22 +1237,23 @@
     scratch = dict(
         term=wide_row,
         landed=wide_row,
-        dattended=pltpu.VMEM((rows, half), BF16),
-        dq=pltpu.VMEM((rows, half), BF16),
         dkeyvals=pltpu.VMEM((4, rows, width), BF16),
         landing=pltpu.VMEM((3, rows, width), BF16),
     )
     if moving:
-        scratch.update(branch=wide_row, drows=pltpu.VMEM((rows, 3 * half), BF16))
+        scratch.update(drows=pltpu.VMEM((rows, 3 * half), BF16))
     else:
+        scratch.update(held=wide_row)
         outs.update(
             branch=shape_of((rows, width), BF16), drows=shape_of((rows, 3 * half), BF16)
         )
-    return Part(body, ins=ins, given=given, sums=sums, outs=outs, scratch=scratch)
-
-
-def encoder_back_part(ins, given, sums):
-    rows, width = ins["x"].shape
+    return Part(
+        body, ins=ins, far=far, given=given, halves=halves, sums=sums, outs=outs, scratch=scratch
+    )
+
+
+def encoder_back_part(ins, far, given, halves, sums):
+    rows, width = far["x"].shape
     half = width // 2
     pairs = half // (2 * HEAD)
     inner = ins["pre"].shape[1]
@@ -981,29 +1263,30 @@
         r.term[...] = feed_back(r, r.image_grad[...])
         copy = crew.send(r.term, r.landed, crew.grp)
         if moving:
-            grad_into(r.d_fc2, pipe, r.act, r.image_grad)
-            grad_into(r.d_fc1, pipe, r.normed_two, r.dpre)
+            grad_into(crew, r.d_fc2, pipe, r.act, r.image_grad)
+            grad_into(crew, r.d_fc1, pipe, r.normed_two, r.dpre)
         yield
         copy.wait_recv()
         grad_in, r.gain_two_grad[...], r.shift_two_grad[...] = norm_back(
             r.hidden[...], r.gain_two[...], both_of(r)
         )
         grad_hidden = r.image_grad[...].astype(F32) + grad_in
-        r.grad_hidden[...] = grad_hidden
-        r.branch[...] = to_bf16(grad_hidden)
-        r.branch_sums[...] = column_sums(r.branch[...])
+        r.x_grad[...] = grad_hidden
+        branch = r.drows if moving else r.branch
+        whole = pl.ds(0, width)
+        branch[:, whole] = to_bf16(grad_hidden)
+        r.branch_sums[...] = column_sums(branch[:, whole])
         r.proj.need()
-        r.dattended[...] = to_bf16(dot_right(r.branch[...], r.proj.half(crew.group)))
+        r.term_two[:, pl.ds(0, half)] = to_bf16(dot_right(branch[:, whole], r.proj.all()))
+        if moving:
+            grad_into(crew, r.d_proj, pipe, r.attended, branch[:, own_cut(crew, half)])
         pipe.pump()
         attend_back(
-            r.queries, r.keyvals, r.sums, r.dattended, r.dq, r.dkeyvals, half, 0, pairs
+            r.queries, r.keyvals, r.sums, r.term_two, r.drows, r.dkeyvals, half, 0, pairs
         )
         fold = Fold(crew, r.dkeyvals, r.landing)
-        if moving:
-            grad_into(r.d_proj, pipe, r.attended, r.branch[:, own_cut(crew, half)])
         yield
         fold.turn()
-        r.drows[:, pl.ds(0, half)] = r.dq[...]
         pipe.pump()
         yield
         r.drows[:, pl.ds(half, 2 * half)] = fold.finish()
@@ -1012,14 +1295,17 @@
         r.term_two[...] = to_bf16(dot_right(r.drows[...], r.qkv.all()))
         copy = crew.send(r.term_two, r.landed_two, crew.grp)
         if moving:
-            grad_into(r.d_qkv, pipe, r.normed_one, r.drows)
-        yield
+            grad_into(crew, r.d_qkv, pipe, r.normed_one, r.drows)
+        held = (r.drows if moving else r.held).at[:, pl.ds(0, width)]
+        fetch = crew.keep(r.x, held)
+        yield
+        fetch.wait()
         copy.wait_recv()
         both = r.term_two[...].astype(F32) + r.landed_two[...].astype(F32)
         grad_in, r.gain_one_grad[...], r.shift_one_grad[...] = norm_back(
-            r.x[...].astype(F32), r.gain_one[...], both
+            held[...].astype(F32), r.gain_one[...], both
         )
-        r.x_grad[...] = r.grad_hidden[...] + grad_in
+        r.x_grad[...] += grad_in
 
     vector = shape_of((1, width), F32)
     outs = dict(
@@ -1038,25 +1324,26 @@
         landed=wide_row,
         term_two=wide_row,
         landed_two=wide_row,
-        grad_hidden=pltpu.VMEM((rows, width), F32),
-        dattended=pltpu.VMEM((rows, half), BF16),
-        dq=pltpu.VMEM((rows, half), BF16),
         dkeyvals=pltpu.VMEM((4, rows, width), BF16),
         landing=pltpu.VMEM((3, rows, width), BF16),
     )
     if moving:
         scratch.update(
-            branch=wide_row,
+            act=pltpu.VMEM((rows, inner), BF16),
             dpre=pltpu.VMEM((rows, inner), BF16),
             drows=pltpu.VMEM((rows, 3 * half), BF16),
         )
     else:
+        scratch.update(held=wide_row)
         outs.update(
             branch=shape_of((rows, width), BF16),
+            act=shape_of((rows, inner), BF16),
             dpre=shape_of((rows, inner), BF16),
             drows=shape_of((rows, 3 * half), BF16),
         )
-    return Part(body, ins=ins, given=given, sums=sums, outs=outs, scratch=scratch)
+    return Part(
+        body, ins=ins, far=far, given=given, halves=halves, sums=sums, outs=outs, scratch=scratch
+    )
 
 
 def end_part(small, mods):
@@ -1064,7 +1351,7 @@
 
     def body(r, crew, pipe):
         r.d_small.part[...] = r.packed[...]
-        pipe.begin(r.d_small)
+        scatter(crew, r.d_small, pipe, pl.ds(0, 128))
         copy = crew.send(r.mods, r.held.at[0], crew.core)
         copy.wait_recv()
         r.held[1] = r.mods[...] + r.held[0]
@@ -1085,7 +1372,7 @@
         body,
         ins=dict(packed=small, mods=mods),
         outs=dict(everyone=shape_of((4, 1, width), F32)),
-        sums=dict(small=(small.shape[2], small.shape[3], None, F32)),
+        sums=dict(small=(Scatter, small.shape[2], small.shape[3], None, F32)),
         scratch=dict(held=pltpu.VMEM((4, 1, width), F32)),
     )
 
@@ -1163,17 +1450,16 @@
     small_parts = (
         ln1_gain,
         ln1_bias,
-        enc_qv_bias,
         enc_proj_bias,
         ln2_gain,
         ln2_bias,
+        enc_fc2_bias,
+        enc_qv_bias,
         enc_fc1_bias,
-        enc_fc2_bias,
         dec_fc1_bias,
         dec_fc2_bias,
         dec_head.reshape(-1),
     )
-    small = jnp.concatenate(small_parts)
     piece = types.SimpleNamespace(
         enc_qkv=columns(enc_qkv, 3, enc_half),
         dec_qkv=columns(dec_qkv, 3, dec_half),
@@ -1188,22 +1474,139 @@
         dec_fc2=half_rows(dec_fc2),
     )
 
+    ray_slots = plane_rows * lax.axis_size("narrow") // VIEWS
+    row_index = narrow * plane_rows + jnp.arange(plane_rows, dtype=jnp.int32)
+    view_index, slot_index = row_index // ray_slots, row_index % ray_slots
+    view_ids = jnp.arange(VIEWS, dtype=jnp.int32)
+    limits = jnp.sum(jnp.where(view_index[:, None] == view_ids[None, :], counts, 0), -1)
+    valid_rays = (slot_index < limits).astype(F32)
+    foreground = fg_mask[0].astype(F32)
+
     if moving:
-        length = small.shape[0]
-        padded = jnp.pad(small, (0, 16 * 128 - length)).reshape(16, 128)
+        rows_of = []
+        for part in small_parts:
+            short = -part.shape[0] % 128
+            rows_of.append(jnp.pad(part, (0, short)))
+        small = jnp.concatenate(rows_of)
+        small = jnp.pad(small, (0, 16 * 128 - small.shape[0])).reshape(16, 128)
         cam_blocks = jnp.pad(cam.reshape(blocks, 1, mod_rows), ((0, 0), (0, 0), (0, 128 - mod_rows)))
-        (first,) = run(
-            [begin_part(cam_blocks, dec_mod, padded, piece.enc_qkv, piece.dec_qkv)],
-            1,
+        begin = begin_part(cam_blocks, dec_mod, small, enc_width, dec_width, enc_inner, dec_inner)
+        wide_buffer = pltpu.VMEM((4, 4, dec_fc1.shape[0], dec_ff // 2), BF16)
+        tall_buffer = pltpu.VMEM((4, 4, dec_fc2.shape[0] // 2, dec_width), BF16)
+        square_buffer = pltpu.VMEM((4, 4, dec_proj.shape[0], dec_width), BF16)
+        own_part = self_part(
+            tri_in[0],
+            dict(),
+            dict(modulation=(begin, "modulation")),
+            dict(),
+            dict(
+                qkv=(GatherRow, 2, piece.dec_qkv, cuts_of(piece.dec_qkv), True),
+                proj=(GatherShared, 6, piece.dec_proj, [None], True),
+                cross_q=(Gather, 7, piece.cross_q, cuts_of(piece.cross_q), True),
+            ),
+            dict(qkv=("broad", False), proj=("square", False)),
+            dict(broad=wide_buffer, tall=tall_buffer, square=square_buffer),
+        )
+        enc_part = encoder_part(
+            img_in[0],
+            dict(),
+            dict(
+                gain_one=(begin, "gain_one"),
+                shift_one=(begin, "shift_one"),
+                bias_qkv=(begin, "bias_qkv"),
+                bias_proj=(begin, "bias_proj"),
+                gain_two=(begin, "gain_two"),
+                shift_two=(begin, "shift_two"),
+                bias_fc1=(begin, "bias_fc1"),
+                bias_fc2=(begin, "bias_fc2"),
+                tall=(own_part, "tall"),
+            ),
+            dict(),
+            dict(
+                qkv=(Gather, 1, piece.enc_qkv, cuts_of(piece.enc_qkv), True),
+                proj=(GatherShared, 3, piece.enc_proj, [None], True),
+                fc1=(GatherRow, 4, piece.enc_fc1, cuts_of(piece.enc_fc1), True),
+                fc2=(Gather, 5, piece.enc_fc2, cuts_of(piece.enc_fc2), True),
+                cross_kv=(Gather, 8, piece.cross_kv, cuts_of(piece.cross_kv), True),
+            ),
+            dict(fc2=("tall", False)),
+            enc_ff // 2,
+            dec_half,
+        )
+        last_part = cross_part(
+            plane_rows,
+            dec_width,
+            dec_ff // 2,
+            dict(),
+            dict(
+                queries=(own_part, "cross_queries"),
+                keyvals=(enc_part, "cross_keyvals"),
+                after_self=(own_part, "after_self"),
+                modulation=(begin, "modulation"),
+                bias_fc1=(begin, "bias_dfc1"),
+                bias_fc2=(begin, "bias_dfc2"),
+                broad=(own_part, "broad"),
+                tall=(own_part, "tall"),
+                square=(own_part, "square"),
+            ),
+            dict(),
+            dict(
+                proj=(GatherShared, 9, piece.cross_proj, [None], True),
+                fc1=(Gather, 10, piece.dec_fc1, cuts_of(piece.dec_fc1), True),
+                fc2=(Gather, 11, piece.dec_fc2, cuts_of(piece.dec_fc2), True),
+            ),
+            dict(fc1=("broad", True), fc2=("tall", True), proj=("square", True)),
+        )
+        first, enc, own, cross = run(
+            [begin, enc_part, own_part, last_part],
+            2,
             True,
-            links=64,
+            order=(1, 0, 2, 0, 1, 2, 1, 2, 1, 2, 1, 1, 1),
+            links=320,
         )
-        small_all = first.small.reshape(blocks, 16 * 128)[:, :length]
-        modulation = first.modulation.reshape(6, dec_width)
-        cam_cut = first.cams.reshape(4, 128)[:, :mod_rows]
-        full = types.SimpleNamespace(enc_qkv=first.enc_qkv, dec_qkv=first.dec_qkv)
+        modulation, cam_cut = first.modulation, first.cams.reshape(4, 128)[:, :mod_rows]
+        gain_one, gain_two = first.gain_one, first.gain_two
+        head = first.small.reshape(blocks, 16, 128)[:, 12:14]
+        head = head.reshape(dec_width, 4).astype(F32)
+        full = types.SimpleNamespace(
+            enc_qkv=enc.qkv,
+            enc_proj=enc.proj,
+            enc_fc1=enc.fc1,
+            enc_fc2=enc.fc2,
+            cross_kv=enc.cross_kv,
+            dec_qkv=own.qkv,
+            dec_proj=own.proj,
+            cross_q=own.cross_q,
+            cross_proj=cross.proj,
+            dec_fc1=cross.fc1,
+            dec_fc2=cross.fc2,
+        )
     else:
-        small_all = lax.all_gather(small, BLOCKS, axis=0)
+        small_all = lax.all_gather(jnp.concatenate(small_parts), BLOCKS, axis=0)
+        unpacked, offset = [], 0
+        for part in small_parts:
+            length = part.shape[0]
+            unpacked.append(small_all[:, offset : offset + length].reshape(1, -1).astype(F32))
+            offset += length
+        (
+            gain_one,
+            shift_one,
+            bias_proj,
+            gain_two,
+            shift_two,
+            bias_fc2,
+            bias_qv,
+            bias_fc1,
+            bias_dfc1,
+            bias_dfc2,
+            head_flat,
+        ) = unpacked
+        head = head_flat.reshape(dec_width, 4)
+        qv_half = take(bias_qv.reshape(2, 2, enc_half), group, 1)
+        bias_qkv = jnp.concatenate([qv_half[0], jnp.zeros((enc_half,), F32), qv_half[1]])
+        bias_qkv = bias_qkv.reshape(1, -1)
+        fc1_half = take(bias_fc1.reshape(blocks, 2, enc_inner), group, 1).reshape(1, -1)
+        dfc1_half = take(bias_dfc1.reshape(blocks, 2, dec_inner), group, 1).reshape(1, -1)
         cam_all = lax.all_gather(cam, "wide", axis=0, tiled=True)
         cam_cut = lax.dynamic_slice_in_dim(cam_all, block * mod_rows, mod_rows, 1)
         term = jnp.dot(cam_cut, dec_mod.astype(F32), precision=PRECISE)
@@ -1216,122 +1619,71 @@
                 for name, value in vars(piece).items()
             }
         )
-    unpacked, offset = [], 0
-    for part in small_parts:
-        length = part.shape[0]
-        unpacked.append(small_all[:, offset : offset + length].reshape(1, -1).astype(F32))
-        offset += length
-    (
-        gain_one,
-        shift_one,
-        bias_qv,
-        bias_proj,
-        gain_two,
-        shift_two,
-        bias_fc1,
-        bias_fc2,
-        bias_dfc1,
-        bias_dfc2,
-        head_flat,
-    ) = unpacked
-    head = head_flat.reshape(dec_width, 4)
-    qv_half = take(bias_qv.reshape(2, 2, enc_half), group, 1)
-    bias_qkv = jnp.concatenate([qv_half[0], jnp.zeros((enc_half,), F32), qv_half[1]])
-    bias_qkv = bias_qkv.reshape(1, -1)
-    fc1_half = take(bias_fc1.reshape(blocks, 2, enc_inner), group, 1).reshape(1, -1)
-    dfc1_half = take(bias_dfc1.reshape(blocks, 2, dec_inner), group, 1).reshape(1, -1)
-
-    ray_slots = plane_rows * lax.axis_size("narrow") // VIEWS
-    row_index = narrow * plane_rows + jnp.arange(plane_rows, dtype=jnp.int32)
-    view_index, slot_index = row_index // ray_slots, row_index % ray_slots
-    view_ids = jnp.arange(VIEWS, dtype=jnp.int32)
-    limits = jnp.sum(jnp.where(view_index[:, None] == view_ids[None, :], counts, 0), -1)
-    valid_rays = (slot_index < limits).astype(F32)
-    foreground = fg_mask[0].astype(F32)
-
-    every = [slice(None)]
-
-    def split(given, moved):
-        if moving:
-            return given, moved
-        for name, (_, value, _, _) in moved.items():
-            given[name] = full_of(value)
-        return given, {}
-
-    def full_of(value):
-        for name, known in vars(piece).items():
-            if known is value:
-                return getattr(full, name)
-        raise KeyError
-
-    enc_given, enc_moved = split(
-        dict(qkv=full.enc_qkv),
-        dict(
-            proj=(0, piece.enc_proj, every, True),
-            fc1=(1, piece.enc_fc1, every, True),
-            fc2=(2, piece.enc_fc2, every, True),
-            cross_kv=(5, piece.cross_kv, every, True),
-        ),
-    )
-    self_given, self_moved = split(
-        dict(qkv=full.dec_qkv),
-        dict(proj=(3, piece.dec_proj, every, True), cross_q=(4, piece.cross_q, every, True)),
-    )
-    enc, own = run(
-        [
-            encoder_part(
-                img_in[0],
-                dict(
-                    gain_one=gain_one,
-                    shift_one=shift_one,
-                    bias_qkv=bias_qkv,
-                    bias_proj=bias_proj,
-                    gain_two=gain_two,
-                    shift_two=shift_two,
-                    bias_fc1=fc1_half,
-                    bias_fc2=bias_fc2,
+        enc, own = run(
+            [
+                encoder_part(
+                    img_in[0],
+                    dict(
+                        gain_one=gain_one,
+                        shift_one=shift_one,
+                        bias_qkv=bias_qkv,
+                        bias_proj=bias_proj,
+                        gain_two=gain_two,
+                        shift_two=shift_two,
+                        bias_fc1=fc1_half,
+                        bias_fc2=bias_fc2,
+                    ),
+                    dict(),
+                    dict(
+                        qkv=full.enc_qkv,
+                        proj=full.enc_proj,
+                        fc1=full.enc_fc1,
+                        fc2=full.enc_fc2,
+                        cross_kv=full.cross_kv,
+                    ),
+                    dict(),
+                    dict(),
+                    enc_ff // 2,
+                    dec_half,
                 ),
-                enc_given,
-                enc_moved,
-                dec_half,
-            ),
-            self_part(tri_in[0], modulation, self_given, self_moved),
-        ],
-        2,
-        moving,
-        links=64,
-    )
-    if moving:
-        full.enc_proj, full.enc_fc1, full.enc_fc2 = enc.proj, enc.fc1, enc.fc2
-        full.cross_kv, full.dec_proj, full.cross_q = enc.cross_kv, own.proj, own.cross_q
-    pair_cuts = [pl.ds(0, dec_ff // 4), pl.ds(dec_ff // 4, dec_ff // 4)]
-    cross_given, cross_moved = split(
-        dict(),
-        dict(
-            proj=(0, piece.cross_proj, every, True),
-            fc1=(1, piece.dec_fc1, pair_cuts, True),
-            fc2=(2, piece.dec_fc2, [pl.ds(0, dec_half), pl.ds(dec_half, dec_half)], True),
-        ),
-    )
-    (cross,) = run(
-        [
-            cross_part(
-                own.cross_queries,
-                enc.cross_keyvals,
-                own.after_self,
-                modulation,
-                dfc1_half,
-                bias_dfc2,
-                cross_given,
-                cross_moved,
-            )
-        ],
-        3,
-        moving,
-        links=64,
-    )
-    if moving:
-        full.cross_proj, full.dec_fc1, full.dec_fc2 = cross.proj, cross.fc1, cross.fc2
+                self_part(
+                    tri_in[0],
+                    dict(modulation=modulation),
+                    dict(),
+                    dict(qkv=full.dec_qkv, proj=full.dec_proj, cross_q=full.cross_q),
+                    dict(),
+                    dict(),
+                    dict(),
+                ),
+            ],
+            2,
+            False,
+            links=32,
+        )
+        (cross,) = run(
+            [
+                cross_part(
+                    plane_rows,
+                    dec_width,
+                    dec_ff // 2,
+                    dict(
+                        queries=own.cross_queries,
+                        keyvals=enc.cross_keyvals,
+                        after_self=own.after_self,
+                        modulation=modulation,
+                        bias_fc1=dfc1_half,
+                        bias_fc2=bias_dfc2,
+                    ),
+                    dict(),
+                    dict(proj=full.cross_proj, fc1=full.dec_fc1, fc2=full.dec_fc2),
+                    dict(),
+                    dict(),
+                )
+            ],
+            3,
+            False,
+            links=32,
+        )
 
     def ray_total(rows_in, head_in):
         return ray_loss(rows_in, head_in, targets[0], foreground, valid_rays)
@@ -1348,7 +1700,6 @@
                 dict(
                     grad=grad_final,
                     pre=cross.pre,
-                    act=cross.act,
                     normed_three=cross.normed_three,
                     after_cross=cross.after_cross,
                     modulation=modulation,
@@ -1357,69 +1708,58 @@
                     sums=cross.sums,
                     after_self=own.after_self,
                     image=enc.image,
+                    attended=cross.attended,
+                    normed_two=own.normed_two,
                 ),
                 dict(
                     fc2=full.dec_fc2,
                     fc1=full.dec_fc1,
-                    proj=full.cross_proj,
                     cross_q=full.cross_q,
                     cross_kv=full.cross_kv,
                 ),
+                dict(proj=full.cross_proj),
                 sums_of(
-                    fc2=(piece.dec_fc2.shape[0], dec_width, "fc2", BF16),
-                    fc1=(piece.dec_fc1.shape[0], dec_ff // 2, "fc1", BF16),
+                    fc2=(Scatter, piece.dec_fc2.shape[0], dec_width, "fc2", BF16),
+                    fc1=(Scatter, piece.dec_fc1.shape[0], dec_ff // 2, "fc1", BF16),
+                    proj=(ScatterLine, dec_cross_proj.shape[0], dec_half, None, BF16),
+                    cross_q=(ScatterLine, dec_cross_q.shape[0], dec_half, "cross_q", BF16),
                 ),
             )
         ],
         4,
         moving,
-        links=64,
+        links=128,
     )
     self_rows, enc_rows = dec_qkv.shape[0], enc_qkv.shape[0]
-    (front,) = run(
+    front, back = run(
         [
             self_back_part(
                 dict(
-                    grad_self=late.grad_self,
                     attended=own.attended,
                     queries=own.queries,
                     keyvals=own.keyvals,
                     sums=own.sums,
                     normed_one=own.normed_one,
-                    x=tri_in[0],
                     modulation=modulation,
-                    cross_attended=cross.attended,
-                    cross_branch=late.cross_branch,
-                    normed_two=own.normed_two,
-                    cross_dq=late.cross_dq,
                     image=enc.image,
                     cross_dkv=late.cross_dkv,
                 ),
-                dict(proj=full.dec_proj, qkv=full.dec_qkv),
+                dict(grad_self=late.grad_self, x=tri_in[0]),
+                dict(qkv=full.dec_qkv),
+                dict(proj=full.dec_proj),
                 sums_of(
-                    cross_proj=(self_rows, dec_half, None, BF16),
-                    cross_q=(self_rows, dec_half, None, BF16),
-                    cross_kv=(enc_rows, dec_width, None, BF16),
-                    proj=(self_rows, dec_half, None, BF16),
-                    qkv=(self_rows, 3 * dec_half, "qkv", BF16),
+                    cross_kv=(ScatterLine, enc_rows, dec_width, None, BF16),
+                    proj=(Scatter, self_rows, dec_half, None, BF16),
+                    qkv=(Scatter, self_rows, 3 * dec_half, "qkv", BF16),
                 ),
-            )
-        ],
-        5,
-        moving,
-        links=96,
-    )
-    (back,) = run(
-        [
+            ),
             encoder_back_part(
                 dict(
                     image_grad=late.image_grad,
                     pre=enc.pre,
-                    act=enc.act,
                     hidden=enc.hidden,
                     normed_one=enc.normed_one,
                     normed_two=enc.normed_two,
-                    x=img_in[0],
                     attended=enc.attended,
                     queries=enc.queries,
                     keyvals=enc.keyvals,
@@ -1427,20 +1767,20 @@
                     gain_one=gain_one,
                     gain_two=gain_two,
                 ),
-                dict(
-                    fc2=full.enc_fc2, fc1=full.enc_fc1, proj=full.enc_proj, qkv=full.enc_qkv
-                ),
+                dict(x=img_in[0]),
+                dict(fc2=full.enc_fc2, fc1=full.enc_fc1, qkv=full.enc_qkv),
+                dict(proj=full.enc_proj),
                 sums_of(
-                    fc2=(piece.enc_fc2.shape[0], enc_width, "fc2", BF16),
-                    fc1=(enc_rows, enc_ff // 2, "fc1", BF16),
-                    proj=(enc_rows, enc_half, None, BF16),
-                    qkv=(enc_rows, 3 * enc_half, "qkv", BF16),
+                    fc2=(Scatter, piece.enc_fc2.shape[0], enc_width, "fc2", BF16),
+                    fc1=(ScatterLine, enc_rows, enc_ff // 2, "fc1", BF16),
+                    proj=(Scatter, enc_rows, enc_half, None, BF16),
+                    qkv=(Scatter, enc_rows, 3 * enc_half, "qkv", BF16),
                 ),
             )
         ],
-        6,
+        5,
         moving,
-        links=96,
+        links=200,
     )
 
     def placed(half, count, width):
@@ -1502,8 +1842,10 @@
     def halves_of(reduced, x, grad):
         if not moving:
             half = plain_grad(x, grad)
-            reduced = jnp.stack([half, lax.ppermute(half, "grp", [(0, 1), (1, 0)])])
-        return jnp.where(group == 0, reduced, reduced[::-1]).astype(F32)
+            other = lax.ppermute(half, "grp", [(0, 1), (1, 0)])
+            pair = jnp.stack([half, other])
+            reduced = jnp.where(group == 0, pair, pair[::-1])
+        return reduced.astype(F32)
 
     def full_columns(halves, parts):
         cut = halves.reshape(2, halves.shape[1], parts, -1)
@@ -1517,22 +1859,24 @@
 
     if moving:
         self_branch = enc_branch = enc_dpre = dec_dpre = enc_drows = dec_drows = None
+        enc_act = dec_act = None
     else:
         self_branch, enc_branch = own_half(front.branch), own_half(back.branch)
+        enc_act, dec_act = back.act, late.act
         enc_dpre, dec_dpre, enc_drows, dec_drows = back.dpre, late.dpre, back.drows, front.drows
     cross_branch = own_half(late.cross_branch)
     get = reduced_of
     out_qkv = halves_of(get(back, "d_qkv"), enc.normed_one, enc_drows)
     out_proj = halves_of(get(back, "d_proj"), enc.attended, enc_branch)
     out_fc1 = halves_of(get(back, "d_fc1"), enc.normed_two, enc_dpre)
-    out_fc2 = halves_of(get(back, "d_fc2"), enc.act, late.image_grad)
+    out_fc2 = halves_of(get(back, "d_fc2"), enc_act, late.image_grad)
     out_dqkv = halves_of(get(front, "d_qkv"), own.normed_one, dec_drows)
     out_dproj = halves_of(get(front, "d_proj"), own.attended, self_branch)
-    out_cq = halves_of(get(front, "d_cross_q"), own.normed_two, late.cross_dq)
+    out_cq = halves_of(get(late, "d_cross_q"), own.normed_two, late.cross_dq)
     out_ckv = halves_of(get(front, "d_cross_kv"), enc.image, late.cross_dkv)
-    out_cproj = halves_of(get(front, "d_cross_proj"), cross.attended, cross_branch)
+    out_cproj = halves_of(get(late, "d_proj"), cross.attended, cross_branch)
     out_dfc1 = halves_of(get(late, "d_fc1"), cross.normed_three, dec_dpre)
-    out_dfc2 = halves_of(get(late, "d_fc2"), cross.act, to_bf16(grad_final))
+    out_dfc2 = halves_of(get(late, "d_fc2"), dec_act, to_bf16(grad_final))
 
     return (
         loss,

time: 728 us -> 608 us (0.84)
  Pallas kernels: 635 us -> 525 us
    pallas_call x7 -> x4, Pallas kernels: 635 us -> 525 us  [run(): pl.pallas_call(kernel, out_shape=out_shapes, in_specs=in_specs, out_specs...]
    unnamed x99 -> x94, local copies, waits for them, and re-layouts: 14.7 us -> 16.4 us
where the time goes in v2:
time: 608 us; the launch traced here: 604 us
  Pallas kernels  525 us (86%)
  local copies, waits for them, and re-layouts  55.6 us (9%)
  other arithmetic  11.4 us (2%)
  matrix products  7.72 us (1%)
    pallas_call x4, Pallas kernels, run(): pl.pallas_call(kernel, out_shape=out_shapes, in_specs=in_specs, out_specs...  525 us
    unnamed x94, local copies, waits for them, and re-layouts  16.4 us
    reshape x19, local copies, waits for them, and re-layouts, full_columns(): return jnp.transpose(cut, (1, 2, 0, 3)).reshape(halves.shape[1], -1)  12.4 us

profile of v2, /device:TPU:0, one launch (start us, length us, event | category | flops | bytes accessed | tf_op | source)
XLA Modules:
  0.0 604.2 jit_solution(13597278144193162190)
XLA Ops:
  0.7 1.0 copy-done
  7.7 0.7 convert_reduce_fusion.2
  8.4 0.7 select_reduce_fusion
  9.6 1.3 reduce.31
  13.3 0.8 dynamic-update-slice.14
  14.3 0.8 copy.107
  16.2 1.0 reshape.493
  18.0 1.6 dynamic-slice_bitcast_fusion.1.refs_7_
  19.6 1.1 reshape.489
  22.0 0.7 dynamic-slice_reduce_fusion.3
  23.4 0.7 dynamic-slice_bitcast_fusion.refs_15_
  24.5 1.2 dynamic-slice_reduce_fusion.2
  25.8 0.9 reshape.487.refs_6_
  26.9 1.3 dynamic-slice_reduce_fusion.1
  28.2 0.7 copy.138
  29.3 1.5 dynamic-slice_reduce_fusion
  30.9 0.8 copy.158
  31.6 234.6 %shard_map.476 = (bf16[4,4,16,128]{3,2,1,0:T(8,128)(2,1)}, f32[6,1024]{1,0:T(8,128)}, f32[4,1,128]{2,1,0:T(1,128)}, f32[1,768]{1,0:T(1,128)}, f32[1,768]{1,0:T(1...) custom-call(f32[16,1,128]{2,1,0:T(1,128)} %pad.49.refs_0_, ...), custom_call_target="tpu_custom_call" | custom-call | tf_op jit(solution)/shard_map/pallas_call | solution.py:553
  266.3 0.9 slice.107
  267.8 2.2 fusion.29
  270.8 1.4 maximum_multiply_fusion
  272.2 0.9 convolution_multiply_fusion
  273.6 2.0 convert_reduce_fusion
  275.6 119.9 %shard_map.477 = (f32[1,2048]{1,0:T(1,128)}, f32[1,1024]{1,0:T(1,128)}, f32[1,1024]{1,0:T(1,128)}, f32[1,1024]{1,0:T(1,128)}, f32[1,1024]{1,0:T(1,128)}, /*index...) custom-call(f32[384,1024]{1,0:T(8,128)} %get-tuple-element.296.refs_, ...), custom_call_target="tpu_custom_call" | custom-call | tf_op jit(solution)/shard_map/pallas_call | solution.py:553
  395.6 152.6 %shard_map.478 = (f32[1,1024]{1,0:T(1,128)}, f32[1,1024]{1,0:T(1,128)}, f32[384,1024]{1,0:T(8,128)}, bf16[2,48,1024]{2,1,0:T(8,128)(2,1)}, bf16[2,64,512]{2,1,0:...) custom-call(bf16[384,1024]{1,0:T(8,128)(2,1)} %get-tuple-element.98., ...), custom_call_target="tpu_custom_call" | custom-call | tf_op jit(solution)/shard_map/pallas_call | solution.py:553
  548.3 0.7 multiply_reduce_fusion.5
  550.0 0.7 multiply_reduce_fusion.3
  550.9 0.7 multiply_reduce_fusion.1
  551.7 0.7 fusion.4
  552.9 0.7 constant_dynamic-update-slice_fusion.5
  554.4 0.7 copy.140
  555.0 18.3 %shard_map.479 = (f32[4,1,6144]{2,1,0:T(1,128)}, f32[2,16,128]{2,1,0:T(8,128)}) custom-call(f32[4,4,16,128]{3,2,1,0:T(8,128)} %bitcast.144, f32[1,6144]{1,0:T(1,128)} %copy-done.22), custom_call_target="tpu_custom_call" | custom-call | tf_op jit(solution)/shard_map/pallas_call | solution.py:553
  573.3 0.7 fusion.34
  574.1 0.7 slice_add_fusion
  581.5 0.8 copy.142
  583.0 1.1 reshape.555
  584.4 0.8 copy.144
  585.3 0.8 copy.143
  586.6 1.1 reshape.541
  587.7 0.9 bitcast_convert_fusion.1
  589.5 1.9 reshape.545
  592.7 1.6 reshape.549
  594.5 0.8 copy.125
  595.3 1.8 reshape.559
  597.1 1.1 bitcast_convert_fusion
  598.3 2.6 fusion
  600.9 0.9 copy.178
  601.7 1.1 copy.179
  (160 shorter events, 27.6 us)
Async XLA Ops:
  0.7 1.1 copy-start
  0.7 21.3 %copy-start.14 = (bf16[48,2304]{1,0:T(8,128)(2,1)S(1)}, bf16[48,2304]{1,0:T(8,128)(2,1)}, u32[]{:S(2)}) copy-start(bf16[48,2304]{1,0:T(8,128)(2,1)} %param.37) | copy-start | bytes 663556
  17.2 7.0 %copy-start.12 = (bf16[48,3072]{1,0:T(8,128)(2,1)S(1)}, bf16[48,3072]{1,0:T(8,128)(2,1)}, u32[]{:S(2)}) copy-start(bf16[48,3072]{1,0:T(8,128)(2,1)} %param.43) | copy-start | bytes 884740
  22.0 4.7 copy-start.9
  24.5 4.4 copy-start.8
  266.3 3.7 copy-start.23
  266.3 3.8 copy-start.25
  266.3 5.8 copy-start.2
  395.5 152.7 %copy-start.4 = (bf16[256,768]{1,0:T(8,128)(2,1)S(1)}, bf16[256,768]{1,0:T(8,128)(2,1)}, u32[]{:S(2)}) copy-start(bf16[256,768]{1,0:T(8,128)(2,1)} %get-tuple-element.125.refs_12_) | copy-start | bytes 1179652
  395.5 157.0 %copy-start.24 = (f32[1,2048]{1,0:T(1,128)S(1)}, f32[1,2048]{1,0:T(1,128)}, u32[]{:S(2)}) copy-start(f32[1,2048]{1,0:T(1,128)} %get-tuple-element.147) | copy-start | bytes 24580
  395.5 158.7 %copy-start.29 = (f32[1,1024]{1,0:T(1,128)S(1)}, f32[1,1024]{1,0:T(1,128)}, u32[]{:S(2)}) copy-start(f32[1,1024]{1,0:T(1,128)} %get-tuple-element.150) | copy-start | bytes 12292
  395.5 158.7 %copy-start.28 = (f32[1,1024]{1,0:T(1,128)S(1)}, f32[1,1024]{1,0:T(1,128)}, u32[]{:S(2)}) copy-start(f32[1,1024]{1,0:T(1,128)} %get-tuple-element.151) | copy-start | bytes 12292
  395.6 158.7 %copy-start.27 = (f32[1,1024]{1,0:T(1,128)S(1)}, f32[1,1024]{1,0:T(1,128)}, u32[]{:S(2)}) copy-start(f32[1,1024]{1,0:T(1,128)} %get-tuple-element.152) | copy-start | bytes 12292
  395.6 158.7 %copy-start.26 = (f32[1,1024]{1,0:T(1,128)S(1)}, f32[1,1024]{1,0:T(1,128)}, u32[]{:S(2)}) copy-start(f32[1,1024]{1,0:T(1,128)} %get-tuple-element.153) | copy-start | bytes 12292
  548.2 32.3 %copy-start.21 = (bf16[2,48,384]{2,1,0:T(8,128)(2,1)S(1)}, bf16[2,48,384]{2,1,0:T(8,128)(2,1)}, u32[]{:S(2)}) copy-start(bf16[2,48,384]{2,1,0:T(8,128)(2,1)} %get-tuple-element.158) | copy-start | bytes 221188
  548.2 33.1 %copy-start.17 = (bf16[2,64,512]{2,1,0:T(8,128)(2,1)S(1)}, bf16[2,64,512]{2,1,0:T(8,128)(2,1)}, u32[]{:S(2)}) copy-start(bf16[2,64,512]{2,1,0:T(8,128)(2,1)} %get-tuple-element.164) | copy-start | bytes 393220
  552.9 29.4 %copy-start.16 = (bf16[2,48,1024]{2,1,0:T(8,128)(2,1)S(1)}, bf16[2,48,1024]{2,1,0:T(8,128)(2,1)}, u32[]{:S(2)}) copy-start(bf16[2,48,1024]{2,1,0:T(8,128)(2,1)} %get-tuple-element.166) | copy-start | bytes 589828
  554.3 0.7 copy-start.22
  581.3 2.8 copy-start.18
  581.3 2.8 copy-start.19
  584.1 2.0 copy-start.15
  585.3 2.4 copy-start.11
  586.3 2.4 copy-start.13
  588.9 2.5 copy-start.10
  592.1 2.2 copy-start.7
  595.3 1.8 copy-start.6
  595.3 3.0 copy-start.20
  595.3 2.9 copy-start.30
  597.1 3.7 copy-start.5
  598.3 3.5 copy-start.3
  600.9 2.0 copy-start.1

commit v3 on v2

--- a/solution.py
+++ b/solution.py
@@ -94,12 +94,21 @@
 class Gather:
     def __init__(self, crew, piece, full, cut, buf):
         self.crew, self.piece, self.full, self.cut, self.buf = crew, piece, full, cut, buf
+        rows, cols = full.shape[2:]
+        self.source = piece
+        if piece.shape[0] == 2 * rows:
+            self.source = piece.at[pl.ds(pl.multiple_of(crew.group * rows, rows), rows), cut]
+        elif piece.shape[1] == 2 * cols:
+            first = pl.multiple_of(2 * cut.start + crew.group * cut.size, 128)
+            self.source = piece.at[:, pl.ds(first, cut.size)]
+        else:
+            self.source = piece.at[:, cut]
         self.steps = [self.start, self.turn, self.cross, self.finish]
         self.load, self.late = None, False
 
     def start(self):
         crew = self.crew
-        source = self.piece.at[:, self.cut]
+        source = self.source
         own = self.full.at[crew.wide, crew.narrow, :, self.cut]
         self.own = crew.keep(source, own)
         self.lines = [crew.send(source, own, target) for target in crew.line]
@@ -135,7 +144,7 @@
 class GatherRow(Gather):
     def start(self):
         crew = self.crew
-        source = self.piece.at[:, self.cut]
+        source = self.source
         own = self.full.at[crew.wide, crew.narrow, :, self.cut]
         self.row = crew.send(source, own, crew.row)
         self.own = crew.keep(source, own)
@@ -404,8 +413,10 @@
         self.scratch = named.get("scratch", {})
         self.given = named.get("given", {})
         self.links = named.get("links", {})
+        self.packs = named.get("packs", {})
         self.late = named.get("late", {})
         self.halves = named.get("halves", {})
+        self.shapes = named.get("shapes", {})
         self.moved = named.get("moved", {})
         self.sums = named.get("sums", {})
 
@@ -446,14 +457,19 @@
             arrays.append(value)
             in_specs.append(HBM)
             scratch.append(pltpu.VMEM((value.shape[0] // 2,) + value.shape[1:], BF16))
-        for name, (_, _, piece, _, loaded) in part.moved.items():
+        for name, (_, _, piece, cuts, loaded) in part.moved.items():
             arrays.append(piece)
             in_specs.append(HBM)
-            shape = (4, 4) + piece.shape
+            shape = (4, 4) + part.shapes.get(name, piece.shape)
             out_shapes.append(shape_of(shape, piece.dtype))
             out_specs.append(HBM)
             if loaded and name not in part.late:
                 scratch.append(pltpu.VMEM(shape, piece.dtype))
+        for name, shape in part.packs.items():
+            out_shapes.append(shape_of((4, 4) + shape, F32))
+            out_specs.append(HBM)
+            scratch.append(pltpu.VMEM((4, 4) + shape, F32))
+            scratch.append(pltpu.VMEM(shape, F32))
         for name, value in part.outs.items():
             out_shapes.append(value)
             out_specs.append(VMEM)
@@ -512,6 +528,11 @@
                     job = kind(crew, source, full, cut, buf)
                     matrix.jobs.append(job)
                     planned.append((rank + 0.01 * i, job))
+            for name in part.packs:
+                matrix = Matrix(next(rest), pipe)
+                matrix.piece = next(rest)
+                matrix.jobs.append(Gather(crew, matrix.piece, next(outs), slice(None), matrix.buf))
+                setattr(space, name, matrix)
             for name in part.outs:
                 setattr(space, name, next(outs))
             for name, (kind, rows, cols, weight, dtype) in part.sums.items():
@@ -527,8 +548,7 @@
                 setattr(space, name, getattr(spaces[parts.index(other)], known))
         for part, space in zip(parts, spaces):
             for name, (held, _) in part.late.items():
-                cols = part.moved[name][2].shape[1]
-                rows_in = part.moved[name][2].shape[0]
+                rows_in, cols = part.shapes.get(name, part.moved[name][2].shape)
                 matrix = getattr(space, name)
                 matrix.buf = getattr(space, held).at[:, :, pl.ds(0, rows_in), pl.ds(0, cols)]
                 for job in matrix.jobs:
@@ -568,6 +588,8 @@
     for part in parts:
         space = types.SimpleNamespace()
         for name in part.moved:
+            setattr(space, name, next(results))
+        for name in part.packs:
             setattr(space, name, next(results))
         for name in part.outs:
             setattr(space, name, next(results))
@@ -724,12 +746,12 @@
     return crew.send(buffer.at[:, cut], buffer.at[:, cut], crew.grp)
 
 
-def grad_into(crew, whole, pipe, x, grad):
+def grad_into(crew, whole, pipe, x, grad, begin=0, end=None):
     part = whole.part
     wide, narrow, rows, cols = part.shape
     width = width_of(cols)
     turned = x[...].T
-    for first in range(0, cols, width):
+    for first in range(begin, cols if end is None else end, width):
         cut = pl.ds(first, width)
         term = dot_plain(turned, grad[:, first : first + width])
         part[:, :, :, cut] = term.astype(part.dtype).reshape(wide, narrow, rows, width)
@@ -753,8 +775,14 @@
     pick = jnp.where(lane == place_of((span, cols))[1] + first, 1.0, 0.0)
     out = dot_plain(to_bf16(rows), to_bf16(pick))
     block = lax.broadcasted_iota(jnp.int32, (16, cols), 0)
-    kept = jnp.where(block == place_of((16, cols))[0], out, 0.0)
-    return jnp.sum(kept, 0, keepdims=True)
+    kept = block == place_of((16, cols))[0]
+    return [
+        jnp.sum(jnp.where(kept, out[16 * k : 16 * k + 16], 0.0), 0, keepdims=True)
+        for k in range(rows.shape[0] // 16)
+    ]
+
+
+SMALL = [chr(97 + i) + "_in" for i in range(11)]
 
 
 def begin_part(cam, mod, small, enc_width, dec_width, enc_inner, dec_inner):
@@ -768,6 +796,15 @@
             for place, target in zip(crew.places, crew.line)
         ]
         cams[crew.wide] = r.cam[crew.wide * 4 + crew.narrow]
+        row = 0
+        r.small.piece[...] = jnp.zeros((16, 128), F32)
+        for name in SMALL:
+            value = getattr(r, name)[...].astype(F32)
+            for first in range(0, value.shape[1], 128):
+                cut = value[:, first : first + 128]
+                r.small.piece[row : row + 1, 0 : cut.shape[1]] = cut
+                row += 1
+        pipe.begin(r.small.jobs[0])
         yield
         for copy in copies:
             copy.wait_recv()
@@ -776,19 +813,20 @@
         left = rows - high.astype(F32)
         middle = to_bf16(left)
         low = to_bf16(left - middle.astype(F32))
-        terms = [dot_plain(part, r.mod[...]) for part in (high, middle, low)]
-        r.terms[...] = (terms[0] + (terms[1] + terms[2])).reshape(4, 1, width)
+        rows = jnp.concatenate([high.astype(F32), middle.astype(F32), low.astype(F32)], 0)
+        terms = dot_plain(to_bf16(rows), r.mod[...])
+        r.terms[...] = (terms[0:4] + (terms[4:8] + terms[8:12])).reshape(4, 1, width)
         copies = [
             crew.send(r.terms.at[place], r.landed.at[i], target)
             for i, (place, target) in enumerate(zip(crew.places, crew.line))
         ]
         r.small.need()
-        rows = r.small.buf[...].astype(F32).reshape(16, 16, 128)
-        for i, name in enumerate(
-            (r.gain_one, r.shift_one, r.bias_proj, r.gain_two, r.shift_two, r.bias_fc2)
-        ):
-            name[...] = laid(rows[:, i], enc_width // 16, 0)
-        r.bias_qv[...] = laid(rows[:, 6], enc_width // 8, 0)
+        rows = r.small.buf[...].reshape(16, 16, 128)
+        names = (r.gain_one, r.shift_one, r.bias_proj, r.gain_two, r.shift_two, r.bias_fc2)
+        six = jnp.concatenate([rows[:, i] for i in range(6)], 0)
+        for name, vector in zip(names, laid(six, enc_width // 16, 0)):
+            name[...] = vector
+        (r.bias_qv[...],) = laid(rows[:, 6], enc_width // 8, 0)
         for i in range(2):
             source = pl.ds(pl.multiple_of(i * enc_width + crew.group * half, half), half)
             r.bias_qkv[:, pl.ds(2 * i * half, half)] = r.bias_qv[:, source]
@@ -798,23 +836,27 @@
         r.held[0] = r.terms[crew.wide] + (r.landed[0] + r.landed[1] + r.landed[2])
         copy = crew.send(r.held.at[0], r.held.at[1], crew.core)
         two = jnp.concatenate([rows[:, 7], rows[:, 8]], 1)
-        r.bias_fc1[...] = laid(two, enc_inner, crew.group * enc_inner)
+        (r.bias_fc1[...],) = laid(two, enc_inner, crew.group * enc_inner)
         copy.wait_recv()
         r.held[2] = r.held[0] + r.held[1]
         copy = crew.send(r.held.at[2], r.held.at[3], crew.row)
         two = jnp.concatenate([rows[:, 9], rows[:, 10]], 1)
-        r.bias_dfc1[...] = laid(two, dec_inner, crew.group * dec_inner)
-        r.bias_dfc2[...] = laid(rows[:, 11], dec_width // 16, 0)
+        (r.bias_dfc1[...],) = laid(two, dec_inner, crew.group * dec_inner)
+        (r.bias_dfc2[...],) = laid(rows[:, 11], dec_width // 16, 0)
+        pipe.pump()
         copy.wait_recv()
+        pipe.pump()
         for i in range(6):
             cut = pl.ds(i * dec_width, dec_width)
             r.modulation[pl.ds(i, 1), :] = r.held[2, :, cut] + r.held[3, :, cut]
 
     vector = shape_of((1, enc_width), F32)
+    ins = dict(cam=cam, mod=mod)
+    ins.update({SMALL[i]: value for i, value in enumerate(small)})
     return Part(
         body,
-        ins=dict(cam=cam, mod=mod),
-        moved=dict(small=(Gather, 0, small, [slice(None)], True)),
+        ins=ins,
+        packs=dict(small=(16, 128)),
         outs=dict(
             modulation=shape_of((6, dec_width), F32),
             cams=shape_of((4, 1, 128), F32),
@@ -838,7 +880,7 @@
     )
 
 
-def encoder_part(x, params, links, given, moved, late, inner, cross_half):
+def encoder_part(x, params, links, given, moved, late, shapes, inner, cross_half):
     rows, width = x.shape
     half = width // 2
     pairs = half // (2 * HEAD)
@@ -916,6 +958,7 @@
         given=given,
         moved=moved,
         late=late,
+        shapes=shapes,
         outs=dict(
             normed_one=shape_of((rows, width), BF16),
             queries=shape_of((rows, half), BF16),
@@ -936,7 +979,7 @@
     )
 
 
-def self_part(x, params, links, given, moved, late, scratch):
+def self_part(x, params, links, given, moved, late, shapes, scratch):
     rows, width = x.shape
     half = width // 2
     pairs = half // (2 * HEAD)
@@ -994,6 +1037,7 @@
         given=given,
         moved=moved,
         late=late,
+        shapes=shapes,
         outs=dict(
             normed_one=shape_of((rows, width), BF16),
             queries=shape_of((rows, half), BF16),
@@ -1008,7 +1052,7 @@
     )
 
 
-def cross_part(rows, width, inner, ins, links, given, moved, late):
+def cross_part(rows, width, inner, ins, links, given, moved, late, shapes):
     half = width // 2
     pairs = half // (2 * HEAD)
 
@@ -1052,6 +1096,7 @@
         given=given,
         moved=moved,
         late=late,
+        shapes=shapes,
         outs=dict(
             attended=shape_of((rows, width), BF16),
             sums=shape_of((pairs, 2, rows), F32),
@@ -1199,24 +1244,26 @@
         r.term[:, pl.ds(0, half)] = to_bf16(dot_right(branch[:, whole], r.proj.all()))
         if moving:
             grad_into(crew, r.d_proj, pipe, r.attended, branch[:, own_cut(crew, half)])
-        if moving:
-            grad_into(crew, r.d_cross_kv, pipe, r.image, r.cross_dkv)
-        yield
         args = (r.queries, r.keyvals, r.sums, r.term, r.drows, r.dkeyvals, half)
         attend_back(*args, 0, pairs // 2)
-        pipe.pump()
+        pipe.pump(2)
         attend_back(*args, pairs // 2, pairs)
         fold = Fold(crew, r.dkeyvals, r.landing)
+        first, rest = pl.ds(0, half), pl.ds(half, 2 * half)
+        r.qkv.need()
+        r.term[...] = to_bf16(dot_right(r.drows[:, first], r.qkv.cols(first)))
+        fold.turn()
+        if moving:
+            grad_into(crew, r.d_qkv, pipe, r.normed_one, r.drows, 0, half)
+            grad_into(crew, r.d_cross_kv, pipe, r.image, r.cross_dkv)
+        pipe.pump(2)
         yield
-        fold.turn()
-        pipe.pump()
-        yield
-        r.drows[:, pl.ds(half, 2 * half)] = fold.finish()
-        r.qkv.need()
-        r.term[...] = to_bf16(dot_right(r.drows[...], r.qkv.all()))
+        r.drows[:, rest] = fold.finish()
+        term = r.term[...].astype(F32) + dot_right(r.drows[:, rest], r.qkv.cols(rest))
+        r.term[...] = to_bf16(term)
         copy = crew.send(r.term, r.landed, crew.grp)
         if moving:
-            grad_into(crew, r.d_qkv, pipe, r.normed_one, r.drows)
+            grad_into(crew, r.d_qkv, pipe, r.normed_one, r.drows, half)
         held = (r.drows if moving else r.held).at[:, pl.ds(0, width)]
         fetch = crew.keep(r.x, held)
         yield
@@ -1280,22 +1327,26 @@
         r.term_two[:, pl.ds(0, half)] = to_bf16(dot_right(branch[:, whole], r.proj.all()))
         if moving:
             grad_into(crew, r.d_proj, pipe, r.attended, branch[:, own_cut(crew, half)])
-        pipe.pump()
-        attend_back(
-            r.queries, r.keyvals, r.sums, r.term_two, r.drows, r.dkeyvals, half, 0, pairs
-        )
+        pipe.pump(2)
+        args = (r.queries, r.keyvals, r.sums, r.term_two, r.drows, r.dkeyvals, half)
+        attend_back(*args, 0, pairs)
         fold = Fold(crew, r.dkeyvals, r.landing)
+        first, rest = pl.ds(0, half), pl.ds(half, 2 * half)
+        r.qkv.need()
+        r.term_two[...] = to_bf16(dot_right(r.drows[:, first], r.qkv.cols(first)))
+        fold.turn()
+        r.row_sums[:, first] = column_sums(r.drows[:, first])
+        if moving:
+            grad_into(crew, r.d_qkv, pipe, r.normed_one, r.drows, 0, half)
+        pipe.pump(2)
         yield
-        fold.turn()
-        pipe.pump()
-        yield
-        r.drows[:, pl.ds(half, 2 * half)] = fold.finish()
-        r.row_sums[...] = column_sums(r.drows[...])
-        r.qkv.need()
-        r.term_two[...] = to_bf16(dot_right(r.drows[...], r.qkv.all()))
+        r.drows[:, rest] = fold.finish()
+        r.row_sums[:, rest] = column_sums(r.drows[:, rest])
+        term = r.term_two[...].astype(F32) + dot_right(r.drows[:, rest], r.qkv.cols(rest))
+        r.term_two[...] = to_bf16(term)
         copy = crew.send(r.term_two, r.landed_two, crew.grp)
         if moving:
-            grad_into(crew, r.d_qkv, pipe, r.normed_one, r.drows)
+            grad_into(crew, r.d_qkv, pipe, r.normed_one, r.drows, half)
         held = (r.drows if moving else r.held).at[:, pl.ds(0, width)]
         fetch = crew.keep(r.x, held)
         yield
@@ -1473,6 +1524,15 @@
         dec_fc1=columns(dec_fc1, blocks, dec_inner),
         dec_fc2=half_rows(dec_fc2),
     )
+    shape = types.SimpleNamespace(**{name: value.shape for name, value in vars(piece).items()})
+    raw = types.SimpleNamespace(
+        enc_qkv=enc_qkv,
+        dec_qkv=dec_qkv,
+        enc_fc2=enc_fc2,
+        cross_q=dec_cross_q,
+        cross_kv=dec_cross_kv,
+        dec_fc2=dec_fc2,
+    )
 
     ray_slots = plane_rows * lax.axis_size("narrow") // VIEWS
     row_index = narrow * plane_rows + jnp.arange(plane_rows, dtype=jnp.int32)
@@ -1483,12 +1543,7 @@
     foreground = fg_mask[0].astype(F32)
 
     if moving:
-        rows_of = []
-        for part in small_parts:
-            short = -part.shape[0] % 128
-            rows_of.append(jnp.pad(part, (0, short)))
-        small = jnp.concatenate(rows_of)
-        small = jnp.pad(small, (0, 16 * 128 - small.shape[0])).reshape(16, 128)
+        small = [part.reshape(1, -1) for part in small_parts]
         cam_blocks = jnp.pad(cam.reshape(blocks, 1, mod_rows), ((0, 0), (0, 0), (0, 128 - mod_rows)))
         begin = begin_part(cam_blocks, dec_mod, small, enc_width, dec_width, enc_inner, dec_inner)
         wide_buffer = pltpu.VMEM((4, 4, dec_fc1.shape[0], dec_ff // 2), BF16)
@@ -1500,11 +1555,12 @@
             dict(modulation=(begin, "modulation")),
             dict(),
             dict(
-                qkv=(GatherRow, 2, piece.dec_qkv, cuts_of(piece.dec_qkv), True),
+                qkv=(Gather, 2, raw.dec_qkv, cuts_of(piece.dec_qkv), True),
                 proj=(GatherShared, 6, piece.dec_proj, [None], True),
-                cross_q=(Gather, 7, piece.cross_q, cuts_of(piece.cross_q), True),
+                cross_q=(Gather, 7, raw.cross_q, cuts_of(piece.cross_q), True),
             ),
             dict(qkv=("broad", False), proj=("square", False)),
+            dict(qkv=shape.dec_qkv, cross_q=shape.cross_q),
             dict(broad=wide_buffer, tall=tall_buffer, square=square_buffer),
         )
         enc_part = encoder_part(
@@ -1523,13 +1579,14 @@
             ),
             dict(),
             dict(
-                qkv=(Gather, 1, piece.enc_qkv, cuts_of(piece.enc_qkv), True),
+                qkv=(Gather, 1, raw.enc_qkv, cuts_of(piece.enc_qkv), True),
                 proj=(GatherShared, 3, piece.enc_proj, [None], True),
-                fc1=(GatherRow, 4, piece.enc_fc1, cuts_of(piece.enc_fc1), True),
-                fc2=(Gather, 5, piece.enc_fc2, cuts_of(piece.enc_fc2), True),
-                cross_kv=(Gather, 8, piece.cross_kv, cuts_of(piece.cross_kv), True),
+                fc1=(Gather, 4, piece.enc_fc1, cuts_of(piece.enc_fc1), True),
+                fc2=(Gather, 5, raw.enc_fc2, cuts_of(piece.enc_fc2), True),
+                cross_kv=(Gather, 8, raw.cross_kv, cuts_of(piece.cross_kv), True),
             ),
             dict(fc2=("tall", False)),
+            dict(qkv=shape.enc_qkv, fc2=shape.enc_fc2, cross_kv=shape.cross_kv),
             enc_ff // 2,
             dec_half,
         )
@@ -1553,21 +1610,23 @@
             dict(
                 proj=(GatherShared, 9, piece.cross_proj, [None], True),
                 fc1=(Gather, 10, piece.dec_fc1, cuts_of(piece.dec_fc1), True),
-                fc2=(Gather, 11, piece.dec_fc2, cuts_of(piece.dec_fc2), True),
+                fc2=(Gather, 11, raw.dec_fc2, cuts_of(piece.dec_fc2), True),
             ),
             dict(fc1=("broad", True), fc2=("tall", True), proj=("square", True)),
+            dict(fc2=shape.dec_fc2),
         )
         first, enc, own, cross = run(
             [begin, enc_part, own_part, last_part],
             2,
             True,
-            order=(1, 0, 2, 0, 1, 2, 1, 2, 1, 2, 1, 1, 1),
+            order=(1, 0, 0, 2, 1, 2, 1, 2, 1, 2, 1, 1, 1),
+            ahead=2,
             links=320,
         )
         modulation, cam_cut = first.modulation, first.cams.reshape(4, 128)[:, :mod_rows]
         gain_one, gain_two = first.gain_one, first.gain_two
         head = first.small.reshape(blocks, 16, 128)[:, 12:14]
-        head = head.reshape(dec_width, 4).astype(F32)
+        head = head.reshape(dec_width, 4)
         full = types.SimpleNamespace(
             enc_qkv=enc.qkv,
             enc_proj=enc.proj,
@@ -1643,6 +1702,7 @@
                     ),
                     dict(),
                     dict(),
+                    dict(),
                     enc_ff // 2,
                     dec_half,
                 ),
@@ -1651,6 +1711,7 @@
                     dict(modulation=modulation),
                     dict(),
                     dict(qkv=full.dec_qkv, proj=full.dec_proj, cross_q=full.cross_q),
+                    dict(),
                     dict(),
                     dict(),
                     dict(),
@@ -1676,6 +1737,7 @@
                     ),
                     dict(),
                     dict(proj=full.cross_proj, fc1=full.dec_fc1, fc2=full.dec_fc2),
+                    dict(),
                     dict(),
                     dict(),
                 )
@@ -1780,6 +1842,7 @@
         ],
         5,
         moving,
+        order=(1, 0, 1, 0, 1, 0, 1),
         links=200,
     )
 
@@ -1848,8 +1911,11 @@
         return reduced.astype(F32)
 
     def full_columns(halves, parts):
-        cut = halves.reshape(2, halves.shape[1], parts, -1)
-        return jnp.transpose(cut, (1, 2, 0, 3)).reshape(halves.shape[1], -1)
+        width = halves.shape[2] // parts
+        cut = [
+            halves[g, :, p * width : (p + 1) * width] for p in range(parts) for g in range(2)
+        ]
+        return jnp.concatenate(cut, 1)
 
     def full_rows(halves):
         return halves.reshape(-1, halves.shape[2])

time: 608 us -> 564 us (0.928)
  local copies, waits for them, and re-layouts: 55.6 us -> 26.9 us
  Pallas kernels: 525 us -> 501 us
    pallas_call x4, Pallas kernels: 525 us -> 501 us  [run(): pl.pallas_call(kernel, out_shape=out_shapes, in_specs=in_specs, out_specs...]
    reshape x22 -> x3, local copies, waits for them, and re-layouts: 13.7 us -> 3.02 us  [the longest x2 2.49 us: local(): small = [part.reshape(1, -1) for part in small_parts]]
    unnamed x94 -> x112, local copies, waits for them, and re-layouts: 16.4 us -> 8.87 us
where the time goes in v3:
time: 564 us; the launch traced here: 556 us
  Pallas kernels  501 us (89%)
  local copies, waits for them, and re-layouts  26.9 us (5%)
  other arithmetic  14.6 us (3%)
  matrix products  8.9 us (2%)
    pallas_call x4, Pallas kernels, run(): pl.pallas_call(kernel, out_shape=out_shapes, in_specs=in_specs, out_specs...  501 us

profile of v3, /device:TPU:0, one launch (start us, length us, event | category | flops | bytes accessed | tf_op | source)
XLA Modules:
  0.0 555.9 jit_solution(734312129990754478)
XLA Ops:
  0.7 1.3 reshape.389.refs_9_
  2.0 1.2 reshape.390.refs_10_
  3.2 0.7 convert_reduce_fusion.2
  3.9 0.7 select_reduce_fusion
  5.1 1.3 reduce.25
  6.6 0.6 pad.14.refs_0_
  7.2 0.8 copy.68
  8.0 0.7 reshape_reshape.12.refs_12_
  8.6 1.4 reshape.392
  10.0 1.2 dynamic-slice_reduce_fusion.1
  11.3 0.9 reshape.393.refs_16_
  12.5 1.5 dynamic-slice_reduce_fusion
  14.0 0.8 copy.93
  14.8 212.8 %shard_map.476 = (f32[4,4,16,128]{3,2,1,0:T(8,128)}, f32[6,1024]{1,0:T(8,128)}, f32[4,1,128]{2,1,0:T(1,128)}, f32[1,768]{1,0:T(1,128)}, f32[1,768]{1,0:T(1,128)}...) custom-call(f32[16,1,128]{2,1,0:T(1,128)} %pad.14.refs_0_, ...), custom_call_target="tpu_custom_call" | custom-call | tf_op jit(solution)/shard_map/pallas_call | solution.py:573
  227.7 1.0 slice.459
  229.2 2.8 fusion.35
  232.1 0.6 fusion.20
  232.7 1.4 maximum_multiply_fusion
  234.1 0.9 convolution_multiply_fusion
  235.6 2.6 convert_reduce_fusion
  238.2 120.6 %shard_map.477 = (f32[1,2048]{1,0:T(1,128)}, f32[1,1024]{1,0:T(1,128)}, f32[1,1024]{1,0:T(1,128)}, f32[1,1024]{1,0:T(1,128)}, f32[1,1024]{1,0:T(1,128)}, /*index...) custom-call(f32[384,1024]{1,0:T(8,128)} %get-tuple-element.314.refs_, ...), custom_call_target="tpu_custom_call" | custom-call | tf_op jit(solution)/shard_map/pallas_call | solution.py:573
  358.8 145.4 %shard_map.478 = (f32[1,1024]{1,0:T(1,128)}, f32[1,1024]{1,0:T(1,128)}, f32[384,1024]{1,0:T(8,128)}, bf16[2,48,1024]{2,1,0:T(8,128)(2,1)}, bf16[2,64,512]{2,1,0:...) custom-call(bf16[384,1024]{1,0:T(8,128)(2,1)} %get-tuple-element.98., ...), custom_call_target="tpu_custom_call" | custom-call | tf_op jit(solution)/shard_map/pallas_call | solution.py:573
  504.4 0.7 multiply_reduce_fusion.5
  505.1 0.7 slice_bitcast_fusion.89
  506.1 0.7 multiply_reduce_fusion.3
  506.9 0.7 multiply_reduce_fusion.1
  507.8 0.7 fusion.10
  508.9 0.7 constant_dynamic-update-slice_fusion.5
  509.6 0.7 constant_dynamic-update-slice_fusion.4
  510.4 0.7 copy.81
  511.1 22.1 %shard_map.479 = (f32[4,1,6144]{2,1,0:T(1,128)}, f32[2,16,128]{2,1,0:T(8,128)}) custom-call(f32[4,4,16,128]{3,2,1,0:T(8,128)} %bitcast.336, f32[1,6144]{1,0:T(1,128)} %copy-done.17), custom_call_target="tpu_custom_call" | custom-call | tf_op jit(solution)/shard_map/pallas_call | solution.py:573
  533.2 0.7 fusion.40
  533.9 0.7 slice_add_fusion
  535.8 0.6 slice.510
  536.4 0.6 slice.560
  539.0 0.6 fusion.33
  539.7 0.7 copy.74
  540.4 0.7 pad_maximum_fusion.4
  541.2 0.8 pad_maximum_fusion.1
  542.1 0.7 pad_maximum_fusion.3
  542.9 0.8 pad_maximum_fusion
  544.2 1.0 concatenate.77
  545.2 0.9 bitcast_convert_fusion.1
  546.3 0.8 copy-done.5
  548.5 1.1 bitcast_convert_fusion
  549.6 2.6 fusion.6
  552.2 0.9 copy.142
  553.1 1.1 copy.143
  (160 shorter events, 7.0 us)
Async XLA Ops:
  0.7 11.5 %copy-start.6 = (bf16[64,4096]{1,0:T(8,128)(2,1)S(1)}, bf16[64,4096]{1,0:T(8,128)(2,1)}, u32[]{:S(2)}) copy-start(bf16[64,4096]{1,0:T(8,128)(2,1)} %param.53) | copy-start | bytes 1572868
  227.6 4.3 copy-start.19
  227.7 4.4 copy-start.22
  227.7 6.4 %copy-start = (f32[384,1024]{1,0:T(8,128)S(1)}, f32[384,1024]{1,0:T(8,128)}, u32[]{:S(2)}) copy-start(f32[384,1024]{1,0:T(8,128)} %get-tuple-element.105) | copy-start | bytes 4718596
  358.8 145.5 %copy-start.2 = (bf16[256,768]{1,0:T(8,128)(2,1)S(1)}, bf16[256,768]{1,0:T(8,128)(2,1)}, u32[]{:S(2)}) copy-start(bf16[256,768]{1,0:T(8,128)(2,1)} %get-tuple-element.125.refs_12_) | copy-start | bytes 1179652
  358.8 149.8 %copy-start.21 = (f32[1,2048]{1,0:T(1,128)S(1)}, f32[1,2048]{1,0:T(1,128)}, u32[]{:S(2)}) copy-start(f32[1,2048]{1,0:T(1,128)} %get-tuple-element.147) | copy-start | bytes 24580
  358.8 151.5 %copy-start.26 = (f32[1,1024]{1,0:T(1,128)S(1)}, f32[1,1024]{1,0:T(1,128)}, u32[]{:S(2)}) copy-start(f32[1,1024]{1,0:T(1,128)} %get-tuple-element.150) | copy-start | bytes 12292
  358.8 151.5 %copy-start.25 = (f32[1,1024]{1,0:T(1,128)S(1)}, f32[1,1024]{1,0:T(1,128)}, u32[]{:S(2)}) copy-start(f32[1,1024]{1,0:T(1,128)} %get-tuple-element.151) | copy-start | bytes 12292
  358.8 151.5 %copy-start.24 = (f32[1,1024]{1,0:T(1,128)S(1)}, f32[1,1024]{1,0:T(1,128)}, u32[]{:S(2)}) copy-start(f32[1,1024]{1,0:T(1,128)} %get-tuple-element.152) | copy-start | bytes 12292
  358.8 151.5 %copy-start.23 = (f32[1,1024]{1,0:T(1,128)S(1)}, f32[1,1024]{1,0:T(1,128)}, u32[]{:S(2)}) copy-start(f32[1,1024]{1,0:T(1,128)} %get-tuple-element.153) | copy-start | bytes 12292
  504.3 36.1 %copy-start.16 = (bf16[2,48,384]{2,1,0:T(8,128)(2,1)S(1)}, bf16[2,48,384]{2,1,0:T(8,128)(2,1)}, u32[]{:S(2)}) copy-start(bf16[2,48,384]{2,1,0:T(8,128)(2,1)} %get-tuple-element.158) | copy-start | bytes 221188
  504.3 36.8 %copy-start.14 = (bf16[2,64,512]{2,1,0:T(8,128)(2,1)S(1)}, bf16[2,64,512]{2,1,0:T(8,128)(2,1)}, u32[]{:S(2)}) copy-start(bf16[2,64,512]{2,1,0:T(8,128)(2,1)} %get-tuple-element.164) | copy-start | bytes 393220
  505.8 35.3 %copy-start.13 = (bf16[2,64,512]{2,1,0:T(8,128)(2,1)S(1)}, bf16[2,64,512]{2,1,0:T(8,128)(2,1)}, u32[]{:S(2)}) copy-start(bf16[2,64,512]{2,1,0:T(8,128)(2,1)} %get-tuple-element.165) | copy-start | bytes 393220
  510.4 0.7 copy-start.17
  540.4 1.6 copy-start.12
  541.2 1.7 copy-start.11
  542.0 1.6 copy-start.10
  542.8 1.0 copy-start.9
  543.8 1.4 copy-start.20
  543.9 1.4 copy-start.8
  544.0 2.1 copy-start.7
  546.1 1.0 copy-start.5
  547.2 0.9 copy-start.18
  547.2 1.3 copy-start.4
  547.4 2.2 copy-start.15
  547.4 2.2 copy-start.27
  548.5 3.7 copy-start.28
  548.5 3.7 copy-start.3
  549.6 3.5 copy-start.1

commit v4 on v3

--- a/solution.py
+++ b/solution.py
@@ -1166,9 +1166,11 @@
             grad_into(crew, r.d_proj, pipe, r.attended, branch)
         pipe.pump()
         args = (r.queries, r.keyvals, r.sums, r.dattended, r.cross_dq, r.dkeyvals, half)
-        attend_back(*args, 0, pairs // 2)
-        pipe.pump()
-        attend_back(*args, pairs // 2, pairs)
+        for i in range(0, pairs, 2):
+            attend_back(*args, i, i + 1)
+            pipe.pump()
+            attend_back(*args, i + 1, i + 2)
+            pipe.pump()
         fold = Fold(crew, r.dkeyvals, r.landing)
         r.cross_q.need()
         r.term_two[...] = to_bf16(dot_right(r.cross_dq[...], r.cross_q.all()))
@@ -1407,14 +1409,14 @@
         copy.wait_recv()
         r.held[1] = r.mods[...] + r.held[0]
         copy = crew.send(r.held.at[1], r.held.at[2], crew.row)
-        pipe.pump()
+        pipe.pump(0)
         copy.wait_recv()
         r.held[3] = r.held[1] + r.held[2]
         r.everyone[crew.wide] = r.held[3]
         copies = [
             crew.send(r.held.at[3], r.everyone.at[crew.wide], target) for target in crew.line
         ]
-        pipe.pump()
+        pipe.pump(0)
         for copy in copies:
             copy.wait_recv()
         yield

time: 564 us -> 558 us (0.989)
  Pallas kernels: 501 us -> 495 us
    pallas_call x4, Pallas kernels: 501 us -> 495 us  [run(): pl.pallas_call(kernel, out_shape=out_shapes, in_specs=in_specs, out_specs...]
where the time goes in v4:
time: 558 us; the launch traced here: 550 us
  Pallas kernels  495 us (89%)
  local copies, waits for them, and re-layouts  26.9 us (5%)
  other arithmetic  14.6 us (3%)
  matrix products  8.9 us (2%)
    pallas_call x4, Pallas kernels, run(): pl.pallas_call(kernel, out_shape=out_shapes, in_specs=in_specs, out_specs...  495 us

profile of v4, /device:TPU:0, one launch (start us, length us, event | category | flops | bytes accessed | tf_op | source)
XLA Modules:
  0.0 549.5 jit_solution(16667785985537322530)
XLA Ops:
  0.7 1.3 reshape.389.refs_9_
  2.0 1.2 reshape.390.refs_10_
  3.2 0.7 convert_reduce_fusion.2
  3.9 0.7 select_reduce_fusion
  5.1 1.3 reduce.25
  6.6 0.6 pad.14.refs_0_
  7.2 0.8 copy.68
  8.0 0.7 reshape_reshape.12.refs_12_
  8.6 1.4 reshape.392
  10.0 1.2 dynamic-slice_reduce_fusion.1
  11.3 0.9 reshape.393.refs_16_
  12.5 1.5 dynamic-slice_reduce_fusion
  14.0 0.8 copy.93
  14.8 206.2 %shard_map.476 = (f32[4,4,16,128]{3,2,1,0:T(8,128)}, f32[6,1024]{1,0:T(8,128)}, f32[4,1,128]{2,1,0:T(1,128)}, f32[1,768]{1,0:T(1,128)}, f32[1,768]{1,0:T(1,128)}...) custom-call(f32[16,1,128]{2,1,0:T(1,128)} %pad.14.refs_0_, ...), custom_call_target="tpu_custom_call" | custom-call | tf_op jit(solution)/shard_map/pallas_call | solution.py:573
  221.0 1.0 slice.459
  222.6 2.8 fusion.35
  225.5 0.6 fusion.20
  226.1 1.4 maximum_multiply_fusion
  227.5 0.9 convolution_multiply_fusion
  228.9 2.6 convert_reduce_fusion
  231.5 122.2 %shard_map.477 = (f32[1,2048]{1,0:T(1,128)}, f32[1,1024]{1,0:T(1,128)}, f32[1,1024]{1,0:T(1,128)}, f32[1,1024]{1,0:T(1,128)}, f32[1,1024]{1,0:T(1,128)}, /*index...) custom-call(f32[384,1024]{1,0:T(8,128)} %get-tuple-element.314.refs_, ...), custom_call_target="tpu_custom_call" | custom-call | tf_op jit(solution)/shard_map/pallas_call | solution.py:573
  353.8 148.0 %shard_map.478 = (f32[1,1024]{1,0:T(1,128)}, f32[1,1024]{1,0:T(1,128)}, f32[384,1024]{1,0:T(8,128)}, bf16[2,48,1024]{2,1,0:T(8,128)(2,1)}, bf16[2,64,512]{2,1,0:...) custom-call(bf16[384,1024]{1,0:T(8,128)(2,1)} %get-tuple-element.98., ...), custom_call_target="tpu_custom_call" | custom-call | tf_op jit(solution)/shard_map/pallas_call | solution.py:573
  502.0 0.7 multiply_reduce_fusion.5
  502.7 0.7 slice_bitcast_fusion.89
  503.7 0.7 multiply_reduce_fusion.3
  504.5 0.7 multiply_reduce_fusion.1
  505.4 0.7 fusion.10
  506.5 0.7 constant_dynamic-update-slice_fusion.5
  507.2 0.7 constant_dynamic-update-slice_fusion.4
  508.0 0.7 copy.81
  508.7 18.5 %shard_map.479 = (f32[4,1,6144]{2,1,0:T(1,128)}, f32[2,16,128]{2,1,0:T(8,128)}) custom-call(f32[4,4,16,128]{3,2,1,0:T(8,128)} %bitcast.336, f32[1,6144]{1,0:T(1,128)} %copy-done.17), custom_call_target="tpu_custom_call" | custom-call | tf_op jit(solution)/shard_map/pallas_call | solution.py:573
  527.2 0.7 fusion.40
  527.9 0.7 slice_add_fusion
  529.8 0.6 slice.510
  530.4 0.6 slice.560
  533.0 0.6 fusion.33
  533.7 0.7 copy.74
  534.4 0.7 pad_maximum_fusion.4
  535.2 0.8 pad_maximum_fusion.1
  536.1 0.7 pad_maximum_fusion.3
  536.9 0.8 pad_maximum_fusion
  538.2 1.0 concatenate.77
  539.2 0.9 bitcast_convert_fusion.1
  540.3 0.8 copy-done.5
  542.5 1.1 bitcast_convert_fusion
  543.6 2.6 fusion.6
  546.2 0.9 copy.142
  547.1 1.1 copy.143
  (160 shorter events, 7.0 us)
Async XLA Ops:
  0.7 11.5 %copy-start.6 = (bf16[64,4096]{1,0:T(8,128)(2,1)S(1)}, bf16[64,4096]{1,0:T(8,128)(2,1)}, u32[]{:S(2)}) copy-start(bf16[64,4096]{1,0:T(8,128)(2,1)} %param.53) | copy-start | bytes 1572868
  221.0 4.3 copy-start.19
  221.0 4.4 copy-start.22
  221.0 6.4 %copy-start = (f32[384,1024]{1,0:T(8,128)S(1)}, f32[384,1024]{1,0:T(8,128)}, u32[]{:S(2)}) copy-start(f32[384,1024]{1,0:T(8,128)} %get-tuple-element.105) | copy-start | bytes 4718596
  353.8 148.1 %copy-start.2 = (bf16[256,768]{1,0:T(8,128)(2,1)S(1)}, bf16[256,768]{1,0:T(8,128)(2,1)}, u32[]{:S(2)}) copy-start(bf16[256,768]{1,0:T(8,128)(2,1)} %get-tuple-element.125.refs_12_) | copy-start | bytes 1179652
  353.8 152.4 %copy-start.21 = (f32[1,2048]{1,0:T(1,128)S(1)}, f32[1,2048]{1,0:T(1,128)}, u32[]{:S(2)}) copy-start(f32[1,2048]{1,0:T(1,128)} %get-tuple-element.147) | copy-start | bytes 24580
  353.8 154.1 %copy-start.26 = (f32[1,1024]{1,0:T(1,128)S(1)}, f32[1,1024]{1,0:T(1,128)}, u32[]{:S(2)}) copy-start(f32[1,1024]{1,0:T(1,128)} %get-tuple-element.150) | copy-start | bytes 12292
  353.8 154.1 %copy-start.25 = (f32[1,1024]{1,0:T(1,128)S(1)}, f32[1,1024]{1,0:T(1,128)}, u32[]{:S(2)}) copy-start(f32[1,1024]{1,0:T(1,128)} %get-tuple-element.151) | copy-start | bytes 12292
  353.8 154.1 %copy-start.24 = (f32[1,1024]{1,0:T(1,128)S(1)}, f32[1,1024]{1,0:T(1,128)}, u32[]{:S(2)}) copy-start(f32[1,1024]{1,0:T(1,128)} %get-tuple-element.152) | copy-start | bytes 12292
  353.8 154.1 %copy-start.23 = (f32[1,1024]{1,0:T(1,128)S(1)}, f32[1,1024]{1,0:T(1,128)}, u32[]{:S(2)}) copy-start(f32[1,1024]{1,0:T(1,128)} %get-tuple-element.153) | copy-start | bytes 12292
  501.9 32.5 %copy-start.16 = (bf16[2,48,384]{2,1,0:T(8,128)(2,1)S(1)}, bf16[2,48,384]{2,1,0:T(8,128)(2,1)}, u32[]{:S(2)}) copy-start(bf16[2,48,384]{2,1,0:T(8,128)(2,1)} %get-tuple-element.158) | copy-start | bytes 221188
  501.9 33.2 %copy-start.14 = (bf16[2,64,512]{2,1,0:T(8,128)(2,1)S(1)}, bf16[2,64,512]{2,1,0:T(8,128)(2,1)}, u32[]{:S(2)}) copy-start(bf16[2,64,512]{2,1,0:T(8,128)(2,1)} %get-tuple-element.164) | copy-start | bytes 393220
  503.4 31.7 %copy-start.13 = (bf16[2,64,512]{2,1,0:T(8,128)(2,1)S(1)}, bf16[2,64,512]{2,1,0:T(8,128)(2,1)}, u32[]{:S(2)}) copy-start(bf16[2,64,512]{2,1,0:T(8,128)(2,1)} %get-tuple-element.165) | copy-start | bytes 393220
  508.0 0.7 copy-start.17
  534.4 1.6 copy-start.12
  535.1 1.7 copy-start.11
  536.0 1.6 copy-start.10
  536.8 1.0 copy-start.9
  537.8 1.4 copy-start.20
  537.9 1.4 copy-start.8
  538.0 2.1 copy-start.7
  540.1 1.0 copy-start.5
  541.2 0.9 copy-start.18
  541.2 1.3 copy-start.4
  541.4 2.2 copy-start.15
  541.4 2.2 copy-start.27
  542.5 3.7 copy-start.28
  542.5 3.7 copy-start.3
  543.6 3.5 copy-start.1
